TPU v7x, 32 devices: a whole 2x2x4 slice. The times are simulated.
32 devices in a mesh: row: 4 (over z), col: 8 (over y, x, core).
Axes of the slice: x: 2, y: 2, z: 4, core: 2. Of those that a mesh axis runs over, the one named last changes fastest.
Arguments:
- tokens: bfloat16 [8192, 2048], P('row', 'col'), may hold values from -6 to 6
- cotangent: bfloat16 [8192, 2048], P('row', 'col'), may hold values from -6 to 6
- segments: int32 [8192], P('row'), may hold values from 0 to 24, never falling along the last dimension, each value on 1 to 800 neighbouring positions
- query_weight: bfloat16 [2048, 2048], P('row', 'col'), may hold values from -0.125 to 0.125
- query_bias: float32 [2048], P('col'), may hold values from -3 to 3
- key_weight: bfloat16 [2048, 2048], P('row', 'col'), may hold values from -0.125 to 0.125
- value_weight: bfloat16 [2048, 2048], P('row', 'col'), may hold values from -0.125 to 0.125
- value_bias: float32 [2048], P('col'), may hold values from -3 to 3
- output_weight: bfloat16 [2048, 2048], P('col', 'row'), may hold values from -0.5 to 0.5
- output_bias: float32 [2048], P('col'), may hold values from -3 to 3
- first_gain: float32 [2048], P('col'), may hold values from 0.5 to 1.5
- first_shift: float32 [2048], P('col'), may hold values from -1.75 to 1.75
- up_weight: bfloat16 [2048, 8192], P('row', 'col'), may hold values from -0.125 to 0.125
- up_bias: float32 [8192], P('col'), may hold values from -3 to 3
- down_weight: bfloat16 [8192, 2048], P('col', 'row'), may hold values from -0.0625 to 0.0625
- down_bias: float32 [2048], P('col'), may hold values from -3 to 3
- second_gain: float32 [2048], P('col'), may hold values from 0.5 to 1.5
- second_shift: float32 [2048], P('col'), may hold values from -1.75 to 1.75
Outputs:
- output: bfloat16 [8192, 2048], P('row', 'col')
- grad_tokens: float32 [8192, 2048], P('row', 'col')
- query_weight_grad: float32 [2048, 2048], P('row', 'col')
- query_bias_grad: float32 [2048], P('col')
- key_weight_grad: float32 [2048, 2048], P('row', 'col')
- value_weight_grad: float32 [2048, 2048], P('row', 'col')
- value_bias_grad: float32 [2048], P('col')
- output_weight_grad: float32 [2048, 2048], P('col', 'row')
- output_bias_grad: float32 [2048], P('col')
- first_gain_grad: float32 [2048], P('col')
- first_shift_grad: float32 [2048], P('col')
- up_weight_grad: float32 [2048, 8192], P('row', 'col')
- up_bias_grad: float32 [8192], P('col')
- down_weight_grad: float32 [8192, 2048], P('col', 'row')
- down_bias_grad: float32 [2048], P('col')
- second_gain_grad: float32 [2048], P('col')
- second_shift_grad: float32 [2048], P('col')
Inputs may be any that keep to these rules, and one draw needn't show every extreme that they name: `segments`: document numbers never fall along the tokens; a document holds at most 800 tokens.
All inputs are finite; a program needn't handle non-finite values.
Results may differ from a plain program's by a relative error of at most 0.034.
Values may be sent and summed in bfloat16 or wider, within the bound.
No kernel may reach another device: no remote copies, remote signals or barrier semaphores. Data moves between devices by JAX's collectives and lax.ppermute only.
A program may use at most 256 MiB of HBM per device.

v0:
```python
import jax
import jax.numpy as jnp
from jax import lax
from jax.sharding import PartitionSpec as P

D = 2048
HEAD_DIM = 128
LAYERS = 2
SEQ_LEN = 1024


epsilon = 1e-06
masked_score = -1e30


def product(left, right):
    return jnp.dot(left, right, preferred_element_type=jnp.float32)


def features(state):
    return lax.all_gather(state.astype(jnp.bfloat16), "col", axis=1, tiled=True)


def partial_sums(terms):
    return lax.psum_scatter(
        terms.astype(jnp.bfloat16), "col", scatter_dimension=1, tiled=True
    ).astype(jnp.float32)


def grad_features(value):
    return lax.all_gather(value, "col", axis=1, tiled=True)


def grad_partials(terms):
    return lax.psum_scatter(
        terms.astype(jnp.bfloat16), "col", scatter_dimension=1, tiled=True
    ).astype(jnp.float32)


def norm_forward(residual, gain, shift):
    total, squares = lax.psum(
        (jnp.sum(residual, axis=1), jnp.sum(residual * residual, axis=1)), "col"
    )
    mean = total / D
    inverse = lax.rsqrt(squares / D - mean * mean + epsilon)
    normed = (residual - mean[:, None]) * inverse[:, None]
    return (normed * gain + shift, normed, inverse)


def norm_backward(grad_out, normed, inverse, gain):
    scaled = grad_out * gain
    total, along = lax.psum((jnp.sum(scaled, axis=1), jnp.sum(scaled * normed, axis=1)), "col")
    grad_residual = inverse[:, None] * (scaled - total[:, None] / D - normed * (along[:, None] / D))
    return (grad_residual, jnp.sum(grad_out * normed, axis=0), jnp.sum(grad_out, axis=0))


def block_views(query, keys, values, segments, number):
    width = query.shape[1]
    heads = width // HEAD_DIM
    block = min(512, SEQ_LEN)
    start = number * block
    anchor = start // SEQ_LEN * SEQ_LEN
    query_rows = lax.dynamic_slice_in_dim(query, start, block, 0).reshape(block, heads, HEAD_DIM)
    key_rows = lax.dynamic_slice_in_dim(keys, anchor, SEQ_LEN, 0).reshape(SEQ_LEN, heads, HEAD_DIM)
    value_rows = lax.dynamic_slice_in_dim(values, anchor, SEQ_LEN, 0).reshape(
        SEQ_LEN, heads, HEAD_DIM
    )
    query_docs = lax.dynamic_slice_in_dim(segments, start, block, 0)
    key_docs = lax.dynamic_slice_in_dim(segments, anchor, SEQ_LEN, 0)
    allowed = query_docs[:, None] == key_docs[None, :]
    scores = jnp.einsum(
        "qhd,khd->hqk", query_rows, key_rows, preferred_element_type=jnp.float32
    ) * HEAD_DIM ** (-0.5)
    scores = jnp.where(allowed[None], scores, masked_score)
    return (start, anchor, query_rows, key_rows, value_rows, scores)


def attention(query, keys, values, segments):
    rows, width = query.shape
    block = min(512, SEQ_LEN)

    def one_block(number):
        start, anchor, query_rows, key_rows, value_rows, scores = block_views(
            query, keys, values, segments, number
        )
        peak = jnp.max(scores, axis=-1, keepdims=True)
        weight = jnp.exp(scores - peak)
        total = jnp.sum(weight, axis=-1, keepdims=True)
        probs = (weight / total).astype(jnp.bfloat16)
        mixed = jnp.einsum("hqk,khd->qhd", probs, value_rows, preferred_element_type=jnp.float32)
        return (mixed.reshape(block, width), peak[..., 0] + jnp.log(total[..., 0]))

    mixed, log_total = lax.map(one_block, jnp.arange(rows // block))
    return (mixed.reshape(rows, width).astype(jnp.bfloat16), log_total)


def add_rows(total, part, anchor):
    current = lax.dynamic_slice_in_dim(total, anchor, part.shape[0], 0)
    return lax.dynamic_update_slice_in_dim(total, current + part, anchor, 0)


def attention_backward(grad_mixed, query, keys, values, segments, log_total):
    rows, width = query.shape
    heads = width // HEAD_DIM
    block = min(512, SEQ_LEN)
    scale = HEAD_DIM ** (-0.5)

    def one_block(carry, number):
        key_sum, value_sum = carry
        start, anchor, query_rows, key_rows, value_rows, scores = block_views(
            query, keys, values, segments, number
        )
        probs = jnp.exp(scores - log_total[number][..., None])
        grad_rows = lax.dynamic_slice_in_dim(grad_mixed, start, block, 0).reshape(
            block, heads, HEAD_DIM
        )
        value_part = jnp.einsum(
            "hqk,qhd->khd",
            probs.astype(jnp.bfloat16),
            grad_rows,
            preferred_element_type=jnp.float32,
        )
        grad_probs = jnp.einsum(
            "qhd,khd->hqk", grad_rows, value_rows, preferred_element_type=jnp.float32
        )
        grad_scores = probs * (grad_probs - jnp.sum(grad_probs * probs, axis=-1, keepdims=True))
        grad_scores = grad_scores.astype(jnp.bfloat16)
        query_grad = (
            jnp.einsum("hqk,khd->qhd", grad_scores, key_rows, preferred_element_type=jnp.float32)
            * scale
        )
        key_part = (
            jnp.einsum("hqk,qhd->khd", grad_scores, query_rows, preferred_element_type=jnp.float32)
            * scale
        )
        key_sum = add_rows(key_sum, key_part.reshape(SEQ_LEN, width), anchor)
        value_sum = add_rows(value_sum, value_part.reshape(SEQ_LEN, width), anchor)
        return ((key_sum, value_sum), query_grad.reshape(block, width).astype(jnp.bfloat16))

    empty = jnp.zeros((rows, width), jnp.float32)
    (key_sum, value_sum), query_grad = lax.scan(
        one_block, (empty, empty), jnp.arange(rows // block)
    )
    return (
        query_grad.reshape(rows, width),
        key_sum.astype(jnp.bfloat16),
        value_sum.astype(jnp.bfloat16),
    )


def layer_forward(state, segments, weights, biases):
    query_weight, key_weight, value_weight, output_weight, up_weight, down_weight = weights
    (
        query_bias,
        value_bias,
        output_bias,
        first_gain,
        first_shift,
        up_bias,
        down_bias,
        second_gain,
        second_shift,
    ) = biases
    whole = features(state)
    query = (product(whole, query_weight) + query_bias).astype(jnp.bfloat16)
    keys = product(whole, key_weight).astype(jnp.bfloat16)
    values = (product(whole, value_weight) + value_bias).astype(jnp.bfloat16)
    mixed, log_total = attention(query, keys, values, segments)
    branch = partial_sums(product(mixed, output_weight)) + output_bias
    first, first_normed, first_inverse = norm_forward(state + branch, first_gain, first_shift)
    whole_first = features(first)
    hidden = product(whole_first, up_weight) + up_bias
    active = jax.nn.gelu(hidden, approximate=True).astype(jnp.bfloat16)
    second = partial_sums(product(active, down_weight)) + down_bias
    result, second_normed, second_inverse = norm_forward(first + second, second_gain, second_shift)
    saved = (
        whole,
        query,
        keys,
        values,
        log_total,
        mixed,
        first_normed,
        first_inverse,
        whole_first,
        hidden,
        active,
        second_normed,
        second_inverse,
    )
    return (result, saved)


def layer_backward(grad_out, segments, weights, biases, saved):
    query_weight, key_weight, value_weight, output_weight, up_weight, down_weight = weights
    (
        query_bias,
        value_bias,
        output_bias,
        first_gain,
        first_shift,
        up_bias,
        down_bias,
        second_gain,
        second_shift,
    ) = biases
    (
        whole,
        query,
        keys,
        values,
        log_total,
        mixed,
        first_normed,
        first_inverse,
        whole_first,
        hidden,
        active,
        second_normed,
        second_inverse,
    ) = saved
    grad_second, second_gain_grad, second_shift_grad = norm_backward(
        grad_out, second_normed, second_inverse, second_gain
    )
    second_rounded = grad_second.astype(jnp.bfloat16)
    whole_second = grad_features(second_rounded)
    down_grad = jnp.einsum("tf,td->fd", active, whole_second, preferred_element_type=jnp.float32)
    grad_active = jnp.einsum(
        "td,fd->tf", whole_second, down_weight, preferred_element_type=jnp.float32
    )
    unused, gelu_back = jax.vjp(lambda value: jax.nn.gelu(value, approximate=True), hidden)
    grad_hidden = gelu_back(grad_active)[0].astype(jnp.bfloat16)
    up_grad = jnp.einsum("td,tf->df", whole_first, grad_hidden, preferred_element_type=jnp.float32)
    up_terms = jnp.einsum("tf,df->td", grad_hidden, up_weight, preferred_element_type=jnp.float32)
    grad_first = grad_second + grad_partials(up_terms)
    grad_branch, first_gain_grad, first_shift_grad = norm_backward(
        grad_first, first_normed, first_inverse, first_gain
    )
    branch_rounded = grad_branch.astype(jnp.bfloat16)
    whole_branch = grad_features(branch_rounded)
    output_grad = jnp.einsum("tc,td->cd", mixed, whole_branch, preferred_element_type=jnp.float32)
    grad_mixed = jnp.einsum(
        "td,cd->tc", whole_branch, output_weight, preferred_element_type=jnp.float32
    ).astype(jnp.bfloat16)
    query_grad, key_grad, value_grad = attention_backward(
        grad_mixed, query, keys, values, segments, log_total
    )
    input_terms = jnp.einsum(
        "tc,dc->td", query_grad, query_weight, preferred_element_type=jnp.float32
    )
    input_terms = input_terms + jnp.einsum(
        "tc,dc->td", key_grad, key_weight, preferred_element_type=jnp.float32
    )
    input_terms = input_terms + jnp.einsum(
        "tc,dc->td", value_grad, value_weight, preferred_element_type=jnp.float32
    )
    grad_input = grad_branch + grad_partials(input_terms)
    weight_grads = (
        jnp.einsum("td,tc->dc", whole, query_grad, preferred_element_type=jnp.float32),
        jnp.einsum("td,tc->dc", whole, key_grad, preferred_element_type=jnp.float32),
        jnp.einsum("td,tc->dc", whole, value_grad, preferred_element_type=jnp.float32),
        output_grad,
        up_grad,
        down_grad,
    )
    bias_grads = (
        jnp.sum(query_grad, axis=0, dtype=jnp.float32),
        jnp.sum(value_grad, axis=0, dtype=jnp.float32),
        jnp.sum(branch_rounded, axis=0, dtype=jnp.float32),
        first_gain_grad,
        first_shift_grad,
        jnp.sum(grad_hidden, axis=0, dtype=jnp.float32),
        jnp.sum(second_rounded, axis=0, dtype=jnp.float32),
        second_gain_grad,
        second_shift_grad,
    )
    return (grad_input, weight_grads, bias_grads)


def local(
    tokens,
    cotangent,
    segments,
    query_weight,
    query_bias,
    key_weight,
    value_weight,
    value_bias,
    output_weight,
    output_bias,
    first_gain,
    first_shift,
    up_weight,
    up_bias,
    down_weight,
    down_bias,
    second_gain,
    second_shift,
):
    weights = (
        lax.all_gather(query_weight, "row", axis=0, tiled=True),
        lax.all_gather(key_weight, "row", axis=0, tiled=True),
        lax.all_gather(value_weight, "row", axis=0, tiled=True),
        lax.all_gather(output_weight, "row", axis=1, tiled=True),
        lax.all_gather(up_weight, "row", axis=0, tiled=True),
        lax.all_gather(down_weight, "row", axis=1, tiled=True),
    )
    biases = (
        query_bias,
        value_bias,
        output_bias,
        first_gain,
        first_shift,
        up_bias,
        down_bias,
        second_gain,
        second_shift,
    )
    state = tokens.astype(jnp.float32)
    kept = []
    for depth in range(LAYERS):
        state, saved = layer_forward(state, segments, weights, biases)
        kept.append(saved)
    gradient = cotangent.astype(jnp.float32)
    weight_total = None
    bias_total = None
    for depth in reversed(range(LAYERS)):
        gradient, weight_part, bias_part = layer_backward(
            gradient, segments, weights, biases, kept[depth]
        )
        weight_part = (
            lax.psum_scatter(
                weight_part[0].astype(jnp.bfloat16), "row", scatter_dimension=0, tiled=True
            ).astype(jnp.float32),
            lax.psum_scatter(
                weight_part[1].astype(jnp.bfloat16), "row", scatter_dimension=0, tiled=True
            ).astype(jnp.float32),
            lax.psum_scatter(
                weight_part[2].astype(jnp.bfloat16), "row", scatter_dimension=0, tiled=True
            ).astype(jnp.float32),
            lax.psum_scatter(
                weight_part[3].astype(jnp.bfloat16), "row", scatter_dimension=1, tiled=True
            ).astype(jnp.float32),
            lax.psum_scatter(
                weight_part[4].astype(jnp.bfloat16), "row", scatter_dimension=0, tiled=True
            ).astype(jnp.float32),
            lax.psum_scatter(
                weight_part[5].astype(jnp.bfloat16), "row", scatter_dimension=1, tiled=True
            ).astype(jnp.float32),
        )
        bias_part = lax.psum(
            (
                bias_part[0],
                bias_part[1],
                bias_part[2],
                bias_part[3],
                bias_part[4],
                bias_part[5],
                bias_part[6],
                bias_part[7],
                bias_part[8],
            ),
            "row",
        )
        if weight_total is None:
            weight_total = tuple(weight_part)
            bias_total = tuple(bias_part)
        else:
            weight_total = tuple(jax.tree.map(jnp.add, tuple(weight_total), tuple(weight_part)))
            bias_total = tuple(jax.tree.map(jnp.add, tuple(bias_total), tuple(bias_part)))
    return (
        state.astype(jnp.bfloat16),
        gradient,
        weight_total[0],
        bias_total[0],
        weight_total[1],
        weight_total[2],
        bias_total[1],
        weight_total[3],
        bias_total[2],
        bias_total[3],
        bias_total[4],
        weight_total[4],
        bias_total[5],
        weight_total[5],
        bias_total[6],
        bias_total[7],
        bias_total[8],
    )


def solution(mesh):
    placed = (
        P("row", "col"),
        P("row", "col"),
        P("row"),
        P("row", "col"),
        P("col"),
        P("row", "col"),
        P("row", "col"),
        P("col"),
        P("col", "row"),
        P("col"),
        P("col"),
        P("col"),
        P("row", "col"),
        P("col"),
        P("col", "row"),
        P("col"),
        P("col"),
        P("col"),
    )
    return jax.shard_map(
        local,
        mesh=mesh,
        in_specs=placed,
        out_specs=(
            P("row", "col"),
            P("row", "col"),
            P("row", "col"),
            P("col"),
            P("row", "col"),
            P("row", "col"),
            P("col"),
            P("col", "row"),
            P("col"),
            P("col"),
            P("col"),
            P("row", "col"),
            P("col"),
            P("col", "row"),
            P("col"),
            P("col"),
            P("col"),
        ),
        check_vma=False,
    )
```

profile of v0, /device:TPU:0, one launch (start us, length us, event | category | flops | bytes accessed | tf_op | source)
XLA Modules:
  0.0 2406.6 jit_solution(13832007594266843788)
XLA Ops:
  10.6 29.6 %all-gather.21.cloned.1.call-done = bf16[2048,256]{1,0:T(8,128)(2,1)} async-done(((bf16[512,256]{1,0:T(8,128)(2,1)}), bf16[2048,256]{1,0:T(8,128)(2,1)}) %all-gather.21.cloned.1.call-update) | async-done | bytes 1048592 | tf_op jit(solution)/shard_map/all_gather | solution.py:302
  40.3 57.4 %all-gather.15.cloned.1.call-done = bf16[2048,2048]{1,0:T(8,128)(2,1)} async-done(((bf16[2048,256]{1,0:T(8,128)(2,1)}), bf16[2048,2048]{1,0:T(8,128)(2,1)}) %all-gather.15.cloned.1.call-update) | async-done | bytes 8388624 | tf_op jit(solution)/shard_map/all_gather | solution.py:21
  162.8 34.3 %while.60 = (s32[]{:T(128)}, bf16[4,512,256]{2,1,0:T(8,128)(2,1)S(1)}, f32[4,2,512]{2,1,0:T(2,128)S(1)}, s32[4]{0:T(128)S(1)}, bf16[2048,256]{0,1:T(8,128)(2,1)S...) while((s32[]{:T(128)}, ...), condition=%wide.region_3.4_spmd, body=%wide.region_0.3_spmd.sunk | while | flops 549977088 | bytes 19974568 | solution.py:93
  205.8 70.0 %reduce-scatter.21.cloned.1.call-done = bf16[2048,256]{1,0:T(8,128)(2,1)} async-done(((bf16[2048,2048]{1,0:T(8,128)(2,1)}), bf16[2048,256]{1,0:T(8,128)(2,1)}) %reduce-scatter.21.cloned.1.call-update) | async-done | bytes 1048592 | tf_op jit(solution)/shard_map/reduce_scatter | solution.py:25
  277.7 23.9 all-reduce.7
  305.0 53.2 %all-gather.27.cloned.1.call-done = bf16[2048,1024]{1,0:T(8,128)(2,1)} async-done(((bf16[512,1024]{1,0:T(8,128)(2,1)}), bf16[2048,1024]{1,0:T(8,128)(2,1)}) %all-gather.27.cloned.1.call-update) | async-done | bytes 4194320 | tf_op jit(solution)/shard_map/all_gather | solution.py:305
  358.2 57.1 %all-gather.25.cloned.1.call-done = bf16[2048,2048]{1,0:T(8,128)(2,1)} async-done(((bf16[2048,256]{1,0:T(8,128)(2,1)}), bf16[2048,2048]{1,0:T(8,128)(2,1)}) %all-gather.25.cloned.1.call-update) | async-done | bytes 8388624 | tf_op jit(solution)/shard_map/all_gather | solution.py:21
  429.7 68.0 %all-gather.29.cloned.1.call-done = bf16[1024,2048]{1,0:T(8,128)(2,1)} async-done(((bf16[1024,512]{1,0:T(8,128)(2,1)}), bf16[1024,2048]{1,0:T(8,128)(2,1)}) %all-gather.29.cloned.1.call-update) | async-done | bytes 4194320 | tf_op jit(solution)/shard_map/all_gather | solution.py:306
  513.2 69.9 %reduce-scatter.23.cloned.1.call-done = bf16[2048,256]{1,0:T(8,128)(2,1)} async-done(((bf16[2048,2048]{1,0:T(8,128)(2,1)}), bf16[2048,256]{1,0:T(8,128)(2,1)}) %reduce-scatter.23.cloned.1.call-update) | async-done | bytes 1048592 | tf_op jit(solution)/shard_map/reduce_scatter | solution.py:25
  610.5 56.0 %all-gather.31.cloned.1.call-done = bf16[2048,2048]{1,0:T(8,128)(2,1)} async-done(((bf16[2048,256]{1,0:T(8,128)(2,1)}), bf16[2048,2048]{1,0:T(8,128)(2,1)}) %all-gather.31.cloned.1.call-update) | async-done | bytes 8388624 | tf_op jit(solution)/shard_map/all_gather | solution.py:21
  694.5 41.1 %while.61 = (s32[]{:T(128)}, bf16[4,512,256]{2,1,0:T(8,128)(2,1)}, f32[4,2,512]{2,1,0:T(2,128)S(1)}, s32[4]{0:T(128)S(1)}, bf16[2048,256]{0,1:T(8,128)(2,1)}, /*...) while((s32[]{:T(128)}, bf16[4,512,256]{2,1,0:T(8,128)(2,1)}, ...), condition=%wide.region_17.18_spmd, body=%wide.region_14.17_spmd.sunk | while | flops 549977088 | bytes 19974568 | solution.py:93
  742.8 71.4 %reduce-scatter.25.cloned.1.call-done = bf16[2048,256]{1,0:T(8,128)(2,1)} async-done(((bf16[2048,2048]{1,0:T(8,128)(2,1)}), bf16[2048,256]{1,0:T(8,128)(2,1)}) %reduce-scatter.25.cloned.1.call-update) | async-done | bytes 1048592 | tf_op jit(solution)/shard_map/reduce_scatter | solution.py:25
  843.9 56.0 %all-gather.33.cloned.1.call-done = bf16[2048,2048]{1,0:T(8,128)(2,1)} async-done(((bf16[2048,256]{1,0:T(8,128)(2,1)}), bf16[2048,2048]{1,0:T(8,128)(2,1)}) %all-gather.33.cloned.1.call-update) | async-done | bytes 8388624 | tf_op jit(solution)/shard_map/all_gather | solution.py:21
  927.7 71.4 %reduce-scatter.27.cloned.1.call-done = bf16[2048,256]{1,0:T(8,128)(2,1)} async-done(((bf16[2048,2048]{1,0:T(8,128)(2,1)}), bf16[2048,256]{1,0:T(8,128)(2,1)}) %reduce-scatter.27.cloned.1.call-update) | async-done | bytes 1048592 | tf_op jit(solution)/shard_map/reduce_scatter | solution.py:25
  1057.2 55.8 %all-gather.35.cloned.1.call-done = bf16[2048,2048]{1,0:T(8,128)(2,1)} async-done(((bf16[2048,256]{1,0:T(8,128)(2,1)}), bf16[2048,2048]{1,0:T(8,128)(2,1)}) %all-gather.35.cloned.1.call-update) | async-done | bytes 8388624 | tf_op jit(solution)/shard_map/all_gather | solution.py:31
  1146.8 71.4 %reduce-scatter.29.cloned.1.call-done = bf16[2048,256]{1,0:T(8,128)(2,1)} async-done(((bf16[2048,2048]{1,0:T(8,128)(2,1)}), bf16[2048,256]{1,0:T(8,128)(2,1)}) %reduce-scatter.29.cloned.1.call-update) | async-done | bytes 1048592 | tf_op jit(solution)/shard_map/reduce_scatter | solution.py:35
  1250.6 55.6 %all-gather.37.cloned.1.call-done = bf16[2048,2048]{1,0:T(8,128)(2,1)} async-done(((bf16[2048,256]{1,0:T(8,128)(2,1)}), bf16[2048,2048]{1,0:T(8,128)(2,1)}) %all-gather.37.cloned.1.call-update) | async-done | bytes 8388624 | tf_op jit(solution)/shard_map/all_gather | solution.py:31
  1316.1 71.1 %while.62 = (s32[]{:T(128)}, f32[2048,256]{0,1:T(8,128)}, f32[2048,256]{0,1:T(8,128)S(1)}, bf16[4,512,256]{1,2,0:T(8,128)(2,1)}, s32[4]{0:T(128)S(1)}, /*index=5...) while((s32[]{:T(128)}, f32[2048,256]{0,1:T(8,128)}, ...), condition=%wide.region_39.40_spmd, body=%wide.region_37.39_spmd.sunk | while | flops 1359477760 | bytes 65845808 | solution.py:141
  1424.1 71.4 %reduce-scatter.31.cloned.1.call-done = bf16[2048,256]{1,0:T(8,128)(2,1)} async-done(((bf16[2048,2048]{1,0:T(8,128)(2,1)}), bf16[2048,256]{1,0:T(8,128)(2,1)}) %reduce-scatter.31.cloned.1.call-update) | async-done | bytes 1048592 | tf_op jit(solution)/shard_map/reduce_scatter | solution.py:35
  1527.5 56.0 %all-gather.39.cloned.1.call-done = bf16[2048,2048]{1,0:T(8,128)(2,1)} async-done(((bf16[2048,256]{1,0:T(8,128)(2,1)}), bf16[2048,2048]{1,0:T(8,128)(2,1)}) %all-gather.39.cloned.1.call-update) | async-done | bytes 8388624 | tf_op jit(solution)/shard_map/all_gather | solution.py:31
  1617.3 71.4 %reduce-scatter.33.cloned.1.call-done = bf16[2048,256]{1,0:T(8,128)(2,1)} async-done(((bf16[2048,2048]{1,0:T(8,128)(2,1)}), bf16[2048,256]{1,0:T(8,128)(2,1)}) %reduce-scatter.33.cloned.1.call-update) | async-done | bytes 1048592 | tf_op jit(solution)/shard_map/reduce_scatter | solution.py:35
  1815.8 74.1 %while.63 = (s32[]{:T(128)}, f32[2048,256]{0,1:T(8,128)}, f32[2048,256]{0,1:T(8,128)S(1)}, bf16[4,512,256]{1,2,0:T(8,128)(2,1)}, s32[4]{0:T(128)S(1)}, /*index=5...) while((s32[]{:T(128)}, f32[2048,256]{0,1:T(8,128)}, ...), condition=%wide.region_52.53_spmd, body=%wide.region_50.52_spmd.sunk | while | flops 1359477760 | bytes 65845808 | solution.py:141
  1972.4 42.7 %reduce-scatter.57.cloned.1.call-done = bf16[1024,512]{1,0:T(8,128)(2,1)} async-done(((bf16[1024,2048]{1,0:T(8,128)(2,1)}), bf16[1024,512]{1,0:T(8,128)(2,1)}) %reduce-scatter.57.cloned.1.call-update) | async-done | bytes 1048592 | tf_op jit(solution)/shard_map/reduce_scatter | solution.py:347
  2015.2 79.6 %reduce-scatter.59.cloned.1.call-done = bf16[1024,512]{1,0:T(8,128)(2,1)} async-done(((bf16[1024,2048]{1,0:T(8,128)(2,1)}), bf16[1024,512]{1,0:T(8,128)(2,1)}) %reduce-scatter.59.cloned.1.call-update) | async-done | bytes 1048592 | tf_op jit(solution)/shard_map/reduce_scatter | solution.py:347
  2125.0 28.0 %reduce-scatter.51.cloned.1.call-done = bf16[256,512]{1,0:T(8,128)(2,1)} async-done(((bf16[256,2048]{1,0:T(8,128)(2,1)}), bf16[256,512]{1,0:T(8,128)(2,1)}) %reduce-scatter.51.cloned.1.call-update) | async-done | bytes 262160 | tf_op jit(solution)/shard_map/reduce_scatter | solution.py:341
  2154.9 26.3 %reduce-scatter.37.cloned.1.call-done = bf16[512,256]{1,0:T(8,128)(2,1)} async-done(((bf16[2048,256]{1,0:T(8,128)(2,1)}), bf16[512,256]{1,0:T(8,128)(2,1)}) %reduce-scatter.37.cloned.1.call-update) | async-done | bytes 262160 | tf_op jit(solution)/shard_map/reduce_scatter | solution.py:332
  2181.2 28.1 %reduce-scatter.39.cloned.1.call-done = bf16[512,256]{1,0:T(8,128)(2,1)} async-done(((bf16[2048,256]{1,0:T(8,128)(2,1)}), bf16[512,256]{1,0:T(8,128)(2,1)}) %reduce-scatter.39.cloned.1.call-update) | async-done | bytes 262160 | tf_op jit(solution)/shard_map/reduce_scatter | solution.py:332
  2211.2 26.2 %reduce-scatter.45.cloned.1.call-done = bf16[512,256]{1,0:T(8,128)(2,1)} async-done(((bf16[2048,256]{1,0:T(8,128)(2,1)}), bf16[512,256]{1,0:T(8,128)(2,1)}) %reduce-scatter.45.cloned.1.call-update) | async-done | bytes 262160 | tf_op jit(solution)/shard_map/reduce_scatter | solution.py:338
  2237.4 28.1 %reduce-scatter.47.cloned.1.call-done = bf16[512,256]{1,0:T(8,128)(2,1)} async-done(((bf16[2048,256]{1,0:T(8,128)(2,1)}), bf16[512,256]{1,0:T(8,128)(2,1)}) %reduce-scatter.47.cloned.1.call-update) | async-done | bytes 262160 | tf_op jit(solution)/shard_map/reduce_scatter | solution.py:338
  2267.4 26.4 %reduce-scatter.41.cloned.1.call-done = bf16[512,256]{1,0:T(8,128)(2,1)} async-done(((bf16[2048,256]{1,0:T(8,128)(2,1)}), bf16[512,256]{1,0:T(8,128)(2,1)}) %reduce-scatter.41.cloned.1.call-update) | async-done | bytes 262160 | tf_op jit(solution)/shard_map/reduce_scatter | solution.py:335
  2293.8 28.5 %reduce-scatter.43.cloned.1.call-done = bf16[512,256]{1,0:T(8,128)(2,1)} async-done(((bf16[2048,256]{1,0:T(8,128)(2,1)}), bf16[512,256]{1,0:T(8,128)(2,1)}) %reduce-scatter.43.cloned.1.call-update) | async-done | bytes 262160 | tf_op jit(solution)/shard_map/reduce_scatter | solution.py:335
  2324.2 72.0 %reduce-scatter.35.cloned.1.call-done = bf16[2048,256]{1,0:T(8,128)(2,1)} async-done(((bf16[2048,2048]{1,0:T(8,128)(2,1)}), bf16[2048,256]{1,0:T(8,128)(2,1)}) %reduce-scatter.35.cloned.1.call-update) | async-done | bytes 1048592 | tf_op jit(solution)/shard_map/reduce_scatter | solution.py:35
  (601 shorter events, 911.9 us)
Async XLA Ops:
  8.7 118.5 %all-gather.19.cloned.1.call-start = ((), (), s32[]{:S(2)}) async-start(), calls=%async_computation.22 | async-start | bytes 1310720 | tf_op jit(solution)/shard_map/all_gather | solution.py:301
  9.4 146.6 %all-gather.17.cloned.1.call-start = ((), (), s32[]{:S(2)}) async-start(), calls=%async_computation.21 | async-start | bytes 1310720 | tf_op jit(solution)/shard_map/all_gather | solution.py:303
  10.0 187.2 %all-gather.23.cloned.1.call-start = ((), (), s32[]{:S(2)}) async-start(), calls=%async_computation.24 | async-start | bytes 1310720 | tf_op jit(solution)/shard_map/all_gather | solution.py:304
  10.6 265.2 %reduce-scatter.21.cloned.1.call-start = ((), (), s32[]{:S(2)}) async-start(), calls=%async_computation.25 | async-start | bytes 9437184 | tf_op jit(solution)/shard_map/reduce_scatter | solution.py:25
  204.9 153.4 %all-gather.27.cloned.1.call-start = ((), (), s32[]{:S(2)}) async-start(), calls=%async_computation.27 | async-start | bytes 5242880 | tf_op jit(solution)/shard_map/all_gather | solution.py:305
  205.6 209.7 %all-gather.25.cloned.1.call-start = ((), (), s32[]{:S(2)}) async-start(), calls=%async_computation.26 | async-start | bytes 9437184 | tf_op jit(solution)/shard_map/all_gather | solution.py:21
  304.2 193.6 %all-gather.29.cloned.1.call-start = ((), (), s32[]{:S(2)}) async-start(), calls=%async_computation.28 | async-start | bytes 5242880 | tf_op jit(solution)/shard_map/all_gather | solution.py:306
  304.9 278.2 %reduce-scatter.23.cloned.1.call-start = ((), (), s32[]{:S(2)}) async-start(), calls=%async_computation.29 | async-start | bytes 9437184 | tf_op jit(solution)/shard_map/reduce_scatter | solution.py:25
  513.2 153.2 %all-gather.31.cloned.1.call-start = ((), (), s32[]{:S(2)}) async-start(), calls=%async_computation.30 | async-start | bytes 9437184 | tf_op jit(solution)/shard_map/all_gather | solution.py:21
  610.4 203.8 %reduce-scatter.25.cloned.1.call-start = ((), (), s32[]{:S(2)}) async-start(), calls=%async_computation.31 | async-start | bytes 9437184 | tf_op jit(solution)/shard_map/reduce_scatter | solution.py:25
  742.8 157.1 %all-gather.33.cloned.1.call-start = ((), (), s32[]{:S(2)}) async-start(), calls=%async_computation.32 | async-start | bytes 9437184 | tf_op jit(solution)/shard_map/all_gather | solution.py:21
  843.8 155.3 %reduce-scatter.27.cloned.1.call-start = ((), (), s32[]{:S(2)}) async-start(), calls=%async_computation.33 | async-start | bytes 9437184 | tf_op jit(solution)/shard_map/reduce_scatter | solution.py:25
  927.6 185.4 %all-gather.35.cloned.1.call-start = ((), (), s32[]{:S(2)}) async-start(), calls=%async_computation.34 | async-start | bytes 9437184 | tf_op jit(solution)/shard_map/all_gather | solution.py:31
  1057.0 161.2 %reduce-scatter.29.cloned.1.call-start = ((), (), s32[]{:S(2)}) async-start(), calls=%async_computation.35 | async-start | bytes 9437184 | tf_op jit(solution)/shard_map/reduce_scatter | solution.py:35
  1146.7 159.5 %all-gather.37.cloned.1.call-start = ((), (), s32[]{:S(2)}) async-start(), calls=%async_computation.36 | async-start | bytes 9437184 | tf_op jit(solution)/shard_map/all_gather | solution.py:31
  1250.2 245.4 %reduce-scatter.31.cloned.1.call-start = ((), (), s32[]{:S(2)}) async-start(), calls=%async_computation.37 | async-start | bytes 9437184 | tf_op jit(solution)/shard_map/reduce_scatter | solution.py:35
  1424.1 159.3 %all-gather.39.cloned.1.call-start = ((), (), s32[]{:S(2)}) async-start(), calls=%async_computation.38 | async-start | bytes 9437184 | tf_op jit(solution)/shard_map/all_gather | solution.py:31
  1527.4 161.2 %reduce-scatter.33.cloned.1.call-start = ((), (), s32[]{:S(2)}) async-start(), calls=%async_computation.39 | async-start | bytes 9437184 | tf_op jit(solution)/shard_map/reduce_scatter | solution.py:35
  1617.2 174.9 %all-gather.41.cloned.1.call-start = ((), (), s32[]{:S(2)}) async-start(), calls=%async_computation.40 | async-start | bytes 9437184 | tf_op jit(solution)/shard_map/all_gather | solution.py:31
  1720.8 248.3 %reduce-scatter.53.cloned.1.call-start = ((), (), s32[]{:S(2)}) async-start(), calls=%async_computation.50 | async-start | bytes 5242880 | tf_op jit(solution)/shard_map/reduce_scatter | solution.py:344
  1735.0 234.1 %reduce-scatter.55.cloned.1.call-start = ((), (), s32[]{:S(2)}) async-start(), calls=%async_computation.51 | async-start | bytes 5242880 | tf_op jit(solution)/shard_map/reduce_scatter | solution.py:344
  1749.2 266.0 %reduce-scatter.57.cloned.1.call-start = ((), (), s32[]{:S(2)}) async-start(), calls=%async_computation.52 | async-start | bytes 5242880 | tf_op jit(solution)/shard_map/reduce_scatter | solution.py:347
  1766.6 328.2 %reduce-scatter.59.cloned.1.call-start = ((), (), s32[]{:S(2)}) async-start(), calls=%async_computation.53 | async-start | bytes 5242880 | tf_op jit(solution)/shard_map/reduce_scatter | solution.py:347
  1783.2 341.8 %reduce-scatter.49.cloned.1.call-start = ((), (), s32[]{:S(2)}) async-start(), calls=%async_computation.48 | async-start | bytes 1310720 | tf_op jit(solution)/shard_map/reduce_scatter | solution.py:341
  1791.8 361.2 %reduce-scatter.51.cloned.1.call-start = ((), (), s32[]{:S(2)}) async-start(), calls=%async_computation.49 | async-start | bytes 1310720 | tf_op jit(solution)/shard_map/reduce_scatter | solution.py:341
  1799.0 382.3 %reduce-scatter.37.cloned.1.call-start = ((), (), s32[]{:S(2)}) async-start(), calls=%async_computation.42 | async-start | bytes 1310720 | tf_op jit(solution)/shard_map/reduce_scatter | solution.py:332
  1806.1 403.2 %reduce-scatter.39.cloned.1.call-start = ((), (), s32[]{:S(2)}) async-start(), calls=%async_computation.43 | async-start | bytes 1310720 | tf_op jit(solution)/shard_map/reduce_scatter | solution.py:332
  1899.7 337.8 %reduce-scatter.45.cloned.1.call-start = ((), (), s32[]{:S(2)}) async-start(), calls=%async_computation.46 | async-start | bytes 1310720 | tf_op jit(solution)/shard_map/reduce_scatter | solution.py:338
  1907.7 357.9 %reduce-scatter.47.cloned.1.call-start = ((), (), s32[]{:S(2)}) async-start(), calls=%async_computation.47 | async-start | bytes 1310720 | tf_op jit(solution)/shard_map/reduce_scatter | solution.py:338
  1915.6 378.2 %reduce-scatter.41.cloned.1.call-start = ((), (), s32[]{:S(2)}) async-start(), calls=%async_computation.44 | async-start | bytes 1310720 | tf_op jit(solution)/shard_map/reduce_scatter | solution.py:335
  1923.2 399.1 %reduce-scatter.43.cloned.1.call-start = ((), (), s32[]{:S(2)}) async-start(), calls=%async_computation.45 | async-start | bytes 1310720 | tf_op jit(solution)/shard_map/reduce_scatter | solution.py:335
  1932.1 464.1 %reduce-scatter.35.cloned.1.call-start = ((), (), s32[]{:S(2)}) async-start(), calls=%async_computation.41 | async-start | bytes 9437184 | tf_op jit(solution)/shard_map/reduce_scatter | solution.py:35
  (89 other events, 4345.1 us)
Sparse Core Ops, SparseCore 0:
  9.6 30.6 all-gather.20
  42.1 55.4 all-gather.14
  99.2 27.9 all-gather.18
  128.6 27.4 all-gather.16
  157.5 27.4 all-gather.22
  205.0 70.7 reduce-scatter.20
  277.4 80.7 all-gather.26
  360.8 54.4 all-gather.24
  417.0 80.7 all-gather.28
  513.3 69.8 reduce-scatter.22
  610.5 55.8 all-gather.30
  742.9 71.2 reduce-scatter.24
  843.9 55.8 all-gather.32
  927.7 71.3 reduce-scatter.26
  1057.1 55.8 all-gather.34
  1146.8 71.2 reduce-scatter.28
  1250.3 55.8 all-gather.36
  1424.2 71.3 reduce-scatter.30
  1527.5 55.8 all-gather.38
  1617.3 71.2 reduce-scatter.32
  1720.9 55.8 all-gather.40
  1779.2 76.7 reduce-scatter.52
  1858.3 77.2 reduce-scatter.54
  1937.9 77.2 reduce-scatter.56
  2017.5 77.2 reduce-scatter.58
  2097.0 27.9 reduce-scatter.48
  2127.1 25.8 reduce-scatter.50
  2183.5 25.7 reduce-scatter.38
  2239.7 25.7 reduce-scatter.46
  2268.0 25.7 reduce-scatter.40
  2296.5 25.7 reduce-scatter.42
  2326.2 69.9 reduce-scatter.34
  (2 shorter events, 51.5 us)
where the time goes:
time: 2410 us
  waiting for transfers between devices  1480 us (61%)
  matrix products  445 us (18%)
  blocking collectives  204 us (8%)
  local copies, waits for them, and re-layouts  123 us (5%)
  other arithmetic  104 us (4%)
  loops' own time  27.6 us (1%)
    reduce_scatter x4, waiting for transfers between devices, grad_partials(): lax.psum_scatter(terms.astype(jnp.bfloat16), 'col', scatter_dimension=1,...  286 us
    reduce_scatter x4, waiting for transfers between devices, partial_sums(): lax.psum_scatter(terms.astype(jnp.bfloat16), 'col', scatter_dimension=1,...  283 us
    all_gather x4, waiting for transfers between devices, features(): return lax.all_gather(state.astype(jnp.bfloat16), 'col', axis=1, tiled=True)  226 us
    all_gather x4, waiting for transfers between devices, grad_features(): return lax.all_gather(value, 'col', axis=1, tiled=True)  167 us
    reduce_scatter x2, waiting for transfers between devices, local(): lax.psum_scatter(weight_part[5].astype(jnp.bfloat16), 'row', scatter_dime...  122 us
    dot_general x12, matrix products, product(): return jnp.dot(left, right, preferred_element_type=jnp.float32)  108 us
    psum x4, blocking collectives, norm_forward(): lax.psum((jnp.sum(residual, axis=1), jnp.sum(residual * residual, axis=1)...  93.6 us
    psum x4, blocking collectives, norm_backward(): lax.psum((jnp.sum(scaled, axis=1), jnp.sum(scaled * normed, axis=1)), 'col')  91.5 us
  transfers between devices with their start and end apart: 34, of which 30 were waited for; matrix products, arithmetic and copies ran while one was open for 13% of the time, Pallas kernels for 0%

commit v1 on v0

v1 whole, which is shorter than its diff:
```python
import functools

import jax
import jax.numpy as jnp
from jax import lax
from jax.experimental import pallas as pl
from jax.experimental.pallas import tpu as pltpu
from jax.sharding import PartitionSpec as P

HEAD_DIM = 128
LAYERS = 2
SEQ_LEN = 1024

EPSILON = 1e-06
MASKED = -1e30
SCALE = HEAD_DIM ** (-0.5)

bf16 = jnp.bfloat16
f32 = jnp.float32


def dot(left, right):
    return lax.dot_general(left, right, (((1,), (0,)), ((), ())), preferred_element_type=f32)


def dot_t(left, right):
    return lax.dot_general(left, right, (((1,), (1,)), ((), ())), preferred_element_type=f32)


def dot_g(left, right):
    return lax.dot_general(left, right, (((0,), (0,)), ((), ())), preferred_element_type=f32)


def attend_kernel(qkv_ref, docs_row_ref, docs_col_ref, mixed_ref, log_ref):
    step = 256
    span = mixed_ref.shape[1]
    key_docs = docs_col_ref[...]
    for head in range(span // HEAD_DIM):
        low = head * HEAD_DIM
        keys = qkv_ref[:, span + low : span + low + HEAD_DIM]
        values_t = qkv_ref[:, 2 * span + low : 2 * span + low + HEAD_DIM].T
        for start in range(0, SEQ_LEN, step):
            query = qkv_ref[start : start + step, low : low + HEAD_DIM]
            scores = dot_t(keys, query) * SCALE
            allowed = key_docs == docs_row_ref[:, start : start + step]
            scores = jnp.where(allowed, scores, MASKED)
            peak = jnp.max(scores, axis=0, keepdims=True)
            weight = jnp.exp(scores - peak)
            total = jnp.sum(weight, axis=0, keepdims=True)
            mixed_t = dot(values_t, weight.astype(bf16)) * (1.0 / total)
            mixed_ref[start : start + step, low : low + HEAD_DIM] = mixed_t.T.astype(bf16)
            log_ref[head, :, start : start + step] = peak + jnp.log(total)


def attend(qkv, span, docs_row, docs_col):
    groups = qkv.shape[1] // (3 * span)
    heads = span // HEAD_DIM
    return pl.pallas_call(
        attend_kernel,
        grid=(groups,),
        in_specs=[
            pl.BlockSpec((SEQ_LEN, 3 * span), lambda g: (0, g)),
            pl.BlockSpec((1, SEQ_LEN), lambda g: (0, 0)),
            pl.BlockSpec((SEQ_LEN, 1), lambda g: (0, 0)),
        ],
        out_specs=[
            pl.BlockSpec((SEQ_LEN, span), lambda g: (0, g)),
            pl.BlockSpec((heads, 1, SEQ_LEN), lambda g: (g, 0, 0)),
        ],
        out_shape=[
            jax.ShapeDtypeStruct((SEQ_LEN, span * groups), bf16),
            jax.ShapeDtypeStruct((heads * groups, 1, SEQ_LEN), f32),
        ],
        compiler_params=pltpu.CompilerParams(vmem_limit_bytes=48 * 1024 * 1024),
        cost_estimate=pl.CostEstimate(
            flops=groups * heads * 8 * SEQ_LEN * SEQ_LEN * HEAD_DIM,
            bytes_accessed=groups * SEQ_LEN * span * 8,
            transcendentals=groups * heads * SEQ_LEN * SEQ_LEN,
        ),
        name="attend",
    )(qkv, docs_row, docs_col)


def attend_back_kernel(
    qkv_ref, grad_ref, log_ref, docs_row_ref, docs_col_ref, out_ref, probs_ref, dscores_ref
):
    step = 256
    span = grad_ref.shape[1]
    key_docs = docs_col_ref[...]
    for head in range(span // HEAD_DIM):
        low = head * HEAD_DIM
        own = slice(low, low + HEAD_DIM)
        keys = qkv_ref[:, span + low : span + low + HEAD_DIM]
        values = qkv_ref[:, 2 * span + low : 2 * span + low + HEAD_DIM]
        for start in range(0, SEQ_LEN, step):
            at = slice(start, start + step)
            scores = dot_t(keys, qkv_ref[at, own]) * SCALE
            allowed = key_docs == docs_row_ref[:, at]
            probs = jnp.exp(jnp.where(allowed, scores, MASKED) - log_ref[head, :, at])
            dprobs = dot_t(values, grad_ref[at, own])
            along = jnp.sum(dprobs * probs, axis=0, keepdims=True)
            probs_ref[:, at] = probs.astype(bf16)
            dscores_ref[:, at] = (probs * (dprobs - along)).astype(bf16)
        dscores = dscores_ref[...]
        out_ref[:, own] = (dot(keys.T, dscores) * SCALE).T.astype(bf16)
        out_ref[:, span + low : span + low + HEAD_DIM] = (
            dot(dscores, qkv_ref[:, own]) * SCALE
        ).astype(bf16)
        out_ref[:, 2 * span + low : 2 * span + low + HEAD_DIM] = dot(
            probs_ref[...], grad_ref[:, own]
        ).astype(bf16)


def attend_back(qkv, grad, log_total, span, docs_row, docs_col):
    groups = qkv.shape[1] // (3 * span)
    heads = span // HEAD_DIM
    return pl.pallas_call(
        attend_back_kernel,
        grid=(groups,),
        in_specs=[
            pl.BlockSpec((SEQ_LEN, 3 * span), lambda g: (0, g)),
            pl.BlockSpec((SEQ_LEN, span), lambda g: (0, g)),
            pl.BlockSpec((heads, 1, SEQ_LEN), lambda g: (g, 0, 0)),
            pl.BlockSpec((1, SEQ_LEN), lambda g: (0, 0)),
            pl.BlockSpec((SEQ_LEN, 1), lambda g: (0, 0)),
        ],
        out_specs=pl.BlockSpec((SEQ_LEN, 3 * span), lambda g: (0, g)),
        out_shape=jax.ShapeDtypeStruct((SEQ_LEN, 3 * span * groups), bf16),
        scratch_shapes=[pltpu.VMEM((SEQ_LEN, SEQ_LEN), bf16)] * 2,
        compiler_params=pltpu.CompilerParams(vmem_limit_bytes=48 * 1024 * 1024),
        cost_estimate=pl.CostEstimate(
            flops=groups * heads * 20 * SEQ_LEN * SEQ_LEN * HEAD_DIM,
            bytes_accessed=groups * SEQ_LEN * span * 16,
            transcendentals=groups * heads * SEQ_LEN * SEQ_LEN,
        ),
        name="attend_back",
    )(qkv, grad, log_total, docs_row, docs_col)


class Place:
    def __init__(self, mesh):
        self.rows = mesh.shape["row"]
        self.cols = mesh.shape["col"]
        self.a = self.cols // 2
        self.b = self.cols // 4
        self.rest = []
        mask = 1
        while mask < self.b:
            self.rest.append(mask)
            mask *= 2
        self.row = lax.axis_index("row")
        self.col = lax.axis_index("col")
        order = [0]
        for mask in self.rest:
            order = order + [item ^ mask for item in order]
        self.order = order

    def bit(self, mask):
        return (self.col // mask) % 2

    def swap(self, value, mask):
        return lax.ppermute(value, "col", [(i, i ^ mask) for i in range(self.cols)])

    def shift(self, value):
        return lax.ppermute(value, "row", [(i, (i + 1) % self.rows) for i in range(self.rows)])


    def near(self, value):
        for mask in self.rest:
            value = jnp.concatenate([value, self.swap(value, mask)], axis=0)
        return value

    def gather(self, value, far):
        other = self.swap(value, far)
        return (self.near(value), self.near(other))

    def near_sum(self, terms):
        for mask in reversed(self.rest):
            half = terms.shape[0] // 2
            got = self.swap(terms[half:].astype(bf16), mask)
            terms = terms[:half].astype(f32) + got.astype(f32)
        return terms

    def scatter(self, own, other, far):
        sent = self.swap(self.near_sum(other).astype(bf16), far)
        return self.near_sum(own) + sent.astype(f32)


    def ordered(self, mine, got, mask, axis):
        low = self.bit(mask) == 0
        return jnp.concatenate(
            [jnp.where(low, mine, got), jnp.where(low, got, mine)], axis=axis
        )

    def to_tokens(self, value):
        own = value.shape[0] // self.cols
        for mask in self.rest + [self.b, self.a]:
            width = value.shape[-1]
            split = value.reshape(-1, 2, own, width)
            bit = self.bit(mask)
            mine = lax.dynamic_index_in_dim(split, bit, 1, keepdims=False).reshape(-1, width)
            sent = lax.dynamic_index_in_dim(split, 1 - bit, 1, keepdims=False).reshape(-1, width)
            value = self.ordered(mine, self.swap(sent, mask), mask, 1)
        return value

    def to_features(self, value):
        own, width = value.shape
        value = value[None]
        for mask in [self.a, self.b] + self.rest[::-1]:
            width = width // 2
            bit = self.bit(mask)
            mine = lax.dynamic_slice_in_dim(value, bit * width, width, 2)
            sent = lax.dynamic_slice_in_dim(value, (1 - bit) * width, width, 2)
            got = self.swap(sent, mask)
            value = self.ordered(mine[:, None], got[:, None], mask, 1)
            value = value.reshape(-1, own, width)
        return value.reshape(-1, width)

    def all_features(self, value):
        for mask in self.rest + [self.b, self.a]:
            value = self.ordered(value, self.swap(value, mask), mask, 1)
        return value


    def weight(self, block, far, axis):
        other_axis = 1 - axis
        size, span = block.shape[axis], block.shape[other_axis]
        shape = [0, 0]
        shape[axis], shape[other_axis] = self.rows * size, 2 * span
        whole = jnp.zeros(shape, block.dtype)
        for step in range(self.rows):
            at = ((self.row - step + self.rows) % self.rows) * size
            other = self.swap(block, far)
            start = [0, 0]
            start[axis] = at
            whole = lax.dynamic_update_slice(whole, block, start)
            start[other_axis] = span
            whole = lax.dynamic_update_slice(whole, other, start)
            if step < self.rows - 1:
                block = self.shift(block)
        return whole

    def weight_sum(self, own, other, far, axis):
        size = own.shape[axis] // self.rows
        total = None
        for step in range(self.rows):
            at = ((self.row - 1 - step + 2 * self.rows) % self.rows) * size
            sent = lax.dynamic_slice_in_dim(other, at, size, axis).astype(bf16)
            part = lax.dynamic_slice_in_dim(own, at, size, axis) + self.swap(sent, far).astype(f32)
            if total is not None:
                part = part + self.shift(total.astype(bf16)).astype(f32)
            total = part
        return total

    def row_sum(self, value):
        mask = 1
        while mask < self.rows:
            value = value + lax.ppermute(
                value, "row", [(i, i ^ mask) for i in range(self.rows)]
            )
            mask *= 2
        return value


def norm_forward(residual, gain, shift):
    mean = jnp.mean(residual, axis=1, keepdims=True)
    center = residual - mean
    inverse = lax.rsqrt(jnp.mean(center * center, axis=1, keepdims=True) + EPSILON)
    normed = center * inverse
    return (normed * gain + shift, normed, inverse)


def norm_backward(grad, normed, inverse, gain):
    scaled = grad * gain
    mean = jnp.mean(scaled, axis=1, keepdims=True)
    along = jnp.mean(scaled * normed, axis=1, keepdims=True)
    result = inverse * (scaled - mean - normed * along)
    return (result, jnp.sum(grad * normed, axis=0), jnp.sum(grad, axis=0))


def gelu(value):
    return jax.nn.gelu(value, approximate=True)


def gelu_slope(value):
    inner = 0.7978845608028654
    cubic = 0.044715
    square = value * value
    tangent = jnp.tanh(inner * value * (1.0 + cubic * square))
    return 0.5 * (1.0 + tangent) + 0.5 * value * (1.0 - tangent * tangent) * inner * (
        1.0 + 3.0 * cubic * square
    )


def layer_forward(place, state, docs, weights, vectors):
    w_qkv, w_out, w_up, w_down = weights
    b_qkv, b_out, gain1, shift1, b_up, b_down, gain2, shift2 = vectors
    own, other = place.gather(state.astype(bf16), place.b)
    qkv_own = (dot(own, w_qkv) + b_qkv).astype(bf16)
    qkv_other = (dot(other, w_qkv) + b_qkv).astype(bf16)
    qkv = jnp.concatenate([qkv_own, qkv_other], axis=0)
    mixed, log_total = attend(qkv, w_out.shape[0] // 2, *docs)
    half = mixed.shape[0] // 2
    terms_other = dot(mixed[half:], w_out).astype(bf16)
    terms_own = dot(mixed[:half], w_out).astype(bf16)
    branch = place.scatter(terms_own, terms_other, place.b) + b_out
    first, normed1, inverse1 = norm_forward(state + branch, gain1, shift1)
    first_own, first_other = place.gather(first.astype(bf16), place.a)
    hidden_own = dot(first_own, w_up) + b_up
    hidden_other = dot(first_other, w_up) + b_up
    active_own = gelu(hidden_own).astype(bf16)
    active_other = gelu(hidden_other).astype(bf16)
    terms_other = dot(active_other, w_down).astype(bf16)
    terms_own = dot(active_own, w_down).astype(bf16)
    second = place.scatter(terms_own, terms_other, place.a) + b_down
    result, normed2, inverse2 = norm_forward(first + second, gain2, shift2)
    saved = (
        (own, other),
        qkv,
        mixed,
        log_total,
        normed1,
        inverse1,
        (first_own, first_other),
        (hidden_own, hidden_other),
        (active_own, active_other),
        normed2,
        inverse2,
    )
    return (result, saved)


def join(pair):
    return jnp.concatenate(pair, axis=0)


def layer_backward(place, grad, docs, weights, vectors, saved):
    w_qkv, w_out, w_up, w_down = weights
    b_qkv, b_out, gain1, shift1, b_up, b_down, gain2, shift2 = vectors
    tokens, qkv, mixed, log_total, normed1, inverse1, firsts, hiddens, actives, normed2, inverse2 = saved
    dr2, gain2_grad, shift2_grad = norm_backward(grad, normed2, inverse2, gain2)
    dsecond = dr2.astype(bf16)
    seconds = place.gather(dsecond, place.a)
    dhid = tuple(
        (dot_t(second, w_down) * gelu_slope(hidden)).astype(bf16)
        for second, hidden in zip(seconds, hiddens)
    )
    terms = tuple(dot_t(part, w_up).astype(bf16) for part in dhid)
    dfirst = dr2 + place.scatter(terms[0], terms[1], place.a)
    down_grad = dot_g(join(actives), join(seconds))
    dhidden = join(dhid)
    up_grad = dot_g(join(firsts), dhidden)
    dr1, gain1_grad, shift1_grad = norm_backward(dfirst, normed1, inverse1, gain1)
    dbranch = dr1.astype(bf16)
    branches = place.gather(dbranch, place.b)
    branch = join(branches)
    dmixed = join([dot_t(part, w_out).astype(bf16) for part in branches])
    out_grad = dot_g(mixed, branch)
    dqkv = attend_back(qkv, dmixed, log_total, w_out.shape[0] // 2, *docs)
    half = dqkv.shape[0] // 2
    terms_other = dot_t(dqkv[half:], w_qkv).astype(bf16)
    terms_own = dot_t(dqkv[:half], w_qkv).astype(bf16)
    dx = dr1 + place.scatter(terms_own, terms_other, place.b)
    qkv_grad = dot_g(join(tokens), dqkv)
    token_sums = jnp.stack(
        [
            jnp.sum(dbranch, axis=0, dtype=f32),
            gain1_grad,
            shift1_grad,
            jnp.sum(dsecond, axis=0, dtype=f32),
            gain2_grad,
            shift2_grad,
        ]
    )
    sums = (
        qkv_grad,
        out_grad,
        up_grad,
        down_grad,
        token_sums,
        jnp.sum(dqkv, axis=0, dtype=f32),
        jnp.sum(dhidden, axis=0, dtype=f32),
    )
    return (dx, sums)


def local(
    mesh,
    tokens,
    cotangent,
    segments,
    query_weight,
    query_bias,
    key_weight,
    value_weight,
    value_bias,
    output_weight,
    output_bias,
    first_gain,
    first_shift,
    up_weight,
    up_bias,
    down_weight,
    down_bias,
    second_gain,
    second_shift,
):
    place = Place(mesh)
    span = query_weight.shape[1]
    hidden_span = up_weight.shape[1]
    own = tokens.shape[0] // place.cols

    state = place.to_tokens(tokens).astype(f32)
    masks = place.order + [item ^ place.b for item in place.order]
    docs = jnp.concatenate(
        [
            lax.dynamic_slice_in_dim(segments, jnp.bitwise_xor(place.col, mask) * own, own, 0)
            for mask in masks
        ]
    )
    docs = (docs[None, :], docs[:, None])

    vectors = place.all_features(
        jnp.stack([output_bias, first_gain, first_shift, down_bias, second_gain, second_shift])
    )
    pair = jnp.concatenate([query_bias, jnp.zeros_like(query_bias), value_bias])
    b_qkv = jnp.concatenate([pair, place.swap(pair, place.a)])
    b_up = jnp.concatenate([up_bias, place.swap(up_bias, place.b)])
    vectors = (b_qkv, vectors[0], vectors[1], vectors[2], b_up, vectors[3], vectors[4], vectors[5])

    w_qkv = place.weight(
        jnp.concatenate([query_weight, key_weight, value_weight], axis=1), place.a, 0
    )
    w_out = place.weight(output_weight, place.a, 1)
    w_up = place.weight(up_weight, place.b, 0)
    w_down = place.weight(down_weight, place.b, 1)
    weights = (w_qkv, w_out, w_up, w_down)

    kept = []
    for depth in range(LAYERS):
        state, saved = layer_forward(place, state, docs, weights, vectors)
        kept.append(saved)
    output = place.to_features(state.astype(bf16))

    grad = place.to_tokens(cotangent).astype(f32)
    totals = None
    for depth in reversed(range(LAYERS)):
        grad, sums = layer_backward(place, grad, docs, weights, vectors, kept[depth])
        totals = sums if totals is None else tuple(x + y for x, y in zip(totals, sums))
    grad_tokens = place.to_features(grad.astype(bf16)).astype(f32)

    qkv_grad, out_grad, up_grad, down_grad, token_sums, qkv_sums, hidden_sums = totals
    down = place.weight_sum(
        down_grad[:hidden_span], down_grad[hidden_span:], place.b, 1
    )
    up = place.weight_sum(up_grad[:, :hidden_span], up_grad[:, hidden_span:], place.b, 0)
    out = place.weight_sum(out_grad[:span], out_grad[span:], place.a, 1)
    qkv = place.weight_sum(
        qkv_grad[:, : 3 * span], qkv_grad[:, 3 * span :], place.a, 0
    )

    for mask in [place.a, place.b] + place.rest[::-1]:
        width = token_sums.shape[1] // 2
        bit = place.bit(mask)
        mine = lax.dynamic_slice_in_dim(token_sums, bit * width, width, 1)
        sent = lax.dynamic_slice_in_dim(token_sums, (1 - bit) * width, width, 1)
        token_sums = mine + place.swap(sent, mask)
    qkv_sums = qkv_sums[: 3 * span] + place.swap(qkv_sums[3 * span :], place.a)
    hidden_sums = hidden_sums[:hidden_span] + place.swap(hidden_sums[hidden_span:], place.b)
    sums = place.row_sum(
        jnp.concatenate([token_sums.reshape(-1), qkv_sums, hidden_sums])
    )
    token_sums = sums[: 6 * span].reshape(6, span)
    qkv_sums = sums[6 * span : 9 * span]
    hidden_sums = sums[9 * span :]
    return (
        output,
        grad_tokens,
        qkv[:, :span],
        qkv_sums[:span],
        qkv[:, span : 2 * span],
        qkv[:, 2 * span :],
        qkv_sums[2 * span :],
        out,
        token_sums[0],
        token_sums[1],
        token_sums[2],
        up,
        hidden_sums,
        down,
        token_sums[3],
        token_sums[4],
        token_sums[5],
    )


def solution(mesh):
    both, col, back = P("row", "col"), P("col"), P("col", "row")
    return jax.shard_map(
        functools.partial(local, mesh),
        mesh=mesh,
        in_specs=(
            both, both, P("row"), both, col, both, both, col, back, col, col, col, both, col, back,
            col, col, col,
        ),
        out_specs=(
            both, both, both, col, both, both, col, back, col, col, col, both, col, back, col, col,
            col,
        ),
        check_vma=False,
    )
```

time: 2410 us -> 1360 us (0.56)
  waiting for transfers between devices: 1480 us -> 739 us
  blocking collectives: 204 us -> 0 us
  matrix products: 445 us -> 289 us
  starting transfers between devices: 2.89 us -> 99.4 us
  Pallas kernels: 0 us -> 54.7 us
  local copies, waits for them, and re-layouts: 123 us -> 87.6 us
  loops' own time: 27.6 us -> 0 us
    reduce_scatter x20 -> x0, waiting for transfers between devices: 890 us -> none  [the longest x4 286 us: grad_partials(): lax.psum_scatter(terms.astype(jnp.bfloat16), 'col', scatter_dimension=1,...]
    ppermute x0 -> x128, waiting for transfers between devices: none -> 739 us  [the longest x102 598 us: swap(): return lax.ppermute(value, 'col', [(i, i ^ mask) for i in range(self.cols)])]
    all_gather x14 -> x0, waiting for transfers between devices: 589 us -> none  [the longest x4 226 us: features(): return lax.all_gather(state.astype(jnp.bfloat16), 'col', axis=1, tiled=True)]
    psum x9 -> x0, blocking collectives: 204 us -> none  [the longest x4 93.6 us: norm_forward(): lax.psum((jnp.sum(residual, axis=1), jnp.sum(residual * residual, axis=1)...]
    dot_general x92 -> x40, matrix products: 445 us -> 289 us  [the longest x16 106 us: dot_t(): lax.dot_general(left, right, (((1,), (1,)), ((), ())), preferred_element_...]
    ppermute x0 -> x128, starting transfers between devices: none -> 99.4 us  [the longest x102 82.6 us: swap(): return lax.ppermute(value, 'col', [(i, i ^ mask) for i in range(self.cols)])]
    dynamic_slice x104 -> x11, local copies, waits for them, and re-layouts: 62.2 us -> 5.75 us  [the longest x3 2.86 us: to_tokens(): lax.dynamic_index_in_dim(split, bit, 1, keepdims=False).reshape(-1, width)]
    pallas_call x0 -> x4, Pallas kernels: none -> 54.7 us  [the longest x2 28.7 us: attend_back(): pl.pallas_call(attend_back_kernel, grid=(groups,), in_specs=[pl.BlockSpec...]
  transfers between devices with their start and end apart: 34 -> 128, of which waited for: 30 -> 59; matrix products, arithmetic and copies ran while one was open for 13% -> 27% of each run, Pallas kernels for 0% -> 1%
where the time goes in v1:
time: 1360 us
  waiting for transfers between devices  739 us (54%)
  matrix products  289 us (21%)
  starting transfers between devices  99.4 us (7%)
  local copies, waits for them, and re-layouts  87.6 us (6%)
  other arithmetic  82.2 us (6%)
  Pallas kernels  54.7 us (4%)
    ppermute x102, waiting for transfers between devices, swap(): return lax.ppermute(value, 'col', [(i, i ^ mask) for i in range(self.cols)])  598 us
    ppermute x24, waiting for transfers between devices, shift(): lax.ppermute(value, 'row', [(i, (i + 1) % self.rows) for i in range(self....  140 us
    dot_general x16, matrix products, dot_t(): lax.dot_general(left, right, (((1,), (1,)), ((), ())), preferred_element_...  106 us
    dot_general x8, matrix products, dot_g(): lax.dot_general(left, right, (((0,), (0,)), ((), ())), preferred_element_...  102 us
    ppermute x102, starting transfers between devices, swap(): return lax.ppermute(value, 'col', [(i, i ^ mask) for i in range(self.cols)])  82.6 us
    dot_general x16, matrix products, dot(): lax.dot_general(left, right, (((1,), (0,)), ((), ())), preferred_element_...  81.5 us
    pallas_call x2, Pallas kernels, attend_back(): pl.pallas_call(attend_back_kernel, grid=(groups,), in_specs=[pl.BlockSpec...  28.7 us
  transfers between devices with their start and end apart: 128, of which 59 were waited for; matrix products, arithmetic and copies ran while one was open for 27% of the time, Pallas kernels for 1%

profile of v1, /device:TPU:0, one launch (start us, length us, event | category | flops | bytes accessed | tf_op | source)
XLA Modules:
  0.0 1356.1 jit_solution(9385766656475940572)
XLA Ops:
  16.2 16.4 %collective-permute-done.15 = bf16[256,512]{1,0:T(8,128)(2,1)} collective-permute-done((bf16[256,512]{1,0:T(8,128)(2,1)}, bf16[256,512]{1,0:T(8,128)(2,1)}, u32[]{:S(2)}, u32[]{:S(2)}) %collective-permute-start.15) | collective-permute-done | bytes 262176 | tf_op jit(solution)/shard_map/ppermute | solution.py:165
  101.0 15.6 %collective-permute-done.8 = bf16[512,768]{1,0:T(8,128)(2,1)S(1)} collective-permute-done((bf16[512,768]{1,0:T(8,128)(2,1)}, bf16[512,768]{1,0:T(8,128)(2,1)S(1)}, u32[]{:S(2)}, u32[]{:S(2)}) %collective-permute-start.8) | collective-permute-done | bytes 786464 | tf_op jit(solution)/shard_map/ppermute | solution.py:162
  116.8 14.8 %collective-permute-done.10 = bf16[512,768]{1,0:T(8,128)(2,1)S(1)} collective-permute-done((bf16[512,768]{1,0:T(8,128)(2,1)S(1)}, bf16[512,768]{1,0:T(8,128)(2,1)S(1)}, u32[]{:S(2)}, u32[]{:S(2)}) %collective-permute-start.10) | collective-permute-done | bytes 786464 | tf_op jit(solution)/shard_map/ppermute | solution.py:162
  169.0 23.9 %collective-permute-done.25 = f32[6,512]{1,0:T(8,128)S(1)} collective-permute-done((f32[6,512]{1,0:T(8,128)S(1)}, f32[6,512]{1,0:T(8,128)S(1)}, u32[]{:S(2)}, u32[]{:S(2)}) %collective-permute-start.25) | collective-permute-done | bytes 12320 | tf_op jit(solution)/shard_map/ppermute | solution.py:162
  211.9 31.6 %collective-permute-done.35 = f32[1024]{0:T(1024)S(1)} collective-permute-done((f32[1024]{0:T(1024)S(1)}, f32[1024]{0:T(1024)S(1)}, u32[]{:S(2)}, u32[]{:S(2)}) %collective-permute-start.35) | collective-permute-done | bytes 4128 | tf_op jit(solution)/shard_map/ppermute | solution.py:162
  272.8 19.6 %collective-permute-done.38 = bf16[1024,512]{1,0:T(8,128)(2,1)} collective-permute-done((bf16[1024,512]{1,0:T(8,128)(2,1)}, bf16[1024,512]{1,0:T(8,128)(2,1)}, u32[]{:S(2)}, u32[]{:S(2)}) %collective-permute-start.38) | collective-permute-done | bytes 1048608 | tf_op jit(solution)/shard_map/ppermute | solution.py:162
  316.3 21.0 %collective-permute-done.40 = bf16[1024,512]{1,0:T(8,128)(2,1)S(1)} collective-permute-done((bf16[1024,512]{1,0:T(8,128)(2,1)}, bf16[1024,512]{1,0:T(8,128)(2,1)S(1)}, u32[]{:S(2)}, u32[]{:S(2)}) %collective-permute-start.40) | collective-permute-done | bytes 1048608 | tf_op jit(solution)/shard_map/ppermute | solution.py:162
  338.8 20.9 %collective-permute-done.34 = bf16[512,1024]{1,0:T(8,128)(2,1)S(1)} collective-permute-done((bf16[512,1024]{1,0:T(8,128)(2,1)}, bf16[512,1024]{1,0:T(8,128)(2,1)S(1)}, u32[]{:S(2)}, u32[]{:S(2)}) %collective-permute-start.34) | collective-permute-done | bytes 1048608 | tf_op jit(solution)/shard_map/ppermute | solution.py:162
  359.9 19.5 %collective-permute-done.42 = bf16[1024,512]{1,0:T(8,128)(2,1)S(1)} collective-permute-done((bf16[1024,512]{1,0:T(8,128)(2,1)}, bf16[1024,512]{1,0:T(8,128)(2,1)S(1)}, u32[]{:S(2)}, u32[]{:S(2)}) %collective-permute-start.42) | collective-permute-done | bytes 1048608 | tf_op jit(solution)/shard_map/ppermute | solution.py:162
  411.3 23.3 %collective-permute-done.47 = bf16[256,2048]{1,0:T(8,128)(2,1)S(1)} collective-permute-done((bf16[256,2048]{1,0:T(8,128)(2,1)S(1)}, bf16[256,2048]{1,0:T(8,128)(2,1)S(1)}, u32[]{:S(2)}, u32[]{:S(2)}) %collective-permute-start.47) | collective-permute-done | bytes 1048608 | tf_op jit(solution)/shard_map/ppermute | solution.py:162
  437.8 22.9 %collective-permute-done.49 = bf16[256,2048]{1,0:T(8,128)(2,1)S(1)} collective-permute-done((bf16[256,2048]{1,0:T(8,128)(2,1)S(1)}, bf16[256,2048]{1,0:T(8,128)(2,1)S(1)}, u32[]{:S(2)}, u32[]{:S(2)}) %collective-permute-start.49) | collective-permute-done | bytes 1048608 | tf_op jit(solution)/shard_map/ppermute | solution.py:162
  490.5 23.4 %collective-permute-done.53 = bf16[256,2048]{1,0:T(8,128)(2,1)S(1)} collective-permute-done((bf16[256,2048]{1,0:T(8,128)(2,1)S(1)}, bf16[256,2048]{1,0:T(8,128)(2,1)S(1)}, u32[]{:S(2)}, u32[]{:S(2)}) %collective-permute-start.53) | collective-permute-done | bytes 1048608 | tf_op jit(solution)/shard_map/ppermute | solution.py:162
  519.2 21.4 %collective-permute-done.56 = bf16[256,2048]{1,0:T(8,128)(2,1)S(1)} collective-permute-done((bf16[256,2048]{1,0:T(8,128)(2,1)S(1)}, bf16[256,2048]{1,0:T(8,128)(2,1)S(1)}, u32[]{:S(2)}, u32[]{:S(2)}) %collective-permute-start.56) | collective-permute-done | bytes 1048608 | tf_op jit(solution)/shard_map/ppermute | solution.py:162
  587.1 34.5 %collective-permute-done.65 = bf16[256,1024]{1,0:T(8,128)(2,1)S(1)} collective-permute-done((bf16[256,1024]{1,0:T(8,128)(2,1)S(1)}, bf16[256,1024]{1,0:T(8,128)(2,1)S(1)}, u32[]{:S(2)}, u32[]{:S(2)}) %collective-permute-start.65) | collective-permute-done | bytes 524320 | tf_op jit(solution)/shard_map/ppermute | solution.py:162
  626.3 23.4 %collective-permute-done.68 = bf16[256,2048]{1,0:T(8,128)(2,1)S(1)} collective-permute-done((bf16[256,2048]{1,0:T(8,128)(2,1)S(1)}, bf16[256,2048]{1,0:T(8,128)(2,1)S(1)}, u32[]{:S(2)}, u32[]{:S(2)}) %collective-permute-start.68) | collective-permute-done | bytes 1048608 | tf_op jit(solution)/shard_map/ppermute | solution.py:162
  690.5 23.4 %collective-permute-done.71 = bf16[256,2048]{1,0:T(8,128)(2,1)S(1)} collective-permute-done((bf16[256,2048]{1,0:T(8,128)(2,1)S(1)}, bf16[256,2048]{1,0:T(8,128)(2,1)S(1)}, u32[]{:S(2)}, u32[]{:S(2)}) %collective-permute-start.71) | collective-permute-done | bytes 1048608 | tf_op jit(solution)/shard_map/ppermute | solution.py:162
  720.5 23.4 %collective-permute-done.73 = bf16[256,2048]{1,0:T(8,128)(2,1)S(1)} collective-permute-done((bf16[256,2048]{1,0:T(8,128)(2,1)S(1)}, bf16[256,2048]{1,0:T(8,128)(2,1)S(1)}, u32[]{:S(2)}, u32[]{:S(2)}) %collective-permute-start.73) | collective-permute-done | bytes 1048608 | tf_op jit(solution)/shard_map/ppermute | solution.py:162
  751.2 14.4 %attend_back.2 = bf16[1024,1536]{1,0:T(8,128)(2,1)S(1)} custom-call(bf16[1024,1536]{1,0:T(8,128)(2,1)} %copy-done.1, bf16[1024,512]{1,0:T(8,128)(2,1)S(1)} %pad_maximum_fusion.14.grad_ref, f32[4,1,1024]{2,1,0:T(1,128)S(1)} %get-tuple-element.23.log_ref, s32[1,1024]{1,0:T(1,128)S(1)} %bitcast.177, s32[1024,1]{1,0:T(8,128)S(1)} %copy-done.3), custom_call_target="tpu_custom_call" | custom-call | flops 10737418240 | bytes 8388608 | tf_op jit(solution)/shard_map/attend_back/pallas_call | solution.py:117
  818.9 15.3 %collective-permute-done.80 = bf16[256,2048]{1,0:T(8,128)(2,1)} collective-permute-done((bf16[256,2048]{1,0:T(8,128)(2,1)}, bf16[256,2048]{1,0:T(8,128)(2,1)}, u32[]{:S(2)}, u32[]{:S(2)}) %collective-permute-start.80) | collective-permute-done | bytes 1048608 | tf_op jit(solution)/shard_map/ppermute | solution.py:162
  877.9 14.0 %fusion.104 = f32[2048,2048]{1,0:T(8,128)} fusion(bf16[256,2048]{1,0:T(8,128)(2,1)S(1)} %copy-done.94, bf16[256,2048]{1,0:T(8,128)(2,1)} %collective-permute-done.44, bf16[256,2048]{1,0:T(8,128)(2,1)S(1)} %copy-done.96, bf16[256,2048]{1,0:T(8,128)(2,1)} %fusion.205, bf16[512,2048]{1,0:T(8,128)(2,1)S(1)} %copy-done.44, bf16[512,2048]{1,0:T(8,128)(2,1)S(1)} %copy-done.42), kind=kOutput, calls=%fused_computation.125 | convolution fusion | flops 8615100416 | bytes 25165824 | tf_op jit(solution)/shard_map/dot_general | solution.py:31
  891.9 17.7 %convolution_add_fusion.2 = f32[2048,2048]{1,0:T(8,128)} fusion(f32[2048,2048]{1,0:T(8,128)} %fusion.104, bf16[256,2048]{1,0:T(8,128)(2,1)} %copy-done.104, bf16[256,2048]{1,0:T(8,128)(2,1)} %copy-done.103, bf16[256,2048]{1,0:T(8,128)(2,1)} %copy-done.105, bf16[256,2048]{1,0:T(8,128)(2,1)} %copy-done.60, bf16[512,2048]{1,0:T(8,128)(2,1)} %copy-done.40, ...), kind=kOutput, calls=%fused_computation.4 | convolution fusion | flops 8619294720 | bytes 41943040 | tf_op jit(solution)/shard_map/dot_general | solution.py:31
  917.4 14.4 %fusion.122 = f32[2048,2048]{1,0:T(8,128)} fusion(bf16[512,2048]{1,0:T(8,128)(2,1)S(1)} %copy-done.109, bf16[512,2048]{1,0:T(8,128)(2,1)S(1)} %copy-done.107, bf16[256,2048]{1,0:T(8,128)(2,1)} %collective-permute-done.81, bf16[256,2048]{1,0:T(8,128)(2,1)} %collective-permute-done.80, bf16[256,2048]{1,0:T(8,128)(2,1)} %collective-permute-done.78, ...), kind=kOutput, calls=%fused_computation.143 | convolution fusion | flops 8615100416 | bytes 25165824 | tf_op jit(solution)/shard_map/dot_general | solution.py:31
  931.7 18.2 %convolution_add_fusion.1 = f32[2048,2048]{1,0:T(8,128)} fusion(f32[2048,2048]{1,0:T(8,128)} %fusion.122, bf16[512,2048]{1,0:T(8,128)(2,1)} %copy-done.30, bf16[512,2048]{1,0:T(8,128)(2,1)} %copy-done.29, bf16[256,2048]{1,0:T(8,128)(2,1)} %collective-permute-done.69, bf16[256,2048]{1,0:T(8,128)(2,1)} %copy-done.49, bf16[256,2048]{1,0:T(8,128)(2,1)} %copy-done.50, ...), kind=kOutput, calls=%fused_computation.3 | convolution fusion | flops 8619294720 | bytes 41943040 | tf_op jit(solution)/shard_map/dot_general | solution.py:31
  1043.2 52.6 %collective-permute-done.101 = f32[6,512]{1,0:T(8,128)S(1)} collective-permute-done((f32[6,512]{1,0:T(8,128)S(1)}, f32[6,512]{1,0:T(8,128)S(1)}, u32[]{:S(2)}, u32[]{:S(2)}) %collective-permute-start.101) | collective-permute-done | bytes 12320 | tf_op jit(solution)/shard_map/ppermute | solution.py:162
  1099.2 24.8 %collective-permute-done.119 = bf16[512,1024]{1,0:T(8,128)(2,1)} collective-permute-done((bf16[512,1024]{1,0:T(8,128)(2,1)}, bf16[512,1024]{1,0:T(8,128)(2,1)}, u32[]{:S(2)}, u32[]{:S(2)}) %collective-permute-start.119) | collective-permute-done | bytes 1048608 | tf_op jit(solution)/shard_map/ppermute | solution.py:165
  1129.3 17.1 %collective-permute-done.126 = bf16[1024,512]{1,0:T(8,128)(2,1)} collective-permute-done((bf16[1024,512]{1,0:T(8,128)(2,1)}, bf16[1024,512]{1,0:T(8,128)(2,1)}, u32[]{:S(2)}, u32[]{:S(2)}) %collective-permute-start.126) | collective-permute-done | bytes 1048608 | tf_op jit(solution)/shard_map/ppermute | solution.py:165
  1157.4 14.3 %attend_back.3 = bf16[1024,1536]{1,0:T(8,128)(2,1)S(1)} custom-call(bf16[1024,1536]{1,0:T(8,128)(2,1)} %copy-done, bf16[1024,512]{1,0:T(8,128)(2,1)S(1)} %pad_maximum_fusion.15.grad_ref, f32[4,1,1024]{2,1,0:T(1,128)S(1)} %get-tuple-element.24.log_ref, s32[1,1024]{1,0:T(1,128)S(1)} %bitcast.178, s32[1024,1]{1,0:T(8,128)S(1)} %copy-done.4), custom_call_target="tpu_custom_call" | custom-call | flops 10737418240 | bytes 8388608 | tf_op jit(solution)/shard_map/attend_back/pallas_call | solution.py:117
  1182.6 13.1 fusion.71
  1195.7 13.5 convolution_add_fusion
  1246.0 16.7 %collective-permute-done.109 = bf16[256,512]{1,0:T(8,128)(2,1)S(1)} collective-permute-done((bf16[256,512]{1,0:T(8,128)(2,1)S(1)}, bf16[256,512]{1,0:T(8,128)(2,1)S(1)}, u32[]{:S(2)}, u32[]{:S(2)}) %collective-permute-start.109) | collective-permute-done | bytes 262176 | tf_op jit(solution)/shard_map/ppermute | solution.py:162
  1273.0 15.8 %collective-permute-done.89 = bf16[256,2048]{1,0:T(8,128)(2,1)S(1)} collective-permute-done((bf16[256,2048]{1,0:T(8,128)(2,1)S(1)}, bf16[256,2048]{1,0:T(8,128)(2,1)S(1)}, u32[]{:S(2)}, u32[]{:S(2)}) %collective-permute-start.89) | collective-permute-done | bytes 1048608 | tf_op jit(solution)/shard_map/ppermute | solution.py:162
  1289.5 17.6 %collective-permute-done.121 = bf16[1024,512]{1,0:T(8,128)(2,1)S(1)} collective-permute-done((bf16[1024,512]{1,0:T(8,128)(2,1)S(1)}, bf16[1024,512]{1,0:T(8,128)(2,1)S(1)}, u32[]{:S(2)}, u32[]{:S(2)}) %collective-permute-start.121) | collective-permute-done | bytes 1048608 | tf_op jit(solution)/shard_map/ppermute | solution.py:162
  (740 shorter events, 693.9 us)
Async XLA Ops:
  82.8 48.8 %collective-permute-start.3 = (bf16[256,2048]{1,0:T(8,128)(2,1)S(1)}, bf16[256,2048]{1,0:T(8,128)(2,1)S(1)}, u32[]{:S(2)}, u32[]{:S(2)}) collective-permute-start(bf16[256,2048]{1,0:T(8,128)(2,1)S(1)} %pad_maximum_fusion.8), channel_id=1, source_target_pairs={{0,1},{1,0},{2,3},{3,2},{4,5},{5,4},{6,7},{7,6},{8,9},{9,8},{10,11... | collective-permute-start | bytes 3145736 | tf_op jit(solution)/shard_map/ppermute | solution.py:162
  159.8 49.0 %collective-permute-start.37 = (bf16[1024,512]{1,0:T(8,128)(2,1)}, bf16[1024,512]{1,0:T(8,128)(2,1)}, u32[]{:S(2)}, u32[]{:S(2)}) collective-permute-start(bf16[1024,512]{1,0:T(8,128)(2,1)} %param.32), channel_id=1, source_target_pairs={{0,8},{8,16},{16,24},{24,0},{1,9},{9,17},{17,25},{25,1},{2,10},{10... | collective-permute-start | bytes 3145736 | tf_op jit(solution)/shard_map/ppermute | solution.py:165
  196.9 48.4 %collective-permute-start.28 = (bf16[512,1024]{1,0:T(8,128)(2,1)S(1)}, bf16[512,1024]{1,0:T(8,128)(2,1)S(1)}, u32[]{:S(2)}, u32[]{:S(2)}) collective-permute-start(bf16[512,1024]{1,0:T(8,128)(2,1)S(1)} %copy-done.51), channel_id=1, source_target_pairs={{0,2},{1,3},{2,0},{3,1},{4,6},{5,7},{6,4},{7,5},{8,10},{9,11},{10,... | collective-permute-start | bytes 3145736 | tf_op jit(solution)/shard_map/ppermute | solution.py:162
  198.2 47.8 %collective-permute-start.31 = (bf16[512,1024]{1,0:T(8,128)(2,1)}, bf16[512,1024]{1,0:T(8,128)(2,1)}, u32[]{:S(2)}, u32[]{:S(2)}) collective-permute-start(bf16[512,1024]{1,0:T(8,128)(2,1)} %collective-permute-done.29), channel_id=1, source_target_pairs={{0,8},{8,16},{16,24},{24,0},{1,9},{9,17},{17,25},{25,1},{2,10},{10... | collective-permute-start | bytes 3145736 | tf_op jit(solution)/shard_map/ppermute | solution.py:165
  208.8 44.9 %collective-permute-start.39 = (bf16[1024,512]{1,0:T(8,128)(2,1)}, bf16[1024,512]{1,0:T(8,128)(2,1)}, u32[]{:S(2)}, u32[]{:S(2)}) collective-permute-start(bf16[1024,512]{1,0:T(8,128)(2,1)} %collective-permute-done.37), channel_id=1, source_target_pairs={{0,8},{8,16},{16,24},{24,0},{1,9},{9,17},{17,25},{25,1},{2,10},{10... | collective-permute-start | bytes 3145736 | tf_op jit(solution)/shard_map/ppermute | solution.py:165
  208.9 46.4 %collective-permute-start.36 = (bf16[1024,512]{1,0:T(8,128)(2,1)S(1)}, bf16[1024,512]{1,0:T(8,128)(2,1)S(1)}, u32[]{:S(2)}, u32[]{:S(2)}) collective-permute-start(bf16[1024,512]{1,0:T(8,128)(2,1)S(1)} %copy-done.52), channel_id=1, source_target_pairs={{0,2},{1,3},{2,0},{3,1},{4,6},{5,7},{6,4},{7,5},{8,10},{9,11},{10,... | collective-permute-start | bytes 3145736 | tf_op jit(solution)/shard_map/ppermute | solution.py:162
  245.3 47.1 %collective-permute-start.38 = (bf16[1024,512]{1,0:T(8,128)(2,1)}, bf16[1024,512]{1,0:T(8,128)(2,1)}, u32[]{:S(2)}, u32[]{:S(2)}) collective-permute-start(bf16[1024,512]{1,0:T(8,128)(2,1)} %collective-permute-done.37), channel_id=1, source_target_pairs={{0,2},{1,3},{2,0},{3,1},{4,6},{5,7},{6,4},{7,5},{8,10},{9,11},{10,... | collective-permute-start | bytes 3145736 | tf_op jit(solution)/shard_map/ppermute | solution.py:162
  246.0 49.3 %collective-permute-start.33 = (bf16[512,1024]{1,0:T(8,128)(2,1)}, bf16[512,1024]{1,0:T(8,128)(2,1)}, u32[]{:S(2)}, u32[]{:S(2)}) collective-permute-start(bf16[512,1024]{1,0:T(8,128)(2,1)} %collective-permute-done.31), channel_id=1, source_target_pairs={{0,8},{8,16},{16,24},{24,0},{1,9},{9,17},{17,25},{25,1},{2,10},{10... | collective-permute-start | bytes 3145736 | tf_op jit(solution)/shard_map/ppermute | solution.py:165
  253.8 44.1 %collective-permute-start.41 = (bf16[1024,512]{1,0:T(8,128)(2,1)}, bf16[1024,512]{1,0:T(8,128)(2,1)}, u32[]{:S(2)}, u32[]{:S(2)}) collective-permute-start(bf16[1024,512]{1,0:T(8,128)(2,1)} %collective-permute-done.39), channel_id=1, source_target_pairs={{0,8},{8,16},{16,24},{24,0},{1,9},{9,17},{17,25},{25,1},{2,10},{10... | collective-permute-start | bytes 3145736 | tf_op jit(solution)/shard_map/ppermute | solution.py:165
  256.3 44.4 %collective-permute-start.44 = (bf16[256,2048]{1,0:T(8,128)(2,1)}, bf16[256,2048]{1,0:T(8,128)(2,1)}, u32[]{:S(2)}, u32[]{:S(2)}) collective-permute-start(bf16[256,2048]{1,0:T(8,128)(2,1)} %fusion.205), channel_id=1, source_target_pairs={{0,4},{1,5},{2,6},{3,7},{4,0},{5,1},{6,2},{7,3},{8,12},{9,13},{10,... | collective-permute-start | bytes 3145736 | tf_op jit(solution)/shard_map/ppermute | solution.py:162
  269.9 44.8 %collective-permute-start.32 = (bf16[512,1024]{1,0:T(8,128)(2,1)}, bf16[512,1024]{1,0:T(8,128)(2,1)S(1)}, u32[]{:S(2)}, u32[]{:S(2)}) collective-permute-start(bf16[512,1024]{1,0:T(8,128)(2,1)} %collective-permute-done.31), channel_id=1, source_target_pairs={{0,2},{1,3},{2,0},{3,1},{4,6},{5,7},{6,4},{7,5},{8,10},{9,11},{10,... | collective-permute-start | bytes 3145736 | tf_op jit(solution)/shard_map/ppermute | solution.py:162
  292.4 44.8 %collective-permute-start.40 = (bf16[1024,512]{1,0:T(8,128)(2,1)}, bf16[1024,512]{1,0:T(8,128)(2,1)S(1)}, u32[]{:S(2)}, u32[]{:S(2)}) collective-permute-start(bf16[1024,512]{1,0:T(8,128)(2,1)} %collective-permute-done.39), channel_id=1, source_target_pairs={{0,2},{1,3},{2,0},{3,1},{4,6},{5,7},{6,4},{7,5},{8,10},{9,11},{10,... | collective-permute-start | bytes 3145736 | tf_op jit(solution)/shard_map/ppermute | solution.py:162
  295.3 64.4 %collective-permute-start.34 = (bf16[512,1024]{1,0:T(8,128)(2,1)}, bf16[512,1024]{1,0:T(8,128)(2,1)S(1)}, u32[]{:S(2)}, u32[]{:S(2)}) collective-permute-start(bf16[512,1024]{1,0:T(8,128)(2,1)} %collective-permute-done.33), channel_id=1, source_target_pairs={{0,2},{1,3},{2,0},{3,1},{4,6},{5,7},{6,4},{7,5},{8,10},{9,11},{10,... | collective-permute-start | bytes 3145736 | tf_op jit(solution)/shard_map/ppermute | solution.py:162
  297.8 81.6 %collective-permute-start.42 = (bf16[1024,512]{1,0:T(8,128)(2,1)}, bf16[1024,512]{1,0:T(8,128)(2,1)S(1)}, u32[]{:S(2)}, u32[]{:S(2)}) collective-permute-start(bf16[1024,512]{1,0:T(8,128)(2,1)} %collective-permute-done.41), channel_id=1, source_target_pairs={{0,2},{1,3},{2,0},{3,1},{4,6},{5,7},{6,4},{7,5},{8,10},{9,11},{10,... | collective-permute-start | bytes 3145736 | tf_op jit(solution)/shard_map/ppermute | solution.py:162
  300.7 79.0 %collective-permute-start.45 = (bf16[256,2048]{1,0:T(8,128)(2,1)}, bf16[256,2048]{1,0:T(8,128)(2,1)S(1)}, u32[]{:S(2)}, u32[]{:S(2)}) collective-permute-start(bf16[256,2048]{1,0:T(8,128)(2,1)} %collective-permute-done.44), channel_id=1, source_target_pairs={{0,1},{1,0},{2,3},{3,2},{4,5},{5,4},{6,7},{7,6},{8,9},{9,8},{10,11... | collective-permute-start | bytes 3145736 | tf_op jit(solution)/shard_map/ppermute | solution.py:162
  818.4 143.7 %collective-permute-start.62 = (bf16[4,256,256]{2,1,0:T(8,128)(2,1)}, bf16[4,256,256]{2,1,0:T(8,128)(2,1)}, u32[]{:S(2)}, u32[]{:S(2)}) collective-permute-start(bf16[4,256,256]{2,1,0:T(8,128)(2,1)} %constant_dynamic-slice_fusion.10), channel_id=1, source_target_pairs={{0,1},{1,0},{2,3},{3,2},{4,5},{5,4},{6,7},{7,6},{8,9},{9,8},{10,11... | collective-permute-start | bytes 1572872 | tf_op jit(solution)/shard_map/ppermute | solution.py:162
  856.3 133.1 %collective-permute-start.79 = (bf16[256,2048]{1,0:T(8,128)(2,1)}, bf16[256,2048]{1,0:T(8,128)(2,1)}, u32[]{:S(2)}, u32[]{:S(2)}) collective-permute-start(bf16[256,2048]{1,0:T(8,128)(2,1)} %slice.323), channel_id=1, source_target_pairs={{0,1},{1,0},{2,3},{3,2},{4,5},{5,4},{6,7},{7,6},{8,9},{9,8},{10,11... | collective-permute-start | bytes 3145736 | tf_op jit(solution)/shard_map/ppermute | solution.py:162
  877.9 79.7 %collective-permute-start.82 = (bf16[256,2048]{1,0:T(8,128)(2,1)}, bf16[256,2048]{1,0:T(8,128)(2,1)}, u32[]{:S(2)}, u32[]{:S(2)}) collective-permute-start(bf16[256,2048]{1,0:T(8,128)(2,1)} %slice.325), channel_id=1, source_target_pairs={{0,1},{1,0},{2,3},{3,2},{4,5},{5,4},{6,7},{7,6},{8,9},{9,8},{10,11... | collective-permute-start | bytes 3145736 | tf_op jit(solution)/shard_map/ppermute | solution.py:162
  915.9 64.4 %collective-permute-start.117 = (bf16[512,1024]{1,0:T(8,128)(2,1)}, bf16[512,1024]{1,0:T(8,128)(2,1)}, u32[]{:S(2)}, u32[]{:S(2)}) collective-permute-start(bf16[512,1024]{1,0:T(8,128)(2,1)} %get-tuple-element.68), channel_id=1, source_target_pairs={{0,2},{1,3},{2,0},{3,1},{4,6},{5,7},{6,4},{7,5},{8,10},{9,11},{10,... | collective-permute-start | bytes 3145736 | tf_op jit(solution)/shard_map/ppermute | solution.py:162
  979.6 116.5 %collective-permute-start.104 = (f32[1024]{0:T(1024)S(1)}, f32[1024]{0:T(1024)S(1)}, u32[]{:S(2)}, u32[]{:S(2)}) collective-permute-start(f32[1024]{0:T(1024)S(1)} %slice.338), channel_id=1, source_target_pairs={{0,2},{1,3},{2,0},{3,1},{4,6},{5,7},{6,4},{7,5},{8,10},{9,11},{10,... | collective-permute-start | bytes 12296 | tf_op jit(solution)/shard_map/ppermute | solution.py:162
  989.6 48.6 %collective-permute-start.125 = (bf16[1024,512]{1,0:T(8,128)(2,1)}, bf16[1024,512]{1,0:T(8,128)(2,1)}, u32[]{:S(2)}, u32[]{:S(2)}) collective-permute-start(bf16[1024,512]{1,0:T(8,128)(2,1)} %add_convert_fusion.2), channel_id=1, source_target_pairs={{0,8},{8,16},{16,24},{24,0},{1,9},{9,17},{17,25},{25,1},{2,10},{10... | collective-permute-start | bytes 3145736 | tf_op jit(solution)/shard_map/ppermute | solution.py:165
  1006.6 90.9 %collective-permute-start.115 = (bf16[512,1024]{1,0:T(8,128)(2,1)}, bf16[512,1024]{1,0:T(8,128)(2,1)}, u32[]{:S(2)}, u32[]{:S(2)}) collective-permute-start(bf16[512,1024]{1,0:T(8,128)(2,1)} %get-tuple-element.70), channel_id=1, source_target_pairs={{0,2},{1,3},{2,0},{3,1},{4,6},{5,7},{6,4},{7,5},{8,10},{9,11},{10,... | collective-permute-start | bytes 3145736 | tf_op jit(solution)/shard_map/ppermute | solution.py:162
  1021.9 107.2 %collective-permute-start.122 = (bf16[1024,512]{1,0:T(8,128)(2,1)}, bf16[1024,512]{1,0:T(8,128)(2,1)}, u32[]{:S(2)}, u32[]{:S(2)}) collective-permute-start(bf16[1024,512]{1,0:T(8,128)(2,1)} %get-tuple-element.66), channel_id=1, source_target_pairs={{0,2},{1,3},{2,0},{3,1},{4,6},{5,7},{6,4},{7,5},{8,10},{9,11},{10,... | collective-permute-start | bytes 3145736 | tf_op jit(solution)/shard_map/ppermute | solution.py:162
  1029.1 69.8 %collective-permute-start.85 = (bf16[256,2048]{1,0:T(8,128)(2,1)}, bf16[256,2048]{1,0:T(8,128)(2,1)}, u32[]{:S(2)}, u32[]{:S(2)}) collective-permute-start(bf16[256,2048]{1,0:T(8,128)(2,1)} %get-tuple-element.45), channel_id=1, source_target_pairs={{0,2},{1,3},{2,0},{3,1},{4,6},{5,7},{6,4},{7,5},{8,10},{9,11},{10,... | collective-permute-start | bytes 3145736 | tf_op jit(solution)/shard_map/ppermute | solution.py:162
  1038.3 57.5 %collective-permute-start.101 = (f32[6,512]{1,0:T(8,128)S(1)}, f32[6,512]{1,0:T(8,128)S(1)}, u32[]{:S(2)}, u32[]{:S(2)}) collective-permute-start(f32[6,512]{1,0:T(8,128)S(1)} %constant_dynamic-slice_fusion.2), channel_id=1, source_target_pairs={{0,2},{1,3},{2,0},{3,1},{4,6},{5,7},{6,4},{7,5},{8,10},{9,11},{10,... | collective-permute-start | bytes 36872 | tf_op jit(solution)/shard_map/ppermute | solution.py:162
  1096.1 50.4 %collective-permute-start.126 = (bf16[1024,512]{1,0:T(8,128)(2,1)}, bf16[1024,512]{1,0:T(8,128)(2,1)}, u32[]{:S(2)}, u32[]{:S(2)}) collective-permute-start(bf16[1024,512]{1,0:T(8,128)(2,1)} %add_convert_fusion.1), channel_id=1, source_target_pairs={{0,8},{8,16},{16,24},{24,0},{1,9},{9,17},{17,25},{25,1},{2,10},{10... | collective-permute-start | bytes 3145736 | tf_op jit(solution)/shard_map/ppermute | solution.py:165
  1098.6 51.5 %collective-permute-start.84 = (bf16[256,2048]{1,0:T(8,128)(2,1)}, bf16[256,2048]{1,0:T(8,128)(2,1)}, u32[]{:S(2)}, u32[]{:S(2)}) collective-permute-start(bf16[256,2048]{1,0:T(8,128)(2,1)} %get-tuple-element.45), channel_id=1, source_target_pairs={{0,1},{1,0},{2,3},{3,2},{4,5},{5,4},{6,7},{7,6},{8,9},{9,8},{10,11... | collective-permute-start | bytes 3145736 | tf_op jit(solution)/shard_map/ppermute | solution.py:162
  1098.8 54.8 %collective-permute-start.86 = (bf16[256,2048]{1,0:T(8,128)(2,1)}, bf16[256,2048]{1,0:T(8,128)(2,1)}, u32[]{:S(2)}, u32[]{:S(2)}) collective-permute-start(bf16[256,2048]{1,0:T(8,128)(2,1)} %collective-permute-done.85), channel_id=1, source_target_pairs={{0,1},{1,0},{2,3},{3,2},{4,5},{5,4},{6,7},{7,6},{8,9},{9,8},{10,11... | collective-permute-start | bytes 3145736 | tf_op jit(solution)/shard_map/ppermute | solution.py:162
  1124.0 118.7 %collective-permute-start.114 = (bf16[512,1024]{1,0:T(8,128)(2,1)}, bf16[512,1024]{1,0:T(8,128)(2,1)}, u32[]{:S(2)}, u32[]{:S(2)}) collective-permute-start(bf16[512,1024]{1,0:T(8,128)(2,1)} %get-tuple-element.67), channel_id=1, source_target_pairs={{0,2},{1,3},{2,0},{3,1},{4,6},{5,7},{6,4},{7,5},{8,10},{9,11},{10,... | collective-permute-start | bytes 3145736 | tf_op jit(solution)/shard_map/ppermute | solution.py:162
  1129.1 113.7 %collective-permute-start.120 = (bf16[512,1024]{1,0:T(8,128)(2,1)}, bf16[512,1024]{1,0:T(8,128)(2,1)}, u32[]{:S(2)}, u32[]{:S(2)}) collective-permute-start(bf16[512,1024]{1,0:T(8,128)(2,1)} %add_convert_fusion.3), channel_id=1, source_target_pairs={{0,8},{8,16},{16,24},{24,0},{1,9},{9,17},{17,25},{25,1},{2,10},{10... | collective-permute-start | bytes 3145736 | tf_op jit(solution)/shard_map/ppermute | solution.py:165
  1181.7 60.4 %collective-permute-start.88 = (bf16[256,2048]{1,0:T(8,128)(2,1)}, bf16[256,2048]{1,0:T(8,128)(2,1)S(1)}, u32[]{:S(2)}, u32[]{:S(2)}) collective-permute-start(bf16[256,2048]{1,0:T(8,128)(2,1)} %slice.331), channel_id=1, source_target_pairs={{0,1},{1,0},{2,3},{3,2},{4,5},{5,4},{6,7},{7,6},{8,9},{9,8},{10,11... | collective-permute-start | bytes 3145736 | tf_op jit(solution)/shard_map/ppermute | solution.py:162
  1270.6 52.7 %collective-permute-start.94 = (bf16[512,768]{1,0:T(8,128)(2,1)S(1)}, bf16[512,768]{1,0:T(8,128)(2,1)S(1)}, u32[]{:S(2)}, u32[]{:S(2)}) collective-permute-start(bf16[512,768]{1,0:T(8,128)(2,1)S(1)} %get-tuple-element.74), channel_id=1, source_target_pairs={{0,4},{1,5},{2,6},{3,7},{4,0},{5,1},{6,2},{7,3},{8,12},{9,13},{10,... | collective-permute-start | bytes 2359304 | tf_op jit(solution)/shard_map/ppermute | solution.py:162
  (225 other events, 5329.0 us)

commit v2 on v1

v2 whole, which is shorter than its diff:
```python
import functools

import jax
import jax.numpy as jnp
from jax import lax
from jax.experimental import pallas as pl
from jax.experimental.pallas import tpu as pltpu
from jax.sharding import PartitionSpec as P

HEAD_DIM = 128
LAYERS = 2
SEQ_LEN = 1024

EPSILON = 1e-06
MASKED = -1e30
SCALE = HEAD_DIM ** (-0.5)

bf16 = jnp.bfloat16
f32 = jnp.float32


def dot(left, right):
    return lax.dot_general(left, right, (((1,), (0,)), ((), ())), preferred_element_type=f32)


def dot_t(left, right):
    return lax.dot_general(left, right, (((1,), (1,)), ((), ())), preferred_element_type=f32)


def dot_g(left, right):
    return lax.dot_general(left, right, (((0,), (0,)), ((), ())), preferred_element_type=f32)


def after(value, *others):
    others = [item for item in others if item is not None]
    if not others:
        return value
    return lax.optimization_barrier((value, others))[0]


def attend_kernel(qkv_ref, docs_row_ref, docs_col_ref, mixed_ref, log_ref):
    step = 256
    span = mixed_ref.shape[1]
    key_docs = docs_col_ref[...]
    for head in range(span // HEAD_DIM):
        low = head * HEAD_DIM
        keys = qkv_ref[:, span + low : span + low + HEAD_DIM]
        values_t = qkv_ref[:, 2 * span + low : 2 * span + low + HEAD_DIM].T
        for start in range(0, SEQ_LEN, step):
            query = qkv_ref[start : start + step, low : low + HEAD_DIM]
            scores = dot_t(keys, query) * SCALE
            allowed = key_docs == docs_row_ref[:, start : start + step]
            scores = jnp.where(allowed, scores, MASKED)
            peak = jnp.max(scores, axis=0, keepdims=True)
            weight = jnp.exp(scores - peak)
            total = jnp.sum(weight, axis=0, keepdims=True)
            mixed_t = dot(values_t, weight.astype(bf16)) * (1.0 / total)
            mixed_ref[start : start + step, low : low + HEAD_DIM] = mixed_t.T.astype(bf16)
            log_ref[head, :, start : start + step] = peak + jnp.log(total)


def attend(qkv, span, docs_row, docs_col):
    groups = qkv.shape[1] // (3 * span)
    heads = span // HEAD_DIM
    return pl.pallas_call(
        attend_kernel,
        grid=(groups,),
        in_specs=[
            pl.BlockSpec((SEQ_LEN, 3 * span), lambda g: (0, g)),
            pl.BlockSpec((1, SEQ_LEN), lambda g: (0, 0)),
            pl.BlockSpec((SEQ_LEN, 1), lambda g: (0, 0)),
        ],
        out_specs=[
            pl.BlockSpec((SEQ_LEN, span), lambda g: (0, g)),
            pl.BlockSpec((heads, 1, SEQ_LEN), lambda g: (g, 0, 0)),
        ],
        out_shape=[
            jax.ShapeDtypeStruct((SEQ_LEN, span * groups), bf16),
            jax.ShapeDtypeStruct((heads * groups, 1, SEQ_LEN), f32),
        ],
        compiler_params=pltpu.CompilerParams(vmem_limit_bytes=48 * 1024 * 1024),
        cost_estimate=pl.CostEstimate(
            flops=groups * heads * 8 * SEQ_LEN * SEQ_LEN * HEAD_DIM,
            bytes_accessed=groups * SEQ_LEN * span * 8,
            transcendentals=groups * heads * SEQ_LEN * SEQ_LEN,
        ),
        name="attend",
    )(qkv, docs_row, docs_col)


def attend_back_kernel(
    qkv_ref, grad_ref, log_ref, docs_row_ref, docs_col_ref, out_ref, probs_ref, dscores_ref
):
    step = 256
    span = grad_ref.shape[1]
    key_docs = docs_col_ref[...]
    for head in range(span // HEAD_DIM):
        low = head * HEAD_DIM
        own = slice(low, low + HEAD_DIM)
        keys = qkv_ref[:, span + low : span + low + HEAD_DIM]
        values = qkv_ref[:, 2 * span + low : 2 * span + low + HEAD_DIM]
        for start in range(0, SEQ_LEN, step):
            at = slice(start, start + step)
            scores = dot_t(keys, qkv_ref[at, own]) * SCALE
            allowed = key_docs == docs_row_ref[:, at]
            probs = jnp.exp(jnp.where(allowed, scores, MASKED) - log_ref[head, :, at])
            dprobs = dot_t(values, grad_ref[at, own])
            along = jnp.sum(dprobs * probs, axis=0, keepdims=True)
            probs_ref[:, at] = probs.astype(bf16)
            dscores_ref[:, at] = (probs * (dprobs - along)).astype(bf16)
        dscores = dscores_ref[...]
        out_ref[:, own] = (dot(keys.T, dscores) * SCALE).T.astype(bf16)
        out_ref[:, span + low : span + low + HEAD_DIM] = (
            dot(dscores, qkv_ref[:, own]) * SCALE
        ).astype(bf16)
        out_ref[:, 2 * span + low : 2 * span + low + HEAD_DIM] = dot(
            probs_ref[...], grad_ref[:, own]
        ).astype(bf16)


def attend_back(qkv, grad, log_total, span, docs_row, docs_col):
    groups = qkv.shape[1] // (3 * span)
    heads = span // HEAD_DIM
    return pl.pallas_call(
        attend_back_kernel,
        grid=(groups,),
        in_specs=[
            pl.BlockSpec((SEQ_LEN, 3 * span), lambda g: (0, g)),
            pl.BlockSpec((SEQ_LEN, span), lambda g: (0, g)),
            pl.BlockSpec((heads, 1, SEQ_LEN), lambda g: (g, 0, 0)),
            pl.BlockSpec((1, SEQ_LEN), lambda g: (0, 0)),
            pl.BlockSpec((SEQ_LEN, 1), lambda g: (0, 0)),
        ],
        out_specs=pl.BlockSpec((SEQ_LEN, 3 * span), lambda g: (0, g)),
        out_shape=jax.ShapeDtypeStruct((SEQ_LEN, 3 * span * groups), bf16),
        scratch_shapes=[pltpu.VMEM((SEQ_LEN, SEQ_LEN), bf16)] * 2,
        compiler_params=pltpu.CompilerParams(vmem_limit_bytes=48 * 1024 * 1024),
        cost_estimate=pl.CostEstimate(
            flops=groups * heads * 20 * SEQ_LEN * SEQ_LEN * HEAD_DIM,
            bytes_accessed=groups * SEQ_LEN * span * 16,
            transcendentals=groups * heads * SEQ_LEN * SEQ_LEN,
        ),
        name="attend_back",
    )(qkv, grad, log_total, docs_row, docs_col)


class Place:
    def __init__(self, mesh, own_rows):
        self.own_rows = own_rows
        self.rows = mesh.shape["row"]
        self.cols = mesh.shape["col"]
        self.a = self.cols // 2
        self.b = self.cols // 4
        self.rest = []
        mask = 1
        while mask < self.b:
            self.rest.append(mask)
            mask *= 2
        self.row = lax.axis_index("row")
        self.col = lax.axis_index("col")
        order = [0]
        for mask in self.rest:
            order = order + [item ^ mask for item in order]
        self.order = order

    def bit(self, mask):
        return (self.col // mask) % 2

    def swap(self, value, mask):
        return lax.ppermute(value, "col", [(i, i ^ mask) for i in range(self.cols)])

    def shift(self, value):
        return lax.ppermute(value, "row", [(i, (i + 1) % self.rows) for i in range(self.rows)])

    def on(self, lane, value, mask):
        if lane is None:
            return self.swap(value, mask)
        return lane.send(lambda item: self.swap(item, mask), value)

    def tokens_send(self, value, mask, lane, inner=1):
        width = value.shape[-1]
        split = value.reshape(-1, 2, inner * self.own_rows, width)
        bit = self.bit(mask)
        mine = lax.dynamic_index_in_dim(split, bit, 1, keepdims=False).reshape(-1, width)
        sent = lax.dynamic_index_in_dim(split, 1 - bit, 1, keepdims=False).reshape(-1, width)
        return (mine, self.on(lane, sent, mask))

    def tokens_merge(self, mine, got, mask, groups=1):
        part = mine.shape[-1] // groups
        return jnp.concatenate(
            [
                self.ordered(
                    mine[:, i * part : (i + 1) * part], got[:, i * part : (i + 1) * part], mask, 1
                )
                for i in range(groups)
            ],
            axis=1,
        )

    def features_send(self, value, mask, lane, groups=1):
        width = value.shape[2] // (2 * groups)
        bit = self.bit(mask)

        def pick(side):
            return jnp.concatenate(
                [
                    lax.dynamic_slice_in_dim(value, (2 * i + side) * width, width, 2)
                    for i in range(groups)
                ],
                axis=2,
            )

        return (pick(bit), self.on(lane, pick(1 - bit), mask))

    def features_merge(self, mine, got, mask, axis):
        value = self.ordered(jnp.expand_dims(mine, axis), jnp.expand_dims(got, axis), mask, axis)
        return value.reshape(-1, *mine.shape[1:])

    def ordered(self, mine, got, mask, axis):
        low = self.bit(mask) == 0
        return jnp.concatenate(
            [jnp.where(low, mine, got), jnp.where(low, got, mine)], axis=axis
        )

    def all_features(self, value, lane_of):
        for mask in self.rest + [self.b, self.a]:
            value = self.ordered(value, self.on(lane_of(mask), value, mask), mask, 1)
        return value


    def blocks(self, value, pieces, axis):
        size = pieces[0].shape[axis] // self.rows
        found = []
        for step in range(self.rows):
            at = ((self.row - 1 - step + 2 * self.rows) % self.rows) * size
            found.append(
                jnp.concatenate(
                    [lax.dynamic_slice_in_dim(item, at, size, axis) for item in pieces], axis=value
                )
            )
        return found

    def parts(self, sums, mask):
        width = sums.shape[1] // 2
        bit = self.bit(mask)
        return (
            lax.dynamic_slice_in_dim(sums, bit * width, width, 1),
            lax.dynamic_slice_in_dim(sums, (1 - bit) * width, width, 1),
        )

    def halve(self, sums, mask, lane):
        mine, sent = self.parts(sums, mask)
        return mine + self.on(lane, sent, mask)

    def row_sum(self, value, lane):
        mask = 1
        while mask < self.rows:
            pairs = [(i, i ^ mask) for i in range(self.rows)]
            value = value + lane.send(lambda item: lax.ppermute(item, "row", pairs), value)
            mask *= 2
        return value


def norm_forward(residual, gain, shift):
    mean = jnp.mean(residual, axis=1, keepdims=True)
    center = residual - mean
    inverse = lax.rsqrt(jnp.mean(center * center, axis=1, keepdims=True) + EPSILON)
    normed = center * inverse
    return (normed * gain + shift, normed, inverse)


def norm_backward(grad, normed, inverse, gain):
    scaled = grad * gain
    mean = jnp.mean(scaled, axis=1, keepdims=True)
    along = jnp.mean(scaled * normed, axis=1, keepdims=True)
    result = inverse * (scaled - mean - normed * along)
    return (result, jnp.sum(grad * normed, axis=0), jnp.sum(grad, axis=0))


def gelu(value):
    return jax.nn.gelu(value, approximate=True)


def gelu_slope(value):
    inner = 0.7978845608028654
    cubic = 0.044715
    square = value * value
    tangent = jnp.tanh(inner * value * (1.0 + cubic * square))
    return 0.5 * (1.0 + tangent) + 0.5 * value * (1.0 - tangent * tangent) * inner * (
        1.0 + 3.0 * cubic * square
    )


class Clock:
    def __init__(self):
        self.last = None

    def hold(self, value, *others):
        return after(value, self.last, *others)

    def run(self, work, *args):
        self.last = work(*self.hold(args))
        return self.last

    def wait(self, *results):
        self.last = (self.last, results)

    def aside(self, work, *args):
        return work(*self.hold(args))


class Lane:
    def __init__(self, clock, width=1):
        self.clock = clock
        self.width = width
        self.done = []

    def send(self, move, value):
        wait = self.done[-self.width] if len(self.done) >= self.width else None
        result = move(after(value, wait))
        self.done.append(result)
        return result


class Weights:
    def __init__(self, place, clock, ring, blocks):
        self.place, self.clock, self.ring = place, clock, ring
        self.entries = blocks
        self.own = {name: [entry[1]] for name, entry in blocks.items()}
        self.other = {name: [] for name in blocks}
        self.wholes = {}

    def exchange(self, name):
        whole, block, far, lane, axis, corner, spans = self.entries[name]
        step = len(self.other[name])
        self.other[name].append(
            lane.send(lambda value: self.place.swap(value, far), self.own[name][step])
        )

    def exchange_all(self, name):
        whole, block, far, lane, axis, corner, spans = self.entries[name]
        blocks = jnp.concatenate(self.own[name], axis=0)
        got = lane.send(lambda value: self.place.swap(value, far), blocks)
        self.other[name] = jnp.split(got, self.place.rows, axis=0)

    def step(self, name):
        self.own[name].append(self.ring.send(self.place.shift, self.own[name][-1]))

    def arrived(self, step, *names):
        self.clock.wait([self.own[name][step] for name in names])

    def put(self, name, step, side):
        place = self.place
        whole, block, far, lane, axis, corner, spans = self.entries[name]
        items = self.other if side else self.own
        at = ((place.row - step + place.rows) % place.rows) * spans[axis] + corner[axis]
        start = [0, 0]
        start[axis] = at
        start[1 - axis] = side * spans[1 - axis] + corner[1 - axis]
        if whole not in self.wholes:
            shape = [0, 0]
            shape[axis], shape[1 - axis] = place.rows * spans[axis], 2 * spans[1 - axis]
            self.wholes[whole] = jnp.full(shape, len(self.wholes), block.dtype)
        self.wholes[whole] = self.clock.run(
            lambda total, item: lax.dynamic_update_slice(total, item, start),
            self.wholes[whole],
            items[name][step],
        )


def entry(name, block, far, lane, axis):
    return {name: (name, block, far, lane, axis, (0, 0), block.shape)}


def halves(name, block, far, lane, axis):
    half = block.shape[0] // 2
    return {
        name + "0": (name, block[:half], far, lane, axis, (0, 0), block.shape),
        name + "1": (name, block[half:], far, lane, axis, (half, 0), block.shape),
    }


def join(pair):
    return jnp.concatenate(pair, axis=0)


def columns(pair, split):
    return (join([item[:, :split] for item in pair]), join([item[:, split:] for item in pair]))


class Exchange:
    def __init__(self, place, clock, lane, far):
        self.place, self.clock, self.lane, self.bit = place, clock, lane, far

    def far(self, value):
        return self.lane.send(lambda item: self.place.swap(item, self.bit), value)

    def near(self, value):
        for mask in self.place.rest:
            value = self.clock.run(
                lambda own, got: jnp.concatenate([own, got], axis=0),
                value,
                self.place.swap(self.clock.hold(value), mask),
            )
        return value

    def halved(self, terms):
        for mask in self.place.rest[::-1]:
            half = terms.shape[0] // 2
            got = self.place.swap(self.clock.hold(terms[half:]), mask)
            if mask == self.place.rest[0]:
                return (terms[:half], got)
            terms = self.clock.run(
                lambda own, more: (own.astype(f32) + more.astype(f32)).astype(bf16),
                terms[:half],
                got,
            )
        return (terms, jnp.zeros_like(terms))

    def sum_far(self, terms):
        kept, got = self.halved(terms)
        part = self.clock.run(
            lambda own, more: (own.astype(f32) + more.astype(f32)).astype(bf16), kept, got
        )
        return self.far(part)


def plus(*items):
    total = items[0].astype(f32)
    for item in items[1:]:
        total = total + item.astype(f32)
    return total


def local(
    mesh,
    tokens,
    cotangent,
    segments,
    query_weight,
    query_bias,
    key_weight,
    value_weight,
    value_bias,
    output_weight,
    output_bias,
    first_gain,
    first_shift,
    up_weight,
    up_bias,
    down_weight,
    down_bias,
    second_gain,
    second_shift,
):
    place = Place(mesh, tokens.shape[0] // mesh.shape["col"])
    clock = Clock()
    run = clock.run
    rows = place.rows
    steps = range(1, rows)
    span = query_weight.shape[1]
    hidden_span = up_weight.shape[1]
    own_rows = place.own_rows
    lane_a, lane_b, row_lane = Lane(clock), Lane(clock), Lane(clock)
    across_b = Exchange(place, clock, lane_b, place.b)
    across_a = Exchange(place, clock, lane_a, place.a)

    def on_lane(mask):
        return lane_a if mask == place.a else lane_b if mask == place.b else None

    def project(rows_in, weight, bias):
        return (dot(rows_in, weight) + bias).astype(bf16)

    def up_product(rows_in, weight, bias):
        hidden = dot(rows_in, weight) + bias
        return (hidden, gelu(hidden).astype(bf16))

    def product(rows_in, weight):
        return dot(rows_in, weight).astype(bf16)

    def norm(residual, kept, got, sent, bias, gain, shift):
        result, normed, inverse = norm_forward(plus(residual, kept, got, sent) + bias, gain, shift)
        return (result, result.astype(bf16), normed, inverse)

    w_all = jnp.concatenate([query_weight, key_weight, value_weight], axis=1)
    ring = Weights(
        place,
        clock,
        row_lane,
        {
            **entry("qkv", w_all, place.a, lane_a, 0),
            **entry("out", output_weight, place.a, lane_a, 1),
            **entry("up", up_weight, place.b, lane_b, 0),
            **halves("down", down_weight, place.b, lane_b, 1),
        },
    )

    def steps_of(*names):
        for name in names:
            ring.step(name)

    def exchanges(*names):
        for name in names:
            ring.exchange(name)

    def puts(step, side, *names):
        for name in names:
            ring.put(name, step, side)

    def merge(mask, groups=1):
        return lambda mine, got: place.tokens_merge(mine, got, mask, groups)

    def blocks(*pieces):
        return place.blocks(0, pieces, 1)

    exchanges("qkv")
    steps_of("qkv")
    value = tokens
    for mask in place.rest:
        value = run(merge(mask), *place.tokens_send(value, mask, None))
    value = place.tokens_send(value, place.b, lane_b)
    vectors = jnp.stack(
        [output_bias, first_gain, first_shift, down_bias, second_gain, second_shift]
    )
    for mask in place.rest:
        vectors = place.ordered(vectors, place.swap(vectors, mask), mask, 1)
    got, up_bias_other = lane_b.send(
        lambda items: tuple(place.swap(item, place.b) for item in items), (vectors, up_bias)
    )
    vectors = place.ordered(vectors, got, place.b, 1)
    b_up = jnp.concatenate([up_bias, up_bias_other])
    exchanges("up")
    puts(0, 0, "qkv", "out")
    masks = place.order + [item ^ place.b for item in place.order]
    docs = jnp.concatenate(
        [
            lax.dynamic_slice_in_dim(
                segments, jnp.bitwise_xor(place.col, mask) * own_rows, own_rows, 0
            )
            for mask in masks
        ]
    )
    docs = (docs[None, :], docs[:, None])
    value = run(merge(place.b), *value)
    value = place.tokens_send(value, place.a, lane_a)
    ring.arrived(1, "qkv")
    steps_of("qkv")
    puts(0, 1, "qkv")
    pair = jnp.concatenate([query_bias, jnp.zeros_like(query_bias), value_bias])
    pair_other, got = lane_a.send(
        lambda items: tuple(place.swap(item, place.a) for item in items), (pair, vectors)
    )
    b_qkv = jnp.concatenate([pair, pair_other])
    vectors = place.ordered(vectors, got, place.a, 1)
    b_out, gain1, shift1, b_down, gain2, shift2 = (vectors[i] for i in range(6))
    puts(1, 0, "qkv")
    for step in range(1, rows):
        exchanges("qkv")
        if step < rows - 2:
            steps_of("qkv")
    state_low = run(merge(place.a), *value)
    state = state_low.astype(f32)
    far = across_b.far(state_low)
    exchanges("down0", "down1")
    own = across_b.near(state_low)
    clock.wait(b_qkv, b_up, vectors)
    for step in range(2, rows):
        ring.arrived(step, "qkv")
        if step == rows - 1:
            steps_of("out")
        puts(step, 0, "qkv")
        puts(step - 1, 1, "qkv")
    for step in range(1, rows):
        ring.arrived(step, "out")
        steps_of("out" if step < rows - 1 else "up")
        puts(step, 0, "out")
    ring.exchange_all("out")
    other = across_b.near(far)
    puts(0, 0, "up")
    puts(0, 1, "up")
    puts(rows - 1, 1, "qkv")
    w_qkv = ring.wholes["qkv"]
    clock.wait(ring.other["down0"][0])
    qkv_own = run(project, own, w_qkv, b_qkv)
    ring.arrived(1, "up")
    steps_of("up")
    clock.wait(ring.other["down1"][0])
    exchanges("up")
    qkv_other = run(project, other, w_qkv, b_qkv)
    qkv = run(lambda *items: join(items), qkv_own, qkv_other)
    puts(1, 0, "up")
    ring.arrived(2, "up")
    steps_of("up" if rows > 3 else "down0")
    mixed, log_total = run(lambda item: attend(item, span, *docs), qkv)
    for step in range(rows):
        puts(step, 1, "out")
    w_out = ring.wholes["out"]
    half = mixed.shape[0] // 2
    terms = run(product, mixed[half:], w_out)
    sent = across_b.sum_far(terms)
    puts(1, 1, "up")
    terms = run(product, mixed[:half], w_out)
    sums = across_b.halved(terms)
    exchanges("up")
    puts(2, 0, "up")
    for step in range(3, rows):
        ring.arrived(step, "up")
        steps_of("up" if step < rows - 1 else "down0")
        exchanges("up")
        puts(step, 0, "up")
    puts(0, 0, "down0", "down1")
    puts(0, 1, "down0", "down1")
    far_half = ring.entries["down1"]
    corner = (far_half[5][0] + far_half[6][0], 0)
    ring.entries["more"] = (*far_half[:5], corner, far_half[6])
    ring.own["more"] = ring.other["down1"]
    queue = ["down0"] * (rows - 2) + ["down1", "more"] * (rows - 1)
    first, first_low, normed1, inverse1 = run(norm, state, *sums, sent, b_out, gain1, shift1)
    far = across_a.far(first_low)
    ring.arrived(1, "down0")
    steps_of(queue.pop(0))
    exchanges("down0")
    own_first = across_a.near(first_low)
    puts(2, 1, "up")
    puts(1, 0, "down0")
    ring.arrived(2, "down0")
    steps_of(queue.pop(0))
    exchanges("down0")
    puts(2, 0, "down0")
    other_first = across_a.near(far)
    for step in range(3, rows):
        ring.arrived(step, "down0")
        steps_of(queue.pop(0))
        exchanges("down0")
        puts(step, 1, "up")
        puts(step, 0, "down0")
    w_up = ring.wholes["up"]
    ring.arrived(1, "down1")
    steps_of(queue.pop(0))
    hidden_own, active_own = run(up_product, own_first, w_up, b_up)
    ring.arrived(1, "more")
    steps_of(queue.pop(0))
    hidden_other, active_other = run(up_product, other_first, w_up, b_up)
    ring.arrived(2, "down1")
    steps_of(queue.pop(0))
    puts(1, 1, "down0")
    puts(1, 0, "down1", "more")
    token_pieces = run(blocks, own, other)
    ring.arrived(2, "more")
    if queue:
        steps_of(queue.pop(0))
    puts(2, 1, "down0")
    puts(2, 0, "down1", "more")
    for step in range(3, rows):
        ring.arrived(step, "down1")
        if queue:
            steps_of(queue.pop(0))
        puts(step, 1, "down0")
        puts(step, 0, "down1")
        ring.arrived(step, "more")
        if queue:
            steps_of(queue.pop(0))
        if step < rows - 1:
            puts(step, 0, "more")
    first_pieces = run(blocks, own_first, other_first)
    active_sides = run(lambda *items: columns(items, hidden_span), active_own, active_other)
    if rows > 3:
        puts(rows - 1, 0, "more")
    w_down = ring.wholes["down"]
    terms_other = run(product, active_other, w_down)
    sent = across_a.sum_far(terms_other)
    terms_own = run(product, active_own, w_down)
    sums = across_a.halved(terms_own)
    kept_attention = [(token_pieces, qkv, mixed, log_total, normed1, inverse1)]
    state, state_low, normed2, inverse2 = run(
        norm, first, *sums, sent, b_down, gain2, shift2
    )
    kept_feed = [(first_pieces, (hidden_own, hidden_other), active_sides, normed2, inverse2)]

    grad = cotangent
    for mask in place.rest:
        grad = clock.aside(merge(mask), *place.tokens_send(grad, mask, None))
    for depth in range(1, LAYERS):
        far = across_b.far(state_low)
        own = across_b.near(state_low)
        qkv_own = run(project, own, w_qkv, b_qkv)
        other = across_b.near(far)
        qkv_other = run(project, other, w_qkv, b_qkv)
        qkv = run(lambda *items: join(items), qkv_own, qkv_other)
        if depth == 1:
            grad = place.tokens_send(grad, place.a, lane_a, 2)
        mixed, log_total = run(lambda item: attend(item, span, *docs), qkv)
        terms = run(product, mixed[half:], w_out)
        sent = across_b.sum_far(terms)
        terms = run(product, mixed[:half], w_out)
        sums = across_b.halved(terms)
        token_pieces = run(blocks, own, other)
        if depth == 1:
            grad = run(merge(place.a), *grad)
        first, first_low, normed1, inverse1 = run(norm, state, *sums, sent, b_out, gain1, shift1)
        kept_attention.append((token_pieces, qkv, mixed, log_total, normed1, inverse1))
        far = across_a.far(first_low)
        own = across_a.near(first_low)
        if depth == 1:
            grad = place.tokens_send(grad, place.b, lane_b)
        hidden_own, active_own = run(up_product, own, w_up, b_up)
        terms_own = run(product, active_own, w_down)
        own_sums = across_a.halved(terms_own)
        other = across_a.near(far)
        hidden_other, active_other = run(up_product, other, w_up, b_up)
        terms_other = run(product, active_other, w_down)
        sent = across_a.sum_far(terms_other)
        if depth == 1:
            grad = run(merge(place.b, 2), *grad)
        first_pieces = run(blocks, own, other)
        active_sides = run(lambda *items: columns(items, hidden_span), active_own, active_other)
        state, state_low, normed2, inverse2 = run(
            norm, first, *own_sums, sent, b_down, gain2, shift2
        )
        kept_feed.append(
            (first_pieces, (hidden_own, hidden_other), active_sides, normed2, inverse2)
        )
    output = state_low[None]

    def gelu_back(rows_in, weight, hidden):
        return (dot_t(rows_in, weight) * gelu_slope(hidden)).astype(bf16)

    def product_t(rows_in, weight):
        return dot_t(rows_in, weight).astype(bf16)

    def norm_back(grads, normed, inverse, gain):
        result, gain_grad, shift_grad = norm_backward(plus(*grads), normed, inverse, gain)
        low = result.astype(bf16)
        return (result, low, jnp.stack([jnp.sum(low, axis=0, dtype=f32), gain_grad, shift_grad]))

    def sum_rows(*items):
        return jnp.concatenate([jnp.sum(item, axis=0, dtype=f32) for item in items])

    class Share:
        def __init__(self, name, left, right, lane, far):
            self.name, self.left, self.right = name, left, right
            self.lane, self.far = lane, far
            self.before = held.get(name)
            self.got = []
            self.total = None
            self.step = 0

        def keep(self):
            left, right = clock.hold((self.left, self.right))
            clock.last = [
                [dot_g(left[side][step], right[side][step]) for step in range(rows)]
                for side in (0, 1)
            ]
            held[self.name] = clock.last

        def other(self):
            self.sent = []
            for step in range(rows):
                left, right = clock.hold((self.left[1][step], self.right[1][step]))
                clock.last = (dot_g(left, right) + self.before[1][step]).astype(bf16)
                self.sent.append(clock.last)

        def send(self, count=1):
            for step in range(count):
                self.got.append(
                    self.lane.send(
                        lambda item: place.swap(item, self.far), self.sent[len(self.got)]
                    )
                )

        def send_all(self):
            got = self.lane.send(
                lambda item: place.swap(item, self.far), jnp.concatenate(self.sent, axis=0)
            )
            self.got = jnp.split(got, rows, axis=0)

        def advance(self):
            step = self.step
            more = [self.got[step]] + ([] if self.total is None else [self.total])
            left, right, before, more = clock.hold(
                (self.left[0][step], self.right[0][step], self.before[0][step], more)
            )
            value = dot_g(left, right) + before
            for item in more:
                value = value + item.astype(f32)
            self.step += 1
            if step < rows - 1:
                value = value.astype(bf16)
            clock.last = self.result = value
            if step < rows - 1:
                self.total = row_lane.send(place.shift, value)

    held = {}
    norm_sums, qkv_sums, hidden_sums = [], [], []
    grads = (grad,)
    for depth in reversed(range(LAYERS)):
        last = depth == 0
        token_pieces, qkv, mixed, log_total, normed1, inverse1 = kept_attention[depth]
        first_pieces, hiddens, (active_own, active_other), normed2, inverse2 = kept_feed[depth]
        dr2, dsecond, sums2 = run(norm_back, grads, normed2, inverse2, gain2)
        far = across_a.far(dsecond)
        second_own = across_a.near(dsecond)
        if not last:
            output = place.features_send(output, place.b, lane_b, 2)
        dhid_own = run(gelu_back, second_own, w_down, hiddens[0])
        terms_own = run(product_t, dhid_own, w_up)
        own_sums = across_a.halved(terms_own)
        second_other = across_a.near(far)

        def down_share():
            pieces = run(blocks, second_own, second_other)
            return Share(
                "down",
                ([active_own] * rows, [active_other] * rows),
                (pieces, pieces),
                lane_b,
                place.b,
            )

        if last:
            down = down_share()
            down.other()
            down.send(3)
        else:
            output = run(lambda *items: place.features_merge(*items, place.b, 1), *output)
        dhid_other = run(gelu_back, second_other, w_down, hiddens[1])
        if last:
            clock.wait(down.got[0])
        terms_other = run(product_t, dhid_other, w_up)
        sent = across_a.sum_far(terms_other)
        if last:
            down.advance()
        dhid_left, dhid_right = run(lambda *items: columns(items, hidden_span), dhid_own, dhid_other)
        up = Share(
            "up",
            (first_pieces, first_pieces),
            ([dhid_left] * rows, [dhid_right] * rows),
            lane_b,
            place.b,
        )
        if last:
            up.other()
            hidden_total = hidden_sums[0] + clock.aside(sum_rows, dhid_left, dhid_right)
        else:
            down = down_share()
            down.keep()
        dr1, dbranch, sums1 = run(norm_back, (dr2, *own_sums, sent), normed1, inverse1, gain1)
        norm_sums.append(jnp.concatenate([sums1, sums2], axis=0))
        far = across_b.far(dbranch)
        branch_own = across_b.near(dbranch)
        dmixed_own = run(product_t, branch_own, w_out)
        if last:
            token_sums = place.halve(sum(norm_sums), place.a, lane_a)
            down.advance()
            down.send(rows - 3)
            mine, away = place.parts(token_sums, place.b)
            more = lane_b.send(
                lambda items: tuple(place.swap(item, place.b) for item in items),
                (away, hidden_total[hidden_span:]),
            )
            token_sums = mine + more[0]
            hidden_total = hidden_total[:hidden_span] + more[1]
            for mask in place.rest[::-1]:
                token_sums = place.halve(token_sums, mask, None)
        else:
            output = place.features_send(output, place.a, lane_a)
            up.keep()
            hidden_sums.append(clock.aside(sum_rows, dhid_left, dhid_right))
        branch_other = across_b.near(far)
        dmixed_other = run(product_t, branch_other, w_out)
        dmixed = run(lambda *items: join(items), dmixed_own, dmixed_other)
        pieces = run(blocks, branch_own, branch_other)
        out = Share(
            "out",
            ([mixed[:, :span]] * rows, [mixed[:, span:]] * rows),
            (pieces, pieces),
            lane_a,
            place.a,
        )
        if last:
            out.other()
            out.send_all()
            down.advance()
        else:
            output = run(lambda *items: place.features_merge(*items, place.a, 0), *output)
        dqkv = run(lambda *items: attend_back(*items, log_total, span, *docs), qkv, dmixed)
        qkv_sums.append(clock.aside(sum_rows, dqkv))
        if last:
            up.send(2)
            while down.step < rows:
                down.advance()
            up.advance()
        terms_other = run(product_t, dqkv[half:], w_qkv)
        sent = across_b.sum_far(terms_other)
        if not last:
            for mask in place.rest[::-1]:
                output = run(
                    lambda *items: place.features_merge(*items, mask, 1),
                    *place.features_send(output, mask, None),
                )
        both = Share(
            "qkv",
            (token_pieces, token_pieces),
            ([dqkv[:, : 3 * span]] * rows, [dqkv[:, 3 * span :]] * rows),
            lane_a,
            place.a,
        )
        if last:
            both.other()
            qkv_total = sum(qkv_sums)
            qkv_total = qkv_total[: 3 * span] + lane_a.send(
                lambda item: place.swap(item, place.a), qkv_total[3 * span :]
            )
            both.send(2)
            up.advance()
        terms_own = run(product_t, dqkv[:half], w_qkv)
        own_sums = across_b.halved(terms_own)
        if not last:
            out.keep()
            both.keep()
        grads = (dr1, *own_sums, sent)
    for step in range(rows):
        out.advance()
    grad = run(lambda *items: plus(*items).astype(bf16)[None], *grads)
    grad = place.features_send(grad, place.a, lane_a)
    up.send()
    both.send(rows - 2)
    both.advance()
    grad = run(lambda *items: place.features_merge(*items, place.a, 0), *grad)
    grad = place.features_send(grad, place.b, lane_b)
    up.send(rows - len(up.got))
    up.advance()
    sums = place.row_sum(
        jnp.concatenate([token_sums.reshape(-1), qkv_total, hidden_total]), row_lane
    )
    both.advance()
    grad = run(lambda *items: place.features_merge(*items, place.b, 1), *grad)
    for mask in place.rest[::-1]:
        grad = run(
            lambda *items: place.features_merge(*items, mask, 1),
            *place.features_send(grad, mask, None),
        )
    grad_tokens = grad.reshape(-1, span).astype(f32)
    output = output.reshape(-1, span)
    while up.step < rows:
        up.advance()
    while both.step < rows:
        both.advance()

    token_sums = sums[: 6 * span].reshape(6, span)
    qkv_sums = sums[6 * span : 9 * span]
    hidden_sums = sums[9 * span :]
    qkv = both.result
    return (
        output,
        grad_tokens,
        qkv[:, :span],
        qkv_sums[:span],
        qkv[:, span : 2 * span],
        qkv[:, 2 * span :],
        qkv_sums[2 * span :],
        out.result,
        token_sums[0],
        token_sums[1],
        token_sums[2],
        up.result,
        hidden_sums,
        down.result,
        token_sums[3],
        token_sums[4],
        token_sums[5],
    )


def solution(mesh):
    both, col, back = P("row", "col"), P("col"), P("col", "row")
    return jax.shard_map(
        functools.partial(local, mesh),
        mesh=mesh,
        in_specs=(
            both, both, P("row"), both, col, both, both, col, back, col, col, col, both, col, back,
            col, col, col,
        ),
        out_specs=(
            both, both, both, col, both, both, col, back, col, col, col, both, col, back, col, col,
            col,
        ),
        check_vma=False,
    )
```

time: 1360 us -> 1220 us (0.90)
  waiting for transfers between devices: 739 us -> 540 us
  local copies, waits for them, and re-layouts: 87.6 us -> 129 us
  starting transfers between devices: 99.4 us -> 71.7 us
  matrix products: 289 us -> 311 us
    ppermute x102 -> x97, waiting for transfers between devices: 598 us -> 339 us  [swap(): return lax.ppermute(value, 'col', [(i, i ^ mask) for i in range(self.cols)])]
    ppermute x24 -> x30, waiting for transfers between devices: 140 us -> 189 us  [shift(): lax.ppermute(value, 'row', [(i, (i + 1) % self.rows) for i in range(self....]
    unnamed x260 -> x425, local copies, waits for them, and re-layouts: 11.1 us -> 35 us
    dynamic_update_slice x32 -> x40, local copies, waits for them, and re-layouts: 24.2 us -> 45.7 us  [put(): lax.dynamic_update_slice(total, item, start)]
    slice x26 -> x35, local copies, waits for them, and re-layouts: 31.3 us -> 10.5 us  [the longest x16 5.87 us: halved(): got = self.place.swap(self.clock.hold(terms[half:]), mask)]
    concatenate x5 -> x39, other arithmetic: 0.43 us -> 19.7 us  [the longest x32 17.2 us: blocks(): jnp.concatenate([lax.dynamic_slice_in_dim(item, at, size, axis) for item...]
    ppermute x102 -> x97, starting transfers between devices: 82.6 us -> 63.7 us  [swap(): return lax.ppermute(value, 'col', [(i, i ^ mask) for i in range(self.cols)])]
    dot_general x8 -> x64, matrix products: 102 us -> 116 us  [dot_g(): lax.dot_general(left, right, (((0,), (0,)), ((), ())), preferred_element_...]
  transfers between devices with their start and end apart: 128 -> 129, of which waited for: 59 -> 75; matrix products, arithmetic and copies ran while one was open for 27% -> 34% of each run, Pallas kernels for 1% -> 2%
where the time goes in v2:
time: 1220 us; the launch traced here: 1210 us
  waiting for transfers between devices  540 us (44%)
  matrix products  311 us (25%)
  local copies, waits for them, and re-layouts  129 us (11%)
  other arithmetic  95.2 us (8%)
  starting transfers between devices  71.7 us (6%)
  Pallas kernels  54.1 us (4%)
    ppermute x97, waiting for transfers between devices, swap(): return lax.ppermute(value, 'col', [(i, i ^ mask) for i in range(self.cols)])  339 us
    ppermute x30, waiting for transfers between devices, shift(): lax.ppermute(value, 'row', [(i, (i + 1) % self.rows) for i in range(self....  189 us
    dot_general x64, matrix products, dot_g(): lax.dot_general(left, right, (((0,), (0,)), ((), ())), preferred_element_...  116 us
    dot_general x16, matrix products, dot_t(): lax.dot_general(left, right, (((1,), (1,)), ((), ())), preferred_element_...  101 us
    dot_general x16, matrix products, dot(): lax.dot_general(left, right, (((1,), (0,)), ((), ())), preferred_element_...  94.3 us
    ppermute x97, starting transfers between devices, swap(): return lax.ppermute(value, 'col', [(i, i ^ mask) for i in range(self.cols)])  63.7 us
    dynamic_update_slice x40, local copies, waits for them, and re-layouts, put(): lax.dynamic_update_slice(total, item, start)  45.7 us
    unnamed x425, local copies, waits for them, and re-layouts  35 us
  transfers between devices with their start and end apart: 129, of which 75 were waited for; matrix products, arithmetic and copies ran while one was open for 34% of the time, Pallas kernels for 2%

profile of v2, /device:TPU:0, one launch (start us, length us, event | category | flops | bytes accessed | tf_op | source)
XLA Modules:
  0.0 1205.2 jit_solution(16492693659979002302)
XLA Ops:
  59.0 13.0 %collective-permute-done.13 = bf16[512,768]{1,0:T(8,128)(2,1)} collective-permute-done((bf16[512,768]{1,0:T(8,128)(2,1)S(1)}, bf16[512,768]{1,0:T(8,128)(2,1)}, u32[]{:S(2)}, u32[]{:S(2)}) %collective-permute-start.13) | collective-permute-done | bytes 786464 | tf_op jit(solution)/shard_map/ppermute | solution.py:173
  106.4 12.1 %collective-permute-done.22 = bf16[512,512]{1,0:T(8,128)(2,1)} collective-permute-done((bf16[512,512]{1,0:T(8,128)(2,1)}, bf16[512,512]{1,0:T(8,128)(2,1)}, u32[]{:S(2)}, u32[]{:S(2)}) %collective-permute-start.22) | collective-permute-done | bytes 524320 | tf_op jit(solution)/shard_map/ppermute | solution.py:170
  150.1 12.8 %attend.2 = (bf16[1024,512]{1,0:T(8,128)(2,1)S(1)}, f32[4,1,1024]{2,1,0:T(1,128)S(1)}) custom-call(bf16[1024,1536]{1,0:T(8,128)(2,1)S(1)} %constant_dynamic-update-slice_fusion.8.qkv_ref, s32[1,1024]{1,0:T(1,128)S(1)} %bitcast.315, s32[1024,1]{1,0:T(8,128)S(1)} %copy.40.docs_col_ref), custom_call_target="tpu_custom_call" | custom-call | flops 4294967296 | bytes 4194304 | tf_op jit(solution)/shard_map/attend/pallas_call | solution.py:65
  169.6 22.7 %collective-permute-done.27 = bf16[512,1024]{1,0:T(8,128)(2,1)S(1)} collective-permute-done((bf16[512,1024]{1,0:T(8,128)(2,1)}, bf16[512,1024]{1,0:T(8,128)(2,1)S(1)}, u32[]{:S(2)}, u32[]{:S(2)}) %collective-permute-start.27) | collective-permute-done | bytes 1048608 | tf_op jit(solution)/shard_map/ppermute | solution.py:170
  228.9 12.8 %collective-permute-done.39 = bf16[512,512]{1,0:T(8,128)(2,1)S(1)} collective-permute-done((bf16[512,512]{1,0:T(8,128)(2,1)S(1)}, bf16[512,512]{1,0:T(8,128)(2,1)S(1)}, u32[]{:S(2)}, u32[]{:S(2)}) %collective-permute-start.39) | collective-permute-done | bytes 524320 | tf_op jit(solution)/shard_map/ppermute | solution.py:173
  256.5 12.7 %collective-permute-done.42 = bf16[512,512]{1,0:T(8,128)(2,1)} collective-permute-done((bf16[512,512]{1,0:T(8,128)(2,1)S(1)}, bf16[512,512]{1,0:T(8,128)(2,1)}, u32[]{:S(2)}, u32[]{:S(2)}) %collective-permute-start.42) | collective-permute-done | bytes 524320 | tf_op jit(solution)/shard_map/ppermute | solution.py:173
  276.7 10.6 fusion.7
  287.3 10.6 fusion.15
  363.4 15.1 %collective-permute-done.51 = bf16[256,2048]{1,0:T(8,128)(2,1)S(1)} collective-permute-done((bf16[256,2048]{1,0:T(8,128)(2,1)S(1)}, bf16[256,2048]{1,0:T(8,128)(2,1)S(1)}, u32[]{:S(2)}, u32[]{:S(2)}) %collective-permute-start.51) | collective-permute-done | bytes 1048608 | tf_op jit(solution)/shard_map/ppermute | solution.py:170
  387.9 19.2 %collective-permute-done.53 = bf16[256,2048]{1,0:T(8,128)(2,1)S(1)} collective-permute-done((bf16[256,2048]{1,0:T(8,128)(2,1)S(1)}, bf16[256,2048]{1,0:T(8,128)(2,1)S(1)}, u32[]{:S(2)}, u32[]{:S(2)}) %collective-permute-start.53) | collective-permute-done | bytes 1048608 | tf_op jit(solution)/shard_map/ppermute | solution.py:170
  413.6 12.8 %attend.3 = (bf16[1024,512]{1,0:T(8,128)(2,1)S(1)}, f32[4,1,1024]{2,1,0:T(1,128)S(1)}) custom-call(bf16[1024,1536]{1,0:T(8,128)(2,1)S(1)} %constant_dynamic-update-slice_fusion.18.qkv_ref, s32[1,1024]{1,0:T(1,128)S(1)} %bitcast.316, s32[1024,1]{1,0:T(8,128)S(1)} %copy.40.docs_col_ref), custom_call_target="tpu_custom_call" | custom-call | flops 4294967296 | bytes 4194304 | tf_op jit(solution)/shard_map/attend/pallas_call | solution.py:65
  445.3 14.4 %collective-permute-done.57 = bf16[256,2048]{1,0:T(8,128)(2,1)S(1)} collective-permute-done((bf16[256,2048]{1,0:T(8,128)(2,1)S(1)}, bf16[256,2048]{1,0:T(8,128)(2,1)S(1)}, u32[]{:S(2)}, u32[]{:S(2)}) %collective-permute-start.57) | collective-permute-done | bytes 1048608 | tf_op jit(solution)/shard_map/ppermute | solution.py:170
  464.3 10.9 fusion.23
  512.0 11.4 collective-permute-done.66
  532.6 16.1 %collective-permute-done.65 = bf16[256,2048]{1,0:T(8,128)(2,1)S(1)} collective-permute-done((bf16[256,2048]{1,0:T(8,128)(2,1)S(1)}, bf16[256,2048]{1,0:T(8,128)(2,1)S(1)}, u32[]{:S(2)}, u32[]{:S(2)}) %collective-permute-start.65) | collective-permute-done | bytes 1048608 | tf_op jit(solution)/shard_map/ppermute | solution.py:170
  556.6 10.8 multiply_convert_fusion.3
  582.2 10.7 multiply_convert_fusion.2
  639.7 13.8 %collective-permute-done.67 = bf16[1,256,1024]{2,1,0:T(8,128)(2,1)S(1)} collective-permute-done((bf16[1,256,1024]{2,1,0:T(8,128)(2,1)S(1)}, bf16[1,256,1024]{2,1,0:T(8,128)(2,1)S(1)}, u32[]{:S(2)}, u32[]{:S(2)}) %collective-permute-start.67) | collective-permute-done | bytes 524320 | tf_op jit(solution)/shard_map/ppermute | solution.py:170
  696.8 14.4 %attend_back.2 = bf16[1024,1536]{1,0:T(8,128)(2,1)S(1)} custom-call(bf16[1024,1536]{1,0:T(8,128)(2,1)} %copy-done.5, bf16[1024,512]{1,0:T(8,128)(2,1)S(1)} %constant_dynamic-update-slice_fusion.32.grad_ref, f32[4,1,1024]{2,1,0:T(1,128)S(1)} %get-tuple-element.845.log_ref, s32[1,1024]{1,0:T(1,128)S(1)} %bitcast.317, s32[1024,1]{1,0:T(8,128)S(1)} %copy-done.7), custom_call_target="tpu_custom_call" | custom-call | flops 10737418240 | bytes 8388608 | tf_op jit(solution)/shard_map/attend_back/pallas_call | solution.py:124
  749.8 15.2 %collective-permute-done.81 = bf16[256,2048]{1,0:T(8,128)(2,1)S(1)} collective-permute-done((bf16[256,2048]{1,0:T(8,128)(2,1)S(1)}, bf16[256,2048]{1,0:T(8,128)(2,1)S(1)}, u32[]{:S(2)}, u32[]{:S(2)}) %collective-permute-start.81) | collective-permute-done | bytes 1048608 | tf_op jit(solution)/shard_map/ppermute | solution.py:170
  811.0 11.1 multiply_convert_fusion
  822.1 12.9 %collective-permute-done.86 = bf16[1024,512]{1,0:T(8,128)(2,1)S(1)} collective-permute-done((bf16[1024,512]{1,0:T(8,128)(2,1)S(1)}, bf16[1024,512]{1,0:T(8,128)(2,1)S(1)}, u32[]{:S(2)}, u32[]{:S(2)}) %collective-permute-start.86) | collective-permute-done | bytes 1048608 | tf_op jit(solution)/shard_map/ppermute | solution.py:170
  848.5 11.2 collective-permute-done.90
  900.8 18.3 %collective-permute-done.92 = bf16[256,2048]{1,0:T(8,128)(2,1)} collective-permute-done((bf16[256,2048]{1,0:T(8,128)(2,1)}, bf16[256,2048]{1,0:T(8,128)(2,1)}, u32[]{:S(2)}, u32[]{:S(2)}) %collective-permute-start.92) | collective-permute-done | bytes 1048608 | tf_op jit(solution)/shard_map/ppermute | solution.py:170
  968.1 14.2 %attend_back.3 = bf16[1024,1536]{1,0:T(8,128)(2,1)S(1)} custom-call(bf16[1024,1536]{1,0:T(8,128)(2,1)} %copy-done.4, bf16[1024,512]{1,0:T(8,128)(2,1)S(1)} %constant_dynamic-update-slice_fusion.42.grad_ref, f32[4,1,1024]{2,1,0:T(1,128)S(1)} %get-tuple-element.710.log_ref, s32[1,1024]{1,0:T(1,128)S(1)} %bitcast.318, s32[1024,1]{1,0:T(8,128)S(1)} %copy-done.8), custom_call_target="tpu_custom_call" | custom-call | flops 10737418240 | bytes 8388608 | tf_op jit(solution)/shard_map/attend_back/pallas_call | solution.py:124
  1028.8 15.0 %collective-permute-done.101 = bf16[512,1024]{1,0:T(8,128)(2,1)S(1)} collective-permute-done((bf16[512,1024]{1,0:T(8,128)(2,1)S(1)}, bf16[512,1024]{1,0:T(8,128)(2,1)S(1)}, u32[]{:S(2)}, u32[]{:S(2)}) %collective-permute-start.101) | collective-permute-done | bytes 1048608 | tf_op jit(solution)/shard_map/ppermute | solution.py:170
  1054.3 21.7 %collective-permute-done.108 = bf16[512,1024]{1,0:T(8,128)(2,1)S(1)} collective-permute-done((bf16[512,1024]{1,0:T(8,128)(2,1)S(1)}, bf16[512,1024]{1,0:T(8,128)(2,1)S(1)}, u32[]{:S(2)}, u32[]{:S(2)}) %collective-permute-start.108) | collective-permute-done | bytes 1048608 | tf_op jit(solution)/shard_map/ppermute | solution.py:173
  1105.0 16.8 %collective-permute-done.116 = bf16[512,1024]{1,0:T(8,128)(2,1)S(1)} collective-permute-done((bf16[512,1024]{1,0:T(8,128)(2,1)S(1)}, bf16[512,1024]{1,0:T(8,128)(2,1)S(1)}, u32[]{:S(2)}, u32[]{:S(2)}) %collective-permute-start.116) | collective-permute-done | bytes 1048608 | tf_op jit(solution)/shard_map/ppermute | solution.py:170
  1137.4 12.1 %collective-permute-done.123 = bf16[512,1024]{1,0:T(8,128)(2,1)} collective-permute-done((bf16[512,1024]{1,0:T(8,128)(2,1)}, bf16[512,1024]{1,0:T(8,128)(2,1)}, u32[]{:S(2)}, u32[]{:S(2)}) %collective-permute-start.123) | collective-permute-done | bytes 1048608 | tf_op jit(solution)/shard_map/ppermute | solution.py:173
  1155.6 10.9 collective-permute-done.125
  1171.4 14.4 %collective-permute-done.126 = bf16[512,768]{1,0:T(8,128)(2,1)S(1)} collective-permute-done((bf16[512,768]{1,0:T(8,128)(2,1)S(1)}, bf16[512,768]{1,0:T(8,128)(2,1)S(1)}, u32[]{:S(2)}, u32[]{:S(2)}) %collective-permute-start.126) | collective-permute-done | bytes 786464 | tf_op jit(solution)/shard_map/ppermute | solution.py:173
  1191.5 10.9 collective-permute-done.128
  (1050 shorter events, 758.8 us)
Async XLA Ops:
  39.4 32.6 %collective-permute-start.16 = (bf16[512,1024]{1,0:T(8,128)(2,1)}, bf16[512,1024]{1,0:T(8,128)(2,1)}, u32[]{:S(2)}, u32[]{:S(2)}) collective-permute-start(bf16[512,1024]{1,0:T(8,128)(2,1)} %param.30), channel_id=1, source_target_pairs={{0,2},{1,3},{2,0},{3,1},{4,6},{5,7},{6,4},{7,5},{8,10},{9,11},{10,... | collective-permute-start | bytes 3145736 | tf_op jit(solution)/shard_map/ppermute | solution.py:170
  46.0 34.3 %collective-permute-start.5 = (bf16[256,2048]{1,0:T(8,128)(2,1)S(1)}, bf16[256,2048]{1,0:T(8,128)(2,1)}, u32[]{:S(2)}, u32[]{:S(2)}) collective-permute-start(bf16[256,2048]{1,0:T(8,128)(2,1)S(1)} %get-tuple-element.674), channel_id=1, source_target_pairs={{0,1},{1,0},{2,3},{3,2},{4,5},{5,4},{6,7},{7,6},{8,9},{9,8},{10,11... | collective-permute-start | bytes 3145736 | tf_op jit(solution)/shard_map/ppermute | solution.py:170
  72.1 30.5 %collective-permute-start.17 = (bf16[256,2048]{1,0:T(8,128)(2,1)S(1)}, bf16[256,2048]{1,0:T(8,128)(2,1)}, u32[]{:S(2)}, u32[]{:S(2)}) collective-permute-start(bf16[256,2048]{1,0:T(8,128)(2,1)S(1)} %get-tuple-element.674), channel_id=1, source_target_pairs={{0,2},{1,3},{2,0},{3,1},{4,6},{5,7},{6,4},{7,5},{8,10},{9,11},{10,... | collective-permute-start | bytes 3145736 | tf_op jit(solution)/shard_map/ppermute | solution.py:170
  123.4 26.7 %collective-permute-start.25 = (bf16[512,1024]{1,0:T(8,128)(2,1)}, bf16[512,1024]{1,0:T(8,128)(2,1)S(1)}, u32[]{:S(2)}, u32[]{:S(2)}) collective-permute-start(bf16[512,1024]{1,0:T(8,128)(2,1)} %collective-permute-done.23), channel_id=1, source_target_pairs={{0,8},{8,16},{16,24},{24,0},{1,9},{9,17},{17,25},{25,1},{2,10},{10... | collective-permute-start | bytes 3145736 | tf_op jit(solution)/shard_map/ppermute | solution.py:173
  166.5 25.8 %collective-permute-start.27 = (bf16[512,1024]{1,0:T(8,128)(2,1)}, bf16[512,1024]{1,0:T(8,128)(2,1)S(1)}, u32[]{:S(2)}, u32[]{:S(2)}) collective-permute-start(bf16[512,1024]{1,0:T(8,128)(2,1)} %collective-permute-done.23), channel_id=1, source_target_pairs={{0,2},{1,3},{2,0},{3,1},{4,6},{5,7},{6,4},{7,5},{8,10},{9,11},{10,... | collective-permute-start | bytes 3145736 | tf_op jit(solution)/shard_map/ppermute | solution.py:170
  167.1 28.4 %collective-permute-start.31 = (bf16[512,1024]{1,0:T(8,128)(2,1)S(1)}, bf16[512,1024]{1,0:T(8,128)(2,1)}, u32[]{:S(2)}, u32[]{:S(2)}) collective-permute-start(bf16[512,1024]{1,0:T(8,128)(2,1)S(1)} %collective-permute-done.25), channel_id=1, source_target_pairs={{0,8},{8,16},{16,24},{24,0},{1,9},{9,17},{17,25},{25,1},{2,10},{10... | collective-permute-start | bytes 3145736 | tf_op jit(solution)/shard_map/ppermute | solution.py:173
  242.2 27.0 %collective-permute-start.35 = (bf16[512,1024]{1,0:T(8,128)(2,1)}, bf16[512,1024]{1,0:T(8,128)(2,1)}, u32[]{:S(2)}, u32[]{:S(2)}) collective-permute-start(bf16[512,1024]{1,0:T(8,128)(2,1)} %collective-permute-done.31), channel_id=1, source_target_pairs={{0,2},{1,3},{2,0},{3,1},{4,6},{5,7},{6,4},{7,5},{8,10},{9,11},{10,... | collective-permute-start | bytes 3145736 | tf_op jit(solution)/shard_map/ppermute | solution.py:170
  269.2 28.7 %collective-permute-start.43 = (bf16[512,512]{1,0:T(8,128)(2,1)}, bf16[512,512]{1,0:T(8,128)(2,1)S(1)}, u32[]{:S(2)}, u32[]{:S(2)}) collective-permute-start(bf16[512,512]{1,0:T(8,128)(2,1)} %copy-done.149), channel_id=1, source_target_pairs={{0,8},{8,16},{16,24},{24,0},{1,9},{9,17},{17,25},{25,1},{2,10},{10... | collective-permute-start | bytes 1572872 | tf_op jit(solution)/shard_map/ppermute | solution.py:173
  269.2 28.7 %collective-permute-start.41 = (bf16[512,512]{1,0:T(8,128)(2,1)}, bf16[512,512]{1,0:T(8,128)(2,1)S(1)}, u32[]{:S(2)}, u32[]{:S(2)}) collective-permute-start(bf16[512,512]{1,0:T(8,128)(2,1)} %copy-done.148), channel_id=1, source_target_pairs={{0,2},{1,3},{2,0},{3,1},{4,6},{5,7},{6,4},{7,5},{8,10},{9,11},{10,... | collective-permute-start | bytes 1572872 | tf_op jit(solution)/shard_map/ppermute | solution.py:170
  381.5 25.6 %collective-permute-start.53 = (bf16[256,2048]{1,0:T(8,128)(2,1)S(1)}, bf16[256,2048]{1,0:T(8,128)(2,1)S(1)}, u32[]{:S(2)}, u32[]{:S(2)}) collective-permute-start(bf16[256,2048]{1,0:T(8,128)(2,1)S(1)} %get-tuple-element.834), channel_id=1, source_target_pairs={{0,2},{1,3},{2,0},{3,1},{4,6},{5,7},{6,4},{7,5},{8,10},{9,11},{10,... | collective-permute-start | bytes 3145736 | tf_op jit(solution)/shard_map/ppermute | solution.py:170
  461.5 25.6 %collective-permute-start.62 = (bf16[256,2048]{1,0:T(8,128)(2,1)S(1)}, bf16[256,2048]{1,0:T(8,128)(2,1)S(1)}, u32[]{:S(2)}, u32[]{:S(2)}) collective-permute-start(bf16[256,2048]{1,0:T(8,128)(2,1)S(1)} %get-tuple-element.878), channel_id=1, source_target_pairs={{0,4},{1,5},{2,6},{3,7},{4,0},{5,1},{6,2},{7,3},{8,12},{9,13},{10,... | collective-permute-start | bytes 3145736 | tf_op jit(solution)/shard_map/ppermute | solution.py:170
  553.7 25.6 %collective-permute-start.68 = (bf16[256,2048]{1,0:T(8,128)(2,1)S(1)}, bf16[256,2048]{1,0:T(8,128)(2,1)S(1)}, u32[]{:S(2)}, u32[]{:S(2)}) collective-permute-start(bf16[256,2048]{1,0:T(8,128)(2,1)S(1)} %get-tuple-element.912), channel_id=1, source_target_pairs={{0,4},{1,5},{2,6},{3,7},{4,0},{5,1},{6,2},{7,3},{8,12},{9,13},{10,... | collective-permute-start | bytes 3145736 | tf_op jit(solution)/shard_map/ppermute | solution.py:170
  603.3 28.7 %collective-permute-start.74 = (bf16[256,2048]{1,0:T(8,128)(2,1)S(1)}, bf16[256,2048]{1,0:T(8,128)(2,1)S(1)}, u32[]{:S(2)}, u32[]{:S(2)}) collective-permute-start(bf16[256,2048]{1,0:T(8,128)(2,1)S(1)} %get-tuple-element.934), channel_id=1, source_target_pairs={{0,1},{1,0},{2,3},{3,2},{4,5},{5,4},{6,7},{7,6},{8,9},{9,8},{10,11... | collective-permute-start | bytes 3145736 | tf_op jit(solution)/shard_map/ppermute | solution.py:170
  605.0 27.0 %collective-permute-start.72 = (bf16[256,2048]{1,0:T(8,128)(2,1)S(1)}, bf16[256,2048]{1,0:T(8,128)(2,1)S(1)}, u32[]{:S(2)}, u32[]{:S(2)}) collective-permute-start(bf16[256,2048]{1,0:T(8,128)(2,1)S(1)} %add_convert_fusion.19), channel_id=1, source_target_pairs={{0,4},{1,5},{2,6},{3,7},{4,0},{5,1},{6,2},{7,3},{8,12},{9,13},{10,... | collective-permute-start | bytes 3145736 | tf_op jit(solution)/shard_map/ppermute | solution.py:170
  653.5 27.2 %collective-permute-start.76 = (bf16[256,2048]{1,0:T(8,128)(2,1)}, bf16[256,2048]{1,0:T(8,128)(2,1)}, u32[]{:S(2)}, u32[]{:S(2)}) collective-permute-start(bf16[256,2048]{1,0:T(8,128)(2,1)} %get-tuple-element.965), channel_id=1, source_target_pairs={{0,2},{1,3},{2,0},{3,1},{4,6},{5,7},{6,4},{7,5},{8,10},{9,11},{10,... | collective-permute-start | bytes 3145736 | tf_op jit(solution)/shard_map/ppermute | solution.py:170
  715.6 34.2 %collective-permute-start.80 = (bf16[256,2048]{1,0:T(8,128)(2,1)S(1)}, bf16[256,2048]{1,0:T(8,128)(2,1)S(1)}, u32[]{:S(2)}, u32[]{:S(2)}) collective-permute-start(bf16[256,2048]{1,0:T(8,128)(2,1)S(1)} %get-tuple-element.1006), channel_id=1, source_target_pairs={{0,1},{1,0},{2,3},{3,2},{4,5},{5,4},{6,7},{7,6},{8,9},{9,8},{10,11... | collective-permute-start | bytes 3145736 | tf_op jit(solution)/shard_map/ppermute | solution.py:170
  847.9 33.2 %collective-permute-start.83 = (bf16[256,2048]{1,0:T(8,128)(2,1)S(1)}, bf16[256,2048]{1,0:T(8,128)(2,1)S(1)}, u32[]{:S(2)}, u32[]{:S(2)}) collective-permute-start(bf16[256,2048]{1,0:T(8,128)(2,1)S(1)} %get-tuple-element.1055), channel_id=1, source_target_pairs={{0,1},{1,0},{2,3},{3,2},{4,5},{5,4},{6,7},{7,6},{8,9},{9,8},{10,11... | collective-permute-start | bytes 3145736 | tf_op jit(solution)/shard_map/ppermute | solution.py:170
  859.7 33.3 %collective-permute-start.91 = (bf16[1024,512]{1,0:T(8,128)(2,1)S(1)}, bf16[1024,512]{1,0:T(8,128)(2,1)}, u32[]{:S(2)}, u32[]{:S(2)}) collective-permute-start(bf16[1024,512]{1,0:T(8,128)(2,1)S(1)} %copy-done.181), channel_id=1, source_target_pairs={{0,2},{1,3},{2,0},{3,1},{4,6},{5,7},{6,4},{7,5},{8,10},{9,11},{10,... | collective-permute-start | bytes 3145736 | tf_op jit(solution)/shard_map/ppermute | solution.py:170
  893.2 25.9 %collective-permute-start.92 = (bf16[256,2048]{1,0:T(8,128)(2,1)}, bf16[256,2048]{1,0:T(8,128)(2,1)}, u32[]{:S(2)}, u32[]{:S(2)}) collective-permute-start(bf16[256,2048]{1,0:T(8,128)(2,1)} %get-tuple-element.1108), channel_id=1, source_target_pairs={{0,2},{1,3},{2,0},{3,1},{4,6},{5,7},{6,4},{7,5},{8,10},{9,11},{10,... | collective-permute-start | bytes 3145736 | tf_op jit(solution)/shard_map/ppermute | solution.py:170
  899.4 27.4 %collective-permute-start.93 = (bf16[1024,512]{1,0:T(8,128)(2,1)S(1)}, bf16[1024,512]{1,0:T(8,128)(2,1)S(1)}, u32[]{:S(2)}, u32[]{:S(2)}) collective-permute-start(bf16[1024,512]{1,0:T(8,128)(2,1)S(1)} %copy-done.123), channel_id=1, source_target_pairs={{0,8},{8,16},{16,24},{24,0},{1,9},{9,17},{17,25},{25,1},{2,10},{10... | collective-permute-start | bytes 3145736 | tf_op jit(solution)/shard_map/ppermute | solution.py:173
  937.7 25.8 %collective-permute-start.95 = (bf16[1024,512]{1,0:T(8,128)(2,1)}, bf16[1024,512]{1,0:T(8,128)(2,1)S(1)}, u32[]{:S(2)}, u32[]{:S(2)}) collective-permute-start(bf16[1024,512]{1,0:T(8,128)(2,1)} %add_convert_fusion.7), channel_id=1, source_target_pairs={{0,8},{8,16},{16,24},{24,0},{1,9},{9,17},{17,25},{25,1},{2,10},{10... | collective-permute-start | bytes 3145736 | tf_op jit(solution)/shard_map/ppermute | solution.py:173
  944.1 40.8 %collective-permute-start.99 = (f32[1024]{0:T(1024)S(1)}, f32[1024]{0:T(1024)S(1)}, u32[]{:S(2)}, u32[]{:S(2)}) collective-permute-start(f32[1024]{0:T(1024)S(1)} %slice.429), channel_id=1, source_target_pairs={{0,2},{1,3},{2,0},{3,1},{4,6},{5,7},{6,4},{7,5},{8,10},{9,11},{10,... | collective-permute-start | bytes 12296 | tf_op jit(solution)/shard_map/ppermute | solution.py:170
  945.0 39.8 %collective-permute-start.98 = (f32[6,512]{1,0:T(8,128)S(1)}, f32[6,512]{1,0:T(8,128)S(1)}, u32[]{:S(2)}, u32[]{:S(2)}) collective-permute-start(f32[6,512]{1,0:T(8,128)S(1)} %constant_dynamic-slice_fusion.5), channel_id=1, source_target_pairs={{0,2},{1,3},{2,0},{3,1},{4,6},{5,7},{6,4},{7,5},{8,10},{9,11},{10,... | collective-permute-start | bytes 36872 | tf_op jit(solution)/shard_map/ppermute | solution.py:170
  984.4 30.9 %collective-permute-start.107 = (bf16[1024,512]{1,0:T(8,128)(2,1)}, bf16[1024,512]{1,0:T(8,128)(2,1)}, u32[]{:S(2)}, u32[]{:S(2)}) collective-permute-start(bf16[1024,512]{1,0:T(8,128)(2,1)} %pad_maximum_fusion.49), channel_id=1, source_target_pairs={{0,4},{1,5},{2,6},{3,7},{4,0},{5,1},{6,2},{7,3},{8,12},{9,13},{10,... | collective-permute-start | bytes 3145736 | tf_op jit(solution)/shard_map/ppermute | solution.py:170
  1014.7 122.7 %collective-permute-start.122 = (f32[6,256]{1,0:T(8,128)S(1)}, f32[6,256]{1,0:T(8,128)S(1)}, u32[]{:S(2)}, u32[]{:S(2)}) collective-permute-start(f32[6,256]{1,0:T(8,128)S(1)} %constant_dynamic-slice_fusion), channel_id=1, source_target_pairs={{0,1},{1,0},{2,3},{3,2},{4,5},{5,4},{6,7},{7,6},{8,9},{9,8},{10,11... | collective-permute-start | bytes 18440 | tf_op jit(solution)/shard_map/ppermute | solution.py:170
  1020.0 26.8 %collective-permute-start.103 = (bf16[512,1024]{1,0:T(8,128)(2,1)S(1)}, bf16[512,1024]{1,0:T(8,128)(2,1)S(1)}, u32[]{:S(2)}, u32[]{:S(2)}) collective-permute-start(bf16[512,1024]{1,0:T(8,128)(2,1)S(1)} %copy-done.126), channel_id=1, source_target_pairs={{0,8},{8,16},{16,24},{24,0},{1,9},{9,17},{17,25},{25,1},{2,10},{10... | collective-permute-start | bytes 3145736 | tf_op jit(solution)/shard_map/ppermute | solution.py:173
  1046.8 30.3 %collective-permute-start.113 = (bf16[512,768]{1,0:T(8,128)(2,1)}, bf16[512,768]{1,0:T(8,128)(2,1)}, u32[]{:S(2)}, u32[]{:S(2)}) collective-permute-start(bf16[512,768]{1,0:T(8,128)(2,1)} %add_convert_fusion.30), channel_id=1, source_target_pairs={{0,4},{1,5},{2,6},{3,7},{4,0},{5,1},{6,2},{7,3},{8,12},{9,13},{10,... | collective-permute-start | bytes 2359304 | tf_op jit(solution)/shard_map/ppermute | solution.py:170
  1050.0 26.0 %collective-permute-start.108 = (bf16[512,1024]{1,0:T(8,128)(2,1)S(1)}, bf16[512,1024]{1,0:T(8,128)(2,1)S(1)}, u32[]{:S(2)}, u32[]{:S(2)}) collective-permute-start(bf16[512,1024]{1,0:T(8,128)(2,1)S(1)} %add_convert_fusion.3), channel_id=1, source_target_pairs={{0,8},{8,16},{16,24},{24,0},{1,9},{9,17},{17,25},{25,1},{2,10},{10... | collective-permute-start | bytes 3145736 | tf_op jit(solution)/shard_map/ppermute | solution.py:173
  1077.1 26.0 %collective-permute-start.105 = (bf16[256,2048]{1,0:T(8,128)(2,1)S(1)}, bf16[256,2048]{1,0:T(8,128)(2,1)S(1)}, u32[]{:S(2)}, u32[]{:S(2)}) collective-permute-start(bf16[256,2048]{1,0:T(8,128)(2,1)S(1)} %get-tuple-element.1181), channel_id=1, source_target_pairs={{0,1},{1,0},{2,3},{3,2},{4,5},{5,4},{6,7},{7,6},{8,9},{9,8},{10,11... | collective-permute-start | bytes 3145736 | tf_op jit(solution)/shard_map/ppermute | solution.py:170
  1077.1 26.7 %collective-permute-start.114 = (bf16[512,768]{1,0:T(8,128)(2,1)S(1)}, bf16[512,768]{1,0:T(8,128)(2,1)S(1)}, u32[]{:S(2)}, u32[]{:S(2)}) collective-permute-start(bf16[512,768]{1,0:T(8,128)(2,1)S(1)} %copy-done.183), channel_id=1, source_target_pairs={{0,4},{1,5},{2,6},{3,7},{4,0},{5,1},{6,2},{7,3},{8,12},{9,13},{10,... | collective-permute-start | bytes 2359304 | tf_op jit(solution)/shard_map/ppermute | solution.py:170
  1136.5 30.0 %collective-permute-start.127 = (bf16[512,1024]{1,0:T(8,128)(2,1)}, bf16[512,1024]{1,0:T(8,128)(2,1)}, u32[]{:S(2)}, u32[]{:S(2)}) collective-permute-start(bf16[512,1024]{1,0:T(8,128)(2,1)} %add_convert_fusion.8), channel_id=1, source_target_pairs={{0,2},{1,3},{2,0},{3,1},{4,6},{5,7},{6,4},{7,5},{8,10},{9,11},{10,... | collective-permute-start | bytes 3145736 | tf_op jit(solution)/shard_map/ppermute | solution.py:170
  1150.7 40.7 %collective-permute-start.121 = (bf16[512,768]{1,0:T(8,128)(2,1)S(1)}, bf16[512,768]{1,0:T(8,128)(2,1)S(1)}, u32[]{:S(2)}, u32[]{:S(2)}) collective-permute-start(bf16[512,768]{1,0:T(8,128)(2,1)S(1)} %copy-done.182), channel_id=1, source_target_pairs={{0,4},{1,5},{2,6},{3,7},{4,0},{5,1},{6,2},{7,3},{8,12},{9,13},{10,... | collective-permute-start | bytes 2359304 | tf_op jit(solution)/shard_map/ppermute | solution.py:170
  (298 other events, 4502.7 us)

commit v3 on v2

--- a/solution.py
+++ b/solution.py
@@ -417,8 +417,10 @@
             )
         return (terms, jnp.zeros_like(terms))
 
-    def sum_far(self, terms):
+    def sum_far(self, terms, meanwhile=None):
         kept, got = self.halved(terms)
+        if meanwhile is not None:
+            meanwhile()
         part = self.clock.run(
             lambda own, more: (own.astype(f32) + more.astype(f32)).astype(bf16), kept, got
         )
@@ -592,15 +594,20 @@
     ring.arrived(2, "up")
     steps_of("up" if rows > 3 else "down0")
     mixed, log_total = run(lambda item: attend(item, span, *docs), qkv)
+    clock.wait(ring.other["up"][1])
     for step in range(rows):
         puts(step, 1, "out")
     w_out = ring.wholes["out"]
     half = mixed.shape[0] // 2
-    terms = run(product, mixed[half:], w_out)
-    sent = across_b.sum_far(terms)
-    puts(1, 1, "up")
-    terms = run(product, mixed[:half], w_out)
-    sums = across_b.halved(terms)
+    terms_other = run(product, mixed[half:], w_out)
+    terms_own = []
+
+    def meanwhile():
+        terms_own.append(run(product, mixed[:half], w_out))
+        puts(1, 1, "up")
+
+    sent = across_b.sum_far(terms_other, meanwhile)
+    sums = across_b.halved(terms_own[0])
     exchanges("up")
     puts(2, 0, "up")
     for step in range(3, rows):
@@ -690,10 +697,14 @@
         if depth == 1:
             grad = place.tokens_send(grad, place.a, lane_a, 2)
         mixed, log_total = run(lambda item: attend(item, span, *docs), qkv)
-        terms = run(product, mixed[half:], w_out)
-        sent = across_b.sum_far(terms)
-        terms = run(product, mixed[:half], w_out)
-        sums = across_b.halved(terms)
+        if depth == 1:
+            clock.wait(grad[1])
+        terms_other = run(product, mixed[half:], w_out)
+        terms_own = []
+        sent = across_b.sum_far(
+            terms_other, lambda: terms_own.append(run(product, mixed[:half], w_out))
+        )
+        sums = across_b.halved(terms_own[0])
         token_pieces = run(blocks, own, other)
         if depth == 1:
             grad = run(merge(place.a), *grad)
@@ -706,6 +717,8 @@
         hidden_own, active_own = run(up_product, own, w_up, b_up)
         terms_own = run(product, active_own, w_down)
         own_sums = across_a.halved(terms_own)
+        if depth == 1:
+            clock.wait(grad[1])
         other = across_a.near(far)
         hidden_other, active_other = run(up_product, other, w_up, b_up)
         terms_other = run(product, active_other, w_down)
@@ -742,6 +755,7 @@
             self.lane, self.far = lane, far
             self.before = held.get(name)
             self.got = []
+            self.sent = []
             self.total = None
             self.step = 0
 
@@ -753,9 +767,11 @@
             ]
             held[self.name] = clock.last
 
-        def other(self):
-            self.sent = []
-            for step in range(rows):
+        def other_first(self):
+            self.other(1)
+
+        def other(self, count=None):
+            for step in range(len(self.sent), rows if count is None else count):
                 left, right = clock.hold((self.left[1][step], self.right[1][step]))
                 clock.last = (dot_g(left, right) + self.before[1][step]).astype(bf16)
                 self.sent.append(clock.last)
@@ -821,16 +837,21 @@
             down = down_share()
             down.other()
             down.send(3)
-        else:
-            output = run(lambda *items: place.features_merge(*items, place.b, 1), *output)
         dhid_other = run(gelu_back, second_other, w_down, hiddens[1])
-        if last:
-            clock.wait(down.got[0])
         terms_other = run(product_t, dhid_other, w_up)
-        sent = across_a.sum_far(terms_other)
+        if not last:
+            clock.wait(output[1])
+            output = clock.aside(lambda *items: place.features_merge(*items, place.b, 1), *output)
+        sides = []
+        sent = across_a.sum_far(
+            terms_other,
+            lambda: sides.extend(
+                run(lambda *items: columns(items, hidden_span), dhid_own, dhid_other)
+            ),
+        )
+        dhid_left, dhid_right = sides
         if last:
             down.advance()
-        dhid_left, dhid_right = run(lambda *items: columns(items, hidden_span), dhid_own, dhid_other)
         up = Share(
             "up",
             (first_pieces, first_pieces),
@@ -853,18 +874,11 @@
             token_sums = place.halve(sum(norm_sums), place.a, lane_a)
             down.advance()
             down.send(rows - 3)
-            mine, away = place.parts(token_sums, place.b)
-            more = lane_b.send(
-                lambda items: tuple(place.swap(item, place.b) for item in items),
-                (away, hidden_total[hidden_span:]),
-            )
-            token_sums = mine + more[0]
-            hidden_total = hidden_total[:hidden_span] + more[1]
-            for mask in place.rest[::-1]:
-                token_sums = place.halve(token_sums, mask, None)
+            up.send()
         else:
             output = place.features_send(output, place.a, lane_a)
             up.keep()
+            clock.wait(output[1])
             hidden_sums.append(clock.aside(sum_rows, dhid_left, dhid_right))
         branch_other = across_b.near(far)
         dmixed_other = run(product_t, branch_other, w_out)
@@ -881,37 +895,48 @@
             out.other()
             out.send_all()
             down.advance()
+            clock.wait(up.got[0])
+            up.send()
         else:
-            output = run(lambda *items: place.features_merge(*items, place.a, 0), *output)
+            output = clock.aside(lambda *items: place.features_merge(*items, place.a, 0), *output)
         dqkv = run(lambda *items: attend_back(*items, log_total, span, *docs), qkv, dmixed)
         qkv_sums.append(clock.aside(sum_rows, dqkv))
         if last:
-            up.send(2)
+            clock.wait(out.got, up.got[1])
             while down.step < rows:
                 down.advance()
             up.advance()
         terms_other = run(product_t, dqkv[half:], w_qkv)
-        sent = across_b.sum_far(terms_other)
-        if not last:
+        if last:
+            both = Share(
+                "qkv",
+                (token_pieces, token_pieces),
+                ([dqkv[:, : 3 * span]] * rows, [dqkv[:, 3 * span :]] * rows),
+                lane_a,
+                place.a,
+            )
+            sent = across_b.sum_far(terms_other, both.other_first)
+            both.send()
+        else:
+            sent = across_b.sum_far(terms_other)
             for mask in place.rest[::-1]:
                 output = run(
                     lambda *items: place.features_merge(*items, mask, 1),
                     *place.features_send(output, mask, None),
                 )
-        both = Share(
-            "qkv",
-            (token_pieces, token_pieces),
-            ([dqkv[:, : 3 * span]] * rows, [dqkv[:, 3 * span :]] * rows),
-            lane_a,
-            place.a,
-        )
+        if not last:
+            both = Share(
+                "qkv",
+                (token_pieces, token_pieces),
+                ([dqkv[:, : 3 * span]] * rows, [dqkv[:, 3 * span :]] * rows),
+                lane_a,
+                place.a,
+            )
         if last:
             both.other()
-            qkv_total = sum(qkv_sums)
-            qkv_total = qkv_total[: 3 * span] + lane_a.send(
-                lambda item: place.swap(item, place.a), qkv_total[3 * span :]
-            )
-            both.send(2)
+            both.send()
+            clock.wait(sent)
+            up.send()
             up.advance()
         terms_own = run(product_t, dqkv[:half], w_qkv)
         own_sums = across_b.halved(terms_own)
@@ -919,20 +944,17 @@
             out.keep()
             both.keep()
         grads = (dr1, *own_sums, sent)
+    clock.wait(own_sums)
     for step in range(rows):
         out.advance()
     grad = run(lambda *items: plus(*items).astype(bf16)[None], *grads)
     grad = place.features_send(grad, place.a, lane_a)
-    up.send()
     both.send(rows - 2)
     both.advance()
     grad = run(lambda *items: place.features_merge(*items, place.a, 0), *grad)
+    up.send(rows - len(up.got))
     grad = place.features_send(grad, place.b, lane_b)
-    up.send(rows - len(up.got))
     up.advance()
-    sums = place.row_sum(
-        jnp.concatenate([token_sums.reshape(-1), qkv_total, hidden_total]), row_lane
-    )
     both.advance()
     grad = run(lambda *items: place.features_merge(*items, place.b, 1), *grad)
     for mask in place.rest[::-1]:
@@ -942,6 +964,26 @@
         )
     grad_tokens = grad.reshape(-1, span).astype(f32)
     output = output.reshape(-1, span)
+    qkv_total = sum(qkv_sums)
+    qkv_total = qkv_total[: 3 * span] + lane_a.send(
+        lambda item: place.swap(item, place.a), qkv_total[3 * span :]
+    )
+    mine, away = place.parts(token_sums, place.b)
+    more = lane_b.send(
+        lambda items: tuple(place.swap(item, place.b) for item in items),
+        (away, hidden_total[hidden_span:]),
+    )
+    token_sums = mine + more[0]
+    hidden_total = hidden_total[:hidden_span] + more[1]
+    for mask in place.rest[::-1]:
+        token_sums = place.halve(token_sums, mask, None)
+    while both.step < rows - 1:
+        both.advance()
+        if up.step < rows:
+            up.advance()
+    sums = place.row_sum(
+        jnp.concatenate([token_sums.reshape(-1), qkv_total, hidden_total]), row_lane
+    )
     while up.step < rows:
         up.advance()
     while both.step < rows:

time: 1220 us -> 1160 us (0.951)
  waiting for transfers between devices: 540 us -> 466 us
    ppermute x97, waiting for transfers between devices: 339 us -> 270 us  [swap(): return lax.ppermute(value, 'col', [(i, i ^ mask) for i in range(self.cols)])]
    unnamed x425 -> x393, local copies, waits for them, and re-layouts: 35 us -> 33.5 us
  transfers between devices with their start and end apart: 129 -> 129, of which waited for: 75 -> 76; matrix products, arithmetic and copies ran while one was open for 34% -> 36% of each run, Pallas kernels for 2% -> 3%
where the time goes in v3:
time: 1160 us; the launch traced here: 1150 us
  waiting for transfers between devices  466 us (40%)
  matrix products  323 us (28%)
  local copies, waits for them, and re-layouts  126 us (11%)
  other arithmetic  92.5 us (8%)
  starting transfers between devices  80 us (7%)
  Pallas kernels  53.8 us (5%)
    ppermute x97, waiting for transfers between devices, swap(): return lax.ppermute(value, 'col', [(i, i ^ mask) for i in range(self.cols)])  270 us
    ppermute x30, waiting for transfers between devices, shift(): lax.ppermute(value, 'row', [(i, (i + 1) % self.rows) for i in range(self....  191 us
    dot_general x64, matrix products, dot_g(): lax.dot_general(left, right, (((0,), (0,)), ((), ())), preferred_element_...  114 us
    dot_general x16, matrix products, dot_t(): lax.dot_general(left, right, (((1,), (1,)), ((), ())), preferred_element_...  112 us
    dot_general x16, matrix products, dot(): lax.dot_general(left, right, (((1,), (0,)), ((), ())), preferred_element_...  97.6 us
    ppermute x97, starting transfers between devices, swap(): return lax.ppermute(value, 'col', [(i, i ^ mask) for i in range(self.cols)])  68.9 us
    dynamic_update_slice x40, local copies, waits for them, and re-layouts, put(): lax.dynamic_update_slice(total, item, start)  49 us
    unnamed x393, local copies, waits for them, and re-layouts  33.5 us
  transfers between devices with their start and end apart: 129, of which 76 were waited for; matrix products, arithmetic and copies ran while one was open for 36% of the time, Pallas kernels for 3%

profile of v3, /device:TPU:0, one launch (start us, length us, event | category | flops | bytes accessed | tf_op | source)
XLA Modules:
  0.0 1146.3 jit_solution(7069118116070481233)
XLA Ops:
  56.9 13.0 %collective-permute-done.13 = bf16[512,768]{1,0:T(8,128)(2,1)} collective-permute-done((bf16[512,768]{1,0:T(8,128)(2,1)S(1)}, bf16[512,768]{1,0:T(8,128)(2,1)}, u32[]{:S(2)}, u32[]{:S(2)}) %collective-permute-start.13) | collective-permute-done | bytes 786464 | tf_op jit(solution)/shard_map/ppermute | solution.py:173
  110.6 12.9 %collective-permute-done.15 = bf16[512,768]{1,0:T(8,128)(2,1)} collective-permute-done((bf16[512,768]{1,0:T(8,128)(2,1)}, bf16[512,768]{1,0:T(8,128)(2,1)}, u32[]{:S(2)}, u32[]{:S(2)}) %collective-permute-start.15) | collective-permute-done | bytes 786464 | tf_op jit(solution)/shard_map/ppermute | solution.py:170
  150.9 12.6 %attend.2 = (bf16[1024,512]{1,0:T(8,128)(2,1)S(1)}, f32[4,1,1024]{2,1,0:T(1,128)S(1)}) custom-call(bf16[1024,1536]{1,0:T(8,128)(2,1)S(1)} %constant_dynamic-update-slice_fusion.8.qkv_ref, s32[1,1024]{1,0:T(1,128)S(1)} %bitcast.315, s32[1024,1]{1,0:T(8,128)S(1)} %copy.40.docs_col_ref), custom_call_target="tpu_custom_call" | custom-call | flops 4294967296 | bytes 4194304 | tf_op jit(solution)/shard_map/attend/pallas_call | solution.py:65
  180.2 10.9 collective-permute-done.32
  209.3 8.8 collective-permute-done.39
  219.6 11.0 collective-permute-done.40
  242.9 14.3 %collective-permute-done.43 = bf16[512,512]{1,0:T(8,128)(2,1)S(1)} collective-permute-done((bf16[512,512]{1,0:T(8,128)(2,1)}, bf16[512,512]{1,0:T(8,128)(2,1)S(1)}, u32[]{:S(2)}, u32[]{:S(2)}) %collective-permute-start.43) | collective-permute-done | bytes 524320 | tf_op jit(solution)/shard_map/ppermute | solution.py:173
  264.1 10.4 fusion.7
  274.6 10.4 fusion.15
  344.9 15.4 %collective-permute-done.51 = bf16[256,2048]{1,0:T(8,128)(2,1)S(1)} collective-permute-done((bf16[256,2048]{1,0:T(8,128)(2,1)S(1)}, bf16[256,2048]{1,0:T(8,128)(2,1)S(1)}, u32[]{:S(2)}, u32[]{:S(2)}) %collective-permute-start.51) | collective-permute-done | bytes 1048608 | tf_op jit(solution)/shard_map/ppermute | solution.py:170
  369.8 19.2 %collective-permute-done.53 = bf16[256,2048]{1,0:T(8,128)(2,1)S(1)} collective-permute-done((bf16[256,2048]{1,0:T(8,128)(2,1)S(1)}, bf16[256,2048]{1,0:T(8,128)(2,1)S(1)}, u32[]{:S(2)}, u32[]{:S(2)}) %collective-permute-start.53) | collective-permute-done | bytes 1048608 | tf_op jit(solution)/shard_map/ppermute | solution.py:170
  395.6 12.8 %attend.3 = (bf16[1024,512]{1,0:T(8,128)(2,1)S(1)}, f32[4,1,1024]{2,1,0:T(1,128)S(1)}) custom-call(bf16[1024,1536]{1,0:T(8,128)(2,1)S(1)} %constant_dynamic-update-slice_fusion.18.qkv_ref, s32[1,1024]{1,0:T(1,128)S(1)} %bitcast.316, s32[1024,1]{1,0:T(8,128)S(1)} %copy.40.docs_col_ref), custom_call_target="tpu_custom_call" | custom-call | flops 4294967296 | bytes 4194304 | tf_op jit(solution)/shard_map/attend/pallas_call | solution.py:65
  422.1 19.4 %collective-permute-done.59 = bf16[256,2048]{1,0:T(8,128)(2,1)S(1)} collective-permute-done((bf16[256,2048]{1,0:T(8,128)(2,1)S(1)}, bf16[256,2048]{1,0:T(8,128)(2,1)S(1)}, u32[]{:S(2)}, u32[]{:S(2)}) %collective-permute-start.59) | collective-permute-done | bytes 1048608 | tf_op jit(solution)/shard_map/ppermute | solution.py:170
  473.9 10.4 fusion.31
  505.7 15.9 %collective-permute-done.66 = bf16[256,2048]{1,0:T(8,128)(2,1)S(1)} collective-permute-done((bf16[256,2048]{1,0:T(8,128)(2,1)S(1)}, bf16[256,2048]{1,0:T(8,128)(2,1)S(1)}, u32[]{:S(2)}, u32[]{:S(2)}) %collective-permute-start.66) | collective-permute-done | bytes 1048608 | tf_op jit(solution)/shard_map/ppermute | solution.py:170
  529.9 10.9 multiply_convert_fusion.3
  540.9 10.1 convolution_convert_fusion.7
  556.8 10.7 multiply_convert_fusion.2
  567.5 8.8 convolution_convert_fusion.6
  651.0 14.4 %attend_back.2 = bf16[1024,1536]{1,0:T(8,128)(2,1)S(1)} custom-call(bf16[1024,1536]{1,0:T(8,128)(2,1)} %copy-done.7, bf16[1024,512]{1,0:T(8,128)(2,1)S(1)} %constant_dynamic-update-slice_fusion.32.grad_ref, f32[4,1,1024]{2,1,0:T(1,128)S(1)} %get-tuple-element.845.log_ref, s32[1,1024]{1,0:T(1,128)S(1)} %bitcast.317, s32[1024,1]{1,0:T(8,128)S(1)} %copy.40.docs_col_ref), custom_call_target="tpu_custom_call" | custom-call | flops 10737418240 | bytes 8388608 | tf_op jit(solution)/shard_map/attend_back/pallas_call | solution.py:124
  708.4 15.2 %collective-permute-done.81 = bf16[256,2048]{1,0:T(8,128)(2,1)S(1)} collective-permute-done((bf16[256,2048]{1,0:T(8,128)(2,1)S(1)}, bf16[256,2048]{1,0:T(8,128)(2,1)S(1)}, u32[]{:S(2)}, u32[]{:S(2)}) %collective-permute-start.81) | collective-permute-done | bytes 1048608 | tf_op jit(solution)/shard_map/ppermute | solution.py:170
  728.9 10.2 multiply_convert_fusion.1
  767.5 10.9 multiply_convert_fusion
  789.8 14.0 %collective-permute-done.88 = bf16[1024,512]{1,0:T(8,128)(2,1)S(1)} collective-permute-done((bf16[1024,512]{1,0:T(8,128)(2,1)}, bf16[1024,512]{1,0:T(8,128)(2,1)S(1)}, u32[]{:S(2)}, u32[]{:S(2)}) %collective-permute-start.88) | collective-permute-done | bytes 1048608 | tf_op jit(solution)/shard_map/ppermute | solution.py:170
  818.9 9.4 collective-permute-done.90
  839.9 12.1 %collective-permute-done.91 = bf16[1024,512]{1,0:T(8,128)(2,1)} collective-permute-done((bf16[1024,512]{1,0:T(8,128)(2,1)}, bf16[1024,512]{1,0:T(8,128)(2,1)}, u32[]{:S(2)}, u32[]{:S(2)}) %collective-permute-start.91) | collective-permute-done | bytes 1048608 | tf_op jit(solution)/shard_map/ppermute | solution.py:170
  882.0 16.4 %collective-permute-done.96 = bf16[1024,512]{1,0:T(8,128)(2,1)} collective-permute-done((bf16[1024,512]{1,0:T(8,128)(2,1)}, bf16[1024,512]{1,0:T(8,128)(2,1)}, u32[]{:S(2)}, u32[]{:S(2)}) %collective-permute-start.96) | collective-permute-done | bytes 1048608 | tf_op jit(solution)/shard_map/ppermute | solution.py:170
  923.0 14.1 %attend_back.3 = bf16[1024,1536]{1,0:T(8,128)(2,1)S(1)} custom-call(bf16[1024,1536]{1,0:T(8,128)(2,1)} %copy-done.6, bf16[1024,512]{1,0:T(8,128)(2,1)S(1)} %constant_dynamic-update-slice_fusion.42.grad_ref, f32[4,1,1024]{2,1,0:T(1,128)S(1)} %get-tuple-element.710.log_ref, s32[1,1024]{1,0:T(1,128)S(1)} %bitcast.318, s32[1024,1]{1,0:T(8,128)S(1)} %copy.40.docs_col_ref), custom_call_target="tpu_custom_call" | custom-call | flops 10737418240 | bytes 8388608 | tf_op jit(solution)/shard_map/attend_back/pallas_call | solution.py:124
  971.2 16.1 %collective-permute-done.102 = bf16[512,1024]{1,0:T(8,128)(2,1)S(1)} collective-permute-done((bf16[512,1024]{1,0:T(8,128)(2,1)S(1)}, bf16[512,1024]{1,0:T(8,128)(2,1)S(1)}, u32[]{:S(2)}, u32[]{:S(2)}) %collective-permute-start.102) | collective-permute-done | bytes 1048608 | tf_op jit(solution)/shard_map/ppermute | solution.py:173
  1001.1 24.1 %collective-permute-done.106 = bf16[512,1024]{1,0:T(8,128)(2,1)S(1)} collective-permute-done((bf16[512,1024]{1,0:T(8,128)(2,1)S(1)}, bf16[512,1024]{1,0:T(8,128)(2,1)S(1)}, u32[]{:S(2)}, u32[]{:S(2)}) %collective-permute-start.106) | collective-permute-done | bytes 1048608 | tf_op jit(solution)/shard_map/ppermute | solution.py:173
  1092.1 13.0 %collective-permute-done.120 = bf16[512,1024]{1,0:T(8,128)(2,1)} collective-permute-done((bf16[512,1024]{1,0:T(8,128)(2,1)}, bf16[512,1024]{1,0:T(8,128)(2,1)}, u32[]{:S(2)}, u32[]{:S(2)}) %collective-permute-start.120) | collective-permute-done | bytes 1048608 | tf_op jit(solution)/shard_map/ppermute | solution.py:173
  1126.8 9.4 collective-permute-done.122
  (1018 shorter events, 724.2 us)
Async XLA Ops:
  37.3 32.6 %collective-permute-start.16 = (bf16[512,1024]{1,0:T(8,128)(2,1)}, bf16[512,1024]{1,0:T(8,128)(2,1)}, u32[]{:S(2)}, u32[]{:S(2)}) collective-permute-start(bf16[512,1024]{1,0:T(8,128)(2,1)} %param.30), channel_id=1, source_target_pairs={{0,2},{1,3},{2,0},{3,1},{4,6},{5,7},{6,4},{7,5},{8,10},{9,11},{10,... | collective-permute-start | bytes 3145736 | tf_op jit(solution)/shard_map/ppermute | solution.py:170
  43.5 34.8 %collective-permute-start.5 = (bf16[256,2048]{1,0:T(8,128)(2,1)}, bf16[256,2048]{1,0:T(8,128)(2,1)}, u32[]{:S(2)}, u32[]{:S(2)}) collective-permute-start(bf16[256,2048]{1,0:T(8,128)(2,1)} %get-tuple-element.674), channel_id=1, source_target_pairs={{0,1},{1,0},{2,3},{3,2},{4,5},{5,4},{6,7},{7,6},{8,9},{9,8},{10,11... | collective-permute-start | bytes 3145736 | tf_op jit(solution)/shard_map/ppermute | solution.py:170
  70.0 28.2 %collective-permute-start.17 = (bf16[256,2048]{1,0:T(8,128)(2,1)}, bf16[256,2048]{1,0:T(8,128)(2,1)}, u32[]{:S(2)}, u32[]{:S(2)}) collective-permute-start(bf16[256,2048]{1,0:T(8,128)(2,1)} %get-tuple-element.674), channel_id=1, source_target_pairs={{0,2},{1,3},{2,0},{3,1},{4,6},{5,7},{6,4},{7,5},{8,10},{9,11},{10,... | collective-permute-start | bytes 3145736 | tf_op jit(solution)/shard_map/ppermute | solution.py:170
  73.6 25.5 %collective-permute-start.14 = (bf16[512,768]{1,0:T(8,128)(2,1)}, bf16[512,768]{1,0:T(8,128)(2,1)S(1)}, u32[]{:S(2)}, u32[]{:S(2)}) collective-permute-start(bf16[512,768]{1,0:T(8,128)(2,1)} %copy-done.122), channel_id=1, source_target_pairs={{0,4},{1,5},{2,6},{3,7},{4,0},{5,1},{6,2},{7,3},{8,12},{9,13},{10,... | collective-permute-start | bytes 2359304 | tf_op jit(solution)/shard_map/ppermute | solution.py:170
  98.2 25.8 %collective-permute-start.23 = (bf16[512,1024]{1,0:T(8,128)(2,1)}, bf16[512,1024]{1,0:T(8,128)(2,1)}, u32[]{:S(2)}, u32[]{:S(2)}) collective-permute-start(bf16[512,1024]{1,0:T(8,128)(2,1)} %param.30), channel_id=1, source_target_pairs={{0,8},{8,16},{16,24},{24,0},{1,9},{9,17},{17,25},{25,1},{2,10},{10... | collective-permute-start | bytes 3145736 | tf_op jit(solution)/shard_map/ppermute | solution.py:173
  124.0 26.7 %collective-permute-start.25 = (bf16[512,1024]{1,0:T(8,128)(2,1)}, bf16[512,1024]{1,0:T(8,128)(2,1)S(1)}, u32[]{:S(2)}, u32[]{:S(2)}) collective-permute-start(bf16[512,1024]{1,0:T(8,128)(2,1)} %collective-permute-done.23), channel_id=1, source_target_pairs={{0,8},{8,16},{16,24},{24,0},{1,9},{9,17},{17,25},{25,1},{2,10},{10... | collective-permute-start | bytes 3145736 | tf_op jit(solution)/shard_map/ppermute | solution.py:173
  124.0 39.6 %collective-permute-start.27 = (bf16[512,1024]{1,0:T(8,128)(2,1)}, bf16[512,1024]{1,0:T(8,128)(2,1)S(1)}, u32[]{:S(2)}, u32[]{:S(2)}) collective-permute-start(bf16[512,1024]{1,0:T(8,128)(2,1)} %collective-permute-done.23), channel_id=1, source_target_pairs={{0,2},{1,3},{2,0},{3,1},{4,6},{5,7},{6,4},{7,5},{8,10},{9,11},{10,... | collective-permute-start | bytes 3145736 | tf_op jit(solution)/shard_map/ppermute | solution.py:170
  150.7 25.9 %collective-permute-start.31 = (bf16[512,1024]{1,0:T(8,128)(2,1)S(1)}, bf16[512,1024]{1,0:T(8,128)(2,1)}, u32[]{:S(2)}, u32[]{:S(2)}) collective-permute-start(bf16[512,1024]{1,0:T(8,128)(2,1)S(1)} %collective-permute-done.25), channel_id=1, source_target_pairs={{0,8},{8,16},{16,24},{24,0},{1,9},{9,17},{17,25},{25,1},{2,10},{10... | collective-permute-start | bytes 3145736 | tf_op jit(solution)/shard_map/ppermute | solution.py:173
  177.9 28.4 %collective-permute-start.29 = (bf16[256,2048]{1,0:T(8,128)(2,1)S(1)}, bf16[256,2048]{1,0:T(8,128)(2,1)S(1)}, u32[]{:S(2)}, u32[]{:S(2)}) collective-permute-start(bf16[256,2048]{1,0:T(8,128)(2,1)S(1)} %get-tuple-element.729), channel_id=1, source_target_pairs={{0,1},{1,0},{2,3},{3,2},{4,5},{5,4},{6,7},{7,6},{8,9},{9,8},{10,11... | collective-permute-start | bytes 3145736 | tf_op jit(solution)/shard_map/ppermute | solution.py:170
  178.2 27.2 %collective-permute-start.30 = (bf16[256,2048]{1,0:T(8,128)(2,1)S(1)}, bf16[256,2048]{1,0:T(8,128)(2,1)S(1)}, u32[]{:S(2)}, u32[]{:S(2)}) collective-permute-start(bf16[256,2048]{1,0:T(8,128)(2,1)S(1)} %add_convert_fusion.23), channel_id=1, source_target_pairs={{0,2},{1,3},{2,0},{3,1},{4,6},{5,7},{6,4},{7,5},{8,10},{9,11},{10,... | collective-permute-start | bytes 3145736 | tf_op jit(solution)/shard_map/ppermute | solution.py:170
  205.4 25.7 %collective-permute-start.34 = (bf16[512,1024]{1,0:T(8,128)(2,1)S(1)}, bf16[512,1024]{1,0:T(8,128)(2,1)S(1)}, u32[]{:S(2)}, u32[]{:S(2)}) collective-permute-start(bf16[512,1024]{1,0:T(8,128)(2,1)S(1)} %collective-permute-done.25), channel_id=1, source_target_pairs={{0,2},{1,3},{2,0},{3,1},{4,6},{5,7},{6,4},{7,5},{8,10},{9,11},{10,... | collective-permute-start | bytes 3145736 | tf_op jit(solution)/shard_map/ppermute | solution.py:170
  231.0 26.1 %collective-permute-start.35 = (bf16[512,1024]{1,0:T(8,128)(2,1)}, bf16[512,1024]{1,0:T(8,128)(2,1)}, u32[]{:S(2)}, u32[]{:S(2)}) collective-permute-start(bf16[512,1024]{1,0:T(8,128)(2,1)} %collective-permute-done.31), channel_id=1, source_target_pairs={{0,2},{1,3},{2,0},{3,1},{4,6},{5,7},{6,4},{7,5},{8,10},{9,11},{10,... | collective-permute-start | bytes 3145736 | tf_op jit(solution)/shard_map/ppermute | solution.py:170
  257.2 27.8 %collective-permute-start.45 = (bf16[512,512]{1,0:T(8,128)(2,1)}, bf16[512,512]{1,0:T(8,128)(2,1)S(1)}, u32[]{:S(2)}, u32[]{:S(2)}) collective-permute-start(bf16[512,512]{1,0:T(8,128)(2,1)} %collective-permute-done.42), channel_id=1, source_target_pairs={{0,8},{8,16},{16,24},{24,0},{1,9},{9,17},{17,25},{25,1},{2,10},{10... | collective-permute-start | bytes 1572872 | tf_op jit(solution)/shard_map/ppermute | solution.py:173
  257.2 28.4 %collective-permute-start.41 = (bf16[512,512]{1,0:T(8,128)(2,1)}, bf16[512,512]{1,0:T(8,128)(2,1)S(1)}, u32[]{:S(2)}, u32[]{:S(2)}) collective-permute-start(bf16[512,512]{1,0:T(8,128)(2,1)} %copy-done.132), channel_id=1, source_target_pairs={{0,2},{1,3},{2,0},{3,1},{4,6},{5,7},{6,4},{7,5},{8,10},{9,11},{10,... | collective-permute-start | bytes 1572872 | tf_op jit(solution)/shard_map/ppermute | solution.py:170
  363.5 25.6 %collective-permute-start.55 = (bf16[1024,256]{1,0:T(8,128)(2,1)S(1)}, bf16[1024,256]{1,0:T(8,128)(2,1)S(1)}, u32[]{:S(2)}, u32[]{:S(2)}) collective-permute-start(bf16[1024,256]{1,0:T(8,128)(2,1)S(1)} %bitcast.338), channel_id=1, source_target_pairs={{0,1},{1,0},{2,3},{3,2},{4,5},{5,4},{6,7},{7,6},{8,9},{9,8},{10,11... | collective-permute-start | bytes 1572872 | tf_op jit(solution)/shard_map/ppermute | solution.py:170
  445.7 25.3 %collective-permute-start.62 = (bf16[256,2048]{1,0:T(8,128)(2,1)S(1)}, bf16[256,2048]{1,0:T(8,128)(2,1)S(1)}, u32[]{:S(2)}, u32[]{:S(2)}) collective-permute-start(bf16[256,2048]{1,0:T(8,128)(2,1)S(1)} %get-tuple-element.878), channel_id=1, source_target_pairs={{0,4},{1,5},{2,6},{3,7},{4,0},{5,1},{6,2},{7,3},{8,12},{9,13},{10,... | collective-permute-start | bytes 3145736 | tf_op jit(solution)/shard_map/ppermute | solution.py:170
  527.0 25.6 %collective-permute-start.68 = (bf16[256,2048]{1,0:T(8,128)(2,1)S(1)}, bf16[256,2048]{1,0:T(8,128)(2,1)S(1)}, u32[]{:S(2)}, u32[]{:S(2)}) collective-permute-start(bf16[256,2048]{1,0:T(8,128)(2,1)S(1)} %get-tuple-element.912), channel_id=1, source_target_pairs={{0,4},{1,5},{2,6},{3,7},{4,0},{5,1},{6,2},{7,3},{8,12},{9,13},{10,... | collective-permute-start | bytes 3145736 | tf_op jit(solution)/shard_map/ppermute | solution.py:170
  578.3 29.0 %collective-permute-start.74 = (bf16[256,2048]{1,0:T(8,128)(2,1)S(1)}, bf16[256,2048]{1,0:T(8,128)(2,1)S(1)}, u32[]{:S(2)}, u32[]{:S(2)}) collective-permute-start(bf16[256,2048]{1,0:T(8,128)(2,1)S(1)} %get-tuple-element.936), channel_id=1, source_target_pairs={{0,1},{1,0},{2,3},{3,2},{4,5},{5,4},{6,7},{7,6},{8,9},{9,8},{10,11... | collective-permute-start | bytes 3145736 | tf_op jit(solution)/shard_map/ppermute | solution.py:170
  615.3 29.0 %collective-permute-start.73 = (bf16[2,256,512]{2,1,0:T(8,128)(2,1)S(1)}, bf16[2,256,512]{2,1,0:T(8,128)(2,1)S(1)}, u32[]{:S(2)}, u32[]{:S(2)}) collective-permute-start(bf16[2,256,512]{2,1,0:T(8,128)(2,1)S(1)} %get-tuple-element.935), channel_id=1, source_target_pairs={{0,4},{1,5},{2,6},{3,7},{4,0},{5,1},{6,2},{7,3},{8,12},{9,13},{10,... | collective-permute-start | bytes 1572872 | tf_op jit(solution)/shard_map/ppermute | solution.py:170
  616.8 27.5 %collective-permute-start.76 = (bf16[256,2048]{1,0:T(8,128)(2,1)}, bf16[256,2048]{1,0:T(8,128)(2,1)S(1)}, u32[]{:S(2)}, u32[]{:S(2)}) collective-permute-start(bf16[256,2048]{1,0:T(8,128)(2,1)} %get-tuple-element.965), channel_id=1, source_target_pairs={{0,2},{1,3},{2,0},{3,1},{4,6},{5,7},{6,4},{7,5},{8,10},{9,11},{10,... | collective-permute-start | bytes 3145736 | tf_op jit(solution)/shard_map/ppermute | solution.py:170
  674.1 34.4 %collective-permute-start.80 = (bf16[256,2048]{1,0:T(8,128)(2,1)S(1)}, bf16[256,2048]{1,0:T(8,128)(2,1)S(1)}, u32[]{:S(2)}, u32[]{:S(2)}) collective-permute-start(bf16[256,2048]{1,0:T(8,128)(2,1)S(1)} %get-tuple-element.1006), channel_id=1, source_target_pairs={{0,1},{1,0},{2,3},{3,2},{4,5},{5,4},{6,7},{7,6},{8,9},{9,8},{10,11... | collective-permute-start | bytes 3145736 | tf_op jit(solution)/shard_map/ppermute | solution.py:170
  726.0 25.6 %collective-permute-start.84 = (bf16[256,2048]{1,0:T(8,128)(2,1)S(1)}, bf16[256,2048]{1,0:T(8,128)(2,1)S(1)}, u32[]{:S(2)}, u32[]{:S(2)}) collective-permute-start(bf16[256,2048]{1,0:T(8,128)(2,1)S(1)} %get-tuple-element.1056), channel_id=1, source_target_pairs={{0,4},{1,5},{2,6},{3,7},{4,0},{5,1},{6,2},{7,3},{8,12},{9,13},{10,... | collective-permute-start | bytes 3145736 | tf_op jit(solution)/shard_map/ppermute | solution.py:170
  778.4 25.5 %collective-permute-start.88 = (bf16[1024,512]{1,0:T(8,128)(2,1)}, bf16[1024,512]{1,0:T(8,128)(2,1)S(1)}, u32[]{:S(2)}, u32[]{:S(2)}) collective-permute-start(bf16[1024,512]{1,0:T(8,128)(2,1)} %add_convert_fusion.17), channel_id=1, source_target_pairs={{0,2},{1,3},{2,0},{3,1},{4,6},{5,7},{6,4},{7,5},{8,10},{9,11},{10,... | collective-permute-start | bytes 3145736 | tf_op jit(solution)/shard_map/ppermute | solution.py:170
  788.5 41.0 %collective-permute-start.83 = (bf16[256,2048]{1,0:T(8,128)(2,1)S(1)}, bf16[256,2048]{1,0:T(8,128)(2,1)S(1)}, u32[]{:S(2)}, u32[]{:S(2)}) collective-permute-start(bf16[256,2048]{1,0:T(8,128)(2,1)S(1)} %get-tuple-element.1055), channel_id=1, source_target_pairs={{0,1},{1,0},{2,3},{3,2},{4,5},{5,4},{6,7},{7,6},{8,9},{9,8},{10,11... | collective-permute-start | bytes 3145736 | tf_op jit(solution)/shard_map/ppermute | solution.py:170
  839.4 28.1 %collective-permute-start.93 = (bf16[1024,512]{1,0:T(8,128)(2,1)}, bf16[1024,512]{1,0:T(8,128)(2,1)}, u32[]{:S(2)}, u32[]{:S(2)}) collective-permute-start(bf16[1024,512]{1,0:T(8,128)(2,1)} %add_convert_fusion.12), channel_id=1, source_target_pairs={{0,8},{8,16},{16,24},{24,0},{1,9},{9,17},{17,25},{25,1},{2,10},{10... | collective-permute-start | bytes 3145736 | tf_op jit(solution)/shard_map/ppermute | solution.py:173
  880.8 78.9 %collective-permute-start.78 = (bf16[4,256,256]{2,1,0:T(8,128)(2,1)}, bf16[4,256,256]{2,1,0:T(8,128)(2,1)}, u32[]{:S(2)}, u32[]{:S(2)}) collective-permute-start(bf16[4,256,256]{2,1,0:T(8,128)(2,1)} %get-tuple-element.1457), channel_id=1, source_target_pairs={{0,1},{1,0},{2,3},{3,2},{4,5},{5,4},{6,7},{7,6},{8,9},{9,8},{10,11... | collective-permute-start | bytes 1572872 | tf_op jit(solution)/shard_map/ppermute | solution.py:170
  881.4 29.2 %collective-permute-start.100 = (f32[6,1024]{1,0:T(8,128)S(1)}, f32[6,1024]{1,0:T(8,128)S(1)}, u32[]{:S(2)}, u32[]{:S(2)}) collective-permute-start(f32[6,1024]{1,0:T(8,128)S(1)} %constant_dynamic-slice_fusion.6), channel_id=1, source_target_pairs={{0,4},{1,5},{2,6},{3,7},{4,0},{5,1},{6,2},{7,3},{8,12},{9,13},{10,... | collective-permute-start | bytes 73736 | tf_op jit(solution)/shard_map/ppermute | solution.py:170
  882.0 29.1 %collective-permute-start.95 = (bf16[1024,512]{1,0:T(8,128)(2,1)}, bf16[1024,512]{1,0:T(8,128)(2,1)S(1)}, u32[]{:S(2)}, u32[]{:S(2)}) collective-permute-start(bf16[1024,512]{1,0:T(8,128)(2,1)} %add_convert_fusion.7), channel_id=1, source_target_pairs={{0,8},{8,16},{16,24},{24,0},{1,9},{9,17},{17,25},{25,1},{2,10},{10... | collective-permute-start | bytes 3145736 | tf_op jit(solution)/shard_map/ppermute | solution.py:173
  910.6 26.6 %collective-permute-start.101 = (bf16[1024,512]{1,0:T(8,128)(2,1)}, bf16[1024,512]{1,0:T(8,128)(2,1)}, u32[]{:S(2)}, u32[]{:S(2)}) collective-permute-start(bf16[1024,512]{1,0:T(8,128)(2,1)} %pad_maximum_fusion.49), channel_id=1, source_target_pairs={{0,4},{1,5},{2,6},{3,7},{4,0},{5,1},{6,2},{7,3},{8,12},{9,13},{10,... | collective-permute-start | bytes 3145736 | tf_op jit(solution)/shard_map/ppermute | solution.py:170
  960.9 26.4 %collective-permute-start.102 = (bf16[512,1024]{1,0:T(8,128)(2,1)S(1)}, bf16[512,1024]{1,0:T(8,128)(2,1)S(1)}, u32[]{:S(2)}, u32[]{:S(2)}) collective-permute-start(bf16[512,1024]{1,0:T(8,128)(2,1)S(1)} %copy-done.115), channel_id=1, source_target_pairs={{0,8},{8,16},{16,24},{24,0},{1,9},{9,17},{17,25},{25,1},{2,10},{10... | collective-permute-start | bytes 3145736 | tf_op jit(solution)/shard_map/ppermute | solution.py:173
  998.7 26.6 %collective-permute-start.106 = (bf16[512,1024]{1,0:T(8,128)(2,1)S(1)}, bf16[512,1024]{1,0:T(8,128)(2,1)S(1)}, u32[]{:S(2)}, u32[]{:S(2)}) collective-permute-start(bf16[512,1024]{1,0:T(8,128)(2,1)S(1)} %add_convert_fusion.3), channel_id=1, source_target_pairs={{0,8},{8,16},{16,24},{24,0},{1,9},{9,17},{17,25},{25,1},{2,10},{10... | collective-permute-start | bytes 3145736 | tf_op jit(solution)/shard_map/ppermute | solution.py:173
  1000.0 25.8 %collective-permute-start.110 = (bf16[512,768]{1,0:T(8,128)(2,1)S(1)}, bf16[512,768]{1,0:T(8,128)(2,1)S(1)}, u32[]{:S(2)}, u32[]{:S(2)}) collective-permute-start(bf16[512,768]{1,0:T(8,128)(2,1)S(1)} %copy-done.167), channel_id=1, source_target_pairs={{0,4},{1,5},{2,6},{3,7},{4,0},{5,1},{6,2},{7,3},{8,12},{9,13},{10,... | collective-permute-start | bytes 2359304 | tf_op jit(solution)/shard_map/ppermute | solution.py:170
  (282 other events, 3150.5 us)

commit v4 on v3

--- a/solution.py
+++ b/solution.py
@@ -252,11 +252,11 @@
         mine, sent = self.parts(sums, mask)
         return mine + self.on(lane, sent, mask)
 
-    def row_sum(self, value, lane):
+    def row_sum(self, value):
         mask = 1
         while mask < self.rows:
             pairs = [(i, i ^ mask) for i in range(self.rows)]
-            value = value + lane.send(lambda item: lax.ppermute(item, "row", pairs), value)
+            value = value + lax.ppermute(value, "row", pairs)
             mask *= 2
         return value
 
@@ -658,19 +658,22 @@
         steps_of(queue.pop(0))
     puts(2, 1, "down0")
     puts(2, 0, "down1", "more")
+    first_pieces = run(blocks, own_first, other_first)
     for step in range(3, rows):
         ring.arrived(step, "down1")
         if queue:
             steps_of(queue.pop(0))
         puts(step, 1, "down0")
         puts(step, 0, "down1")
+        if step == 3:
+            active_sides = run(
+                lambda *items: columns(items, hidden_span), active_own, active_other
+            )
         ring.arrived(step, "more")
         if queue:
             steps_of(queue.pop(0))
         if step < rows - 1:
             puts(step, 0, "more")
-    first_pieces = run(blocks, own_first, other_first)
-    active_sides = run(lambda *items: columns(items, hidden_span), active_own, active_other)
     if rows > 3:
         puts(rows - 1, 0, "more")
     w_down = ring.wholes["down"]
@@ -918,12 +921,11 @@
             sent = across_b.sum_far(terms_other, both.other_first)
             both.send()
         else:
-            sent = across_b.sum_far(terms_other)
-            for mask in place.rest[::-1]:
-                output = run(
-                    lambda *items: place.features_merge(*items, mask, 1),
-                    *place.features_send(output, mask, None),
-                )
+            terms_own = []
+            sent = across_b.sum_far(
+                terms_other, lambda: terms_own.append(run(product_t, dqkv[:half], w_qkv))
+            )
+            own_sums = across_b.halved(terms_own[0])
         if not last:
             both = Share(
                 "qkv",
@@ -934,13 +936,14 @@
             )
         if last:
             both.other()
+            clock.wait(both.got[0], sent)
             both.send()
-            clock.wait(sent)
             up.send()
             up.advance()
-        terms_own = run(product_t, dqkv[:half], w_qkv)
-        own_sums = across_b.halved(terms_own)
-        if not last:
+        if last:
+            terms_own = run(product_t, dqkv[:half], w_qkv)
+            own_sums = across_b.halved(terms_own)
+        else:
             out.keep()
             both.keep()
         grads = (dr1, *own_sums, sent)
@@ -963,6 +966,11 @@
             *place.features_send(grad, mask, None),
         )
     grad_tokens = grad.reshape(-1, span).astype(f32)
+    for mask in place.rest[::-1]:
+        output = run(
+            lambda *items: place.features_merge(*items, mask, 1),
+            *place.features_send(output, mask, None),
+        )
     output = output.reshape(-1, span)
     qkv_total = sum(qkv_sums)
     qkv_total = qkv_total[: 3 * span] + lane_a.send(
@@ -982,7 +990,7 @@
         if up.step < rows:
             up.advance()
     sums = place.row_sum(
-        jnp.concatenate([token_sums.reshape(-1), qkv_total, hidden_total]), row_lane
+        jnp.concatenate([token_sums.reshape(-1), qkv_total, hidden_total])
     )
     while up.step < rows:
         up.advance()

time: 1160 us -> 1140 us (0.983)
  waiting for transfers between devices: 466 us -> 446 us
    ppermute x30, waiting for transfers between devices: 191 us -> 159 us  [shift(): lax.ppermute(value, 'row', [(i, (i + 1) % self.rows) for i in range(self....]
    ppermute x2, waiting for transfers between devices: 4.54 us -> 20.7 us  [row_sum(): value = value + lax.ppermute(value, 'row', pairs)]
    unnamed x393 -> x395, local copies, waits for them, and re-layouts: 33.5 us -> 31.7 us
  transfers between devices with their start and end apart: 129 -> 129, of which waited for: 76 -> 74; matrix products, arithmetic and copies ran while one was open for 36% -> 37% of each run, Pallas kernels for 3% -> 3%
where the time goes in v4:
time: 1140 us; the launch traced here: 1130 us
  waiting for transfers between devices  446 us (39%)
  matrix products  323 us (28%)
  local copies, waits for them, and re-layouts  125 us (11%)
  other arithmetic  92.5 us (8%)
  starting transfers between devices  89 us (8%)
  Pallas kernels  53.8 us (5%)
    ppermute x97, waiting for transfers between devices, swap(): return lax.ppermute(value, 'col', [(i, i ^ mask) for i in range(self.cols)])  266 us
    ppermute x30, waiting for transfers between devices, shift(): lax.ppermute(value, 'row', [(i, (i + 1) % self.rows) for i in range(self....  159 us
    dot_general x64, matrix products, dot_g(): lax.dot_general(left, right, (((0,), (0,)), ((), ())), preferred_element_...  113 us
    dot_general x16, matrix products, dot_t(): lax.dot_general(left, right, (((1,), (1,)), ((), ())), preferred_element_...  113 us
    dot_general x16, matrix products, dot(): lax.dot_general(left, right, (((1,), (0,)), ((), ())), preferred_element_...  97.5 us
    ppermute x97, starting transfers between devices, swap(): return lax.ppermute(value, 'col', [(i, i ^ mask) for i in range(self.cols)])  74.2 us
    dynamic_update_slice x40, local copies, waits for them, and re-layouts, put(): lax.dynamic_update_slice(total, item, start)  49.2 us
    unnamed x395, local copies, waits for them, and re-layouts  31.7 us
  transfers between devices with their start and end apart: 129, of which 74 were waited for; matrix products, arithmetic and copies ran while one was open for 37% of the time, Pallas kernels for 3%

profile of v4, /device:TPU:0, one launch (start us, length us, event | category | flops | bytes accessed | tf_op | source)
XLA Modules:
  0.0 1134.2 jit_solution(2900939960041026970)
XLA Ops:
  56.9 13.0 %collective-permute-done.13 = bf16[512,768]{1,0:T(8,128)(2,1)} collective-permute-done((bf16[512,768]{1,0:T(8,128)(2,1)S(1)}, bf16[512,768]{1,0:T(8,128)(2,1)}, u32[]{:S(2)}, u32[]{:S(2)}) %collective-permute-start.13) | collective-permute-done | bytes 786464 | tf_op jit(solution)/shard_map/ppermute | solution.py:173
  110.6 12.9 %collective-permute-done.15 = bf16[512,768]{1,0:T(8,128)(2,1)} collective-permute-done((bf16[512,768]{1,0:T(8,128)(2,1)}, bf16[512,768]{1,0:T(8,128)(2,1)}, u32[]{:S(2)}, u32[]{:S(2)}) %collective-permute-start.15) | collective-permute-done | bytes 786464 | tf_op jit(solution)/shard_map/ppermute | solution.py:170
  151.0 12.6 %attend.2 = (bf16[1024,512]{1,0:T(8,128)(2,1)S(1)}, f32[4,1,1024]{2,1,0:T(1,128)S(1)}) custom-call(bf16[1024,1536]{1,0:T(8,128)(2,1)S(1)} %constant_dynamic-update-slice_fusion.8.qkv_ref, s32[1,1024]{1,0:T(1,128)S(1)} %bitcast.315, s32[1024,1]{1,0:T(8,128)S(1)} %copy.40.docs_col_ref), custom_call_target="tpu_custom_call" | custom-call | flops 4294967296 | bytes 4194304 | tf_op jit(solution)/shard_map/attend/pallas_call | solution.py:65
  180.4 10.8 collective-permute-done.32
  209.4 8.8 collective-permute-done.39
  219.8 11.1 collective-permute-done.40
  243.1 14.1 %collective-permute-done.43 = bf16[512,512]{1,0:T(8,128)(2,1)S(1)} collective-permute-done((bf16[512,512]{1,0:T(8,128)(2,1)}, bf16[512,512]{1,0:T(8,128)(2,1)S(1)}, u32[]{:S(2)}, u32[]{:S(2)}) %collective-permute-start.43) | collective-permute-done | bytes 524320 | tf_op jit(solution)/shard_map/ppermute | solution.py:173
  264.2 10.4 fusion.7
  274.6 10.4 fusion.15
  338.8 15.4 %collective-permute-done.51 = bf16[256,2048]{1,0:T(8,128)(2,1)S(1)} collective-permute-done((bf16[256,2048]{1,0:T(8,128)(2,1)S(1)}, bf16[256,2048]{1,0:T(8,128)(2,1)S(1)}, u32[]{:S(2)}, u32[]{:S(2)}) %collective-permute-start.51) | collective-permute-done | bytes 1048608 | tf_op jit(solution)/shard_map/ppermute | solution.py:170
  363.7 19.2 %collective-permute-done.53 = bf16[256,2048]{1,0:T(8,128)(2,1)S(1)} collective-permute-done((bf16[256,2048]{1,0:T(8,128)(2,1)S(1)}, bf16[256,2048]{1,0:T(8,128)(2,1)S(1)}, u32[]{:S(2)}, u32[]{:S(2)}) %collective-permute-start.53) | collective-permute-done | bytes 1048608 | tf_op jit(solution)/shard_map/ppermute | solution.py:170
  389.4 12.8 %attend.3 = (bf16[1024,512]{1,0:T(8,128)(2,1)S(1)}, f32[4,1,1024]{2,1,0:T(1,128)S(1)}) custom-call(bf16[1024,1536]{1,0:T(8,128)(2,1)S(1)} %constant_dynamic-update-slice_fusion.18.qkv_ref, s32[1,1024]{1,0:T(1,128)S(1)} %bitcast.316, s32[1024,1]{1,0:T(8,128)S(1)} %copy.40.docs_col_ref), custom_call_target="tpu_custom_call" | custom-call | flops 4294967296 | bytes 4194304 | tf_op jit(solution)/shard_map/attend/pallas_call | solution.py:65
  415.6 19.8 %collective-permute-done.59 = bf16[256,2048]{1,0:T(8,128)(2,1)S(1)} collective-permute-done((bf16[256,2048]{1,0:T(8,128)(2,1)S(1)}, bf16[256,2048]{1,0:T(8,128)(2,1)S(1)}, u32[]{:S(2)}, u32[]{:S(2)}) %collective-permute-start.59) | collective-permute-done | bytes 1048608 | tf_op jit(solution)/shard_map/ppermute | solution.py:170
  467.3 10.4 fusion.31
  499.2 15.9 %collective-permute-done.66 = bf16[256,2048]{1,0:T(8,128)(2,1)S(1)} collective-permute-done((bf16[256,2048]{1,0:T(8,128)(2,1)S(1)}, bf16[256,2048]{1,0:T(8,128)(2,1)S(1)}, u32[]{:S(2)}, u32[]{:S(2)}) %collective-permute-start.66) | collective-permute-done | bytes 1048608 | tf_op jit(solution)/shard_map/ppermute | solution.py:170
  523.4 10.9 multiply_convert_fusion.3
  534.3 10.1 convolution_convert_fusion.7
  550.2 10.7 multiply_convert_fusion.2
  561.0 8.8 convolution_convert_fusion.6
  644.9 14.4 %attend_back.2 = bf16[1024,1536]{1,0:T(8,128)(2,1)S(1)} custom-call(bf16[1024,1536]{1,0:T(8,128)(2,1)} %copy-done.7, bf16[1024,512]{1,0:T(8,128)(2,1)S(1)} %constant_dynamic-update-slice_fusion.32.grad_ref, f32[4,1,1024]{2,1,0:T(1,128)S(1)} %get-tuple-element.843.log_ref, s32[1,1024]{1,0:T(1,128)S(1)} %bitcast.317, s32[1024,1]{1,0:T(8,128)S(1)} %copy.40.docs_col_ref), custom_call_target="tpu_custom_call" | custom-call | flops 10737418240 | bytes 8388608 | tf_op jit(solution)/shard_map/attend_back/pallas_call | solution.py:124
  707.1 10.2 multiply_convert_fusion.1
  745.7 10.9 multiply_convert_fusion
  768.3 13.8 %collective-permute-done.88 = bf16[1024,512]{1,0:T(8,128)(2,1)S(1)} collective-permute-done((bf16[1024,512]{1,0:T(8,128)(2,1)}, bf16[1024,512]{1,0:T(8,128)(2,1)S(1)}, u32[]{:S(2)}, u32[]{:S(2)}) %collective-permute-start.88) | collective-permute-done | bytes 1048608 | tf_op jit(solution)/shard_map/ppermute | solution.py:170
  797.3 9.1 collective-permute-done.90
  818.7 11.5 %collective-permute-done.91 = bf16[1024,512]{1,0:T(8,128)(2,1)} collective-permute-done((bf16[1024,512]{1,0:T(8,128)(2,1)}, bf16[1024,512]{1,0:T(8,128)(2,1)}, u32[]{:S(2)}, u32[]{:S(2)}) %collective-permute-start.91) | collective-permute-done | bytes 1048608 | tf_op jit(solution)/shard_map/ppermute | solution.py:170
  860.9 15.5 %collective-permute-done.96 = bf16[1024,512]{1,0:T(8,128)(2,1)} collective-permute-done((bf16[1024,512]{1,0:T(8,128)(2,1)}, bf16[1024,512]{1,0:T(8,128)(2,1)}, u32[]{:S(2)}, u32[]{:S(2)}) %collective-permute-start.96) | collective-permute-done | bytes 1048608 | tf_op jit(solution)/shard_map/ppermute | solution.py:170
  901.5 14.1 %attend_back.3 = bf16[1024,1536]{1,0:T(8,128)(2,1)S(1)} custom-call(bf16[1024,1536]{1,0:T(8,128)(2,1)} %copy-done.6, bf16[1024,512]{1,0:T(8,128)(2,1)S(1)} %constant_dynamic-update-slice_fusion.42.grad_ref, f32[4,1,1024]{2,1,0:T(1,128)S(1)} %get-tuple-element.708.log_ref, s32[1,1024]{1,0:T(1,128)S(1)} %bitcast.318, s32[1024,1]{1,0:T(8,128)S(1)} %copy.40.docs_col_ref), custom_call_target="tpu_custom_call" | custom-call | flops 10737418240 | bytes 8388608 | tf_op jit(solution)/shard_map/attend_back/pallas_call | solution.py:124
  949.3 10.8 collective-permute-done.104
  978.7 24.4 %collective-permute-done.107 = bf16[512,1024]{1,0:T(8,128)(2,1)S(1)} collective-permute-done((bf16[512,1024]{1,0:T(8,128)(2,1)S(1)}, bf16[512,1024]{1,0:T(8,128)(2,1)S(1)}, u32[]{:S(2)}, u32[]{:S(2)}) %collective-permute-start.107) | collective-permute-done | bytes 1048608 | tf_op jit(solution)/shard_map/ppermute | solution.py:173
  1073.3 11.5 %collective-permute-done.119 = bf16[512,768]{1,0:T(8,128)(2,1)S(1)} collective-permute-done((bf16[512,768]{1,0:T(8,128)(2,1)}, bf16[512,768]{1,0:T(8,128)(2,1)S(1)}, u32[]{:S(2)}, u32[]{:S(2)}) %collective-permute-start.119) | collective-permute-done | bytes 786464 | tf_op jit(solution)/shard_map/ppermute | solution.py:170
  1099.1 13.9 %collective-permute-done.128 = f32[3328]{0:T(1024)S(1)} collective-permute-done((f32[3328]{0:T(1024)S(1)}, f32[3328]{0:T(1024)S(1)}, u32[]{:S(2)}, u32[]{:S(2)}) %collective-permute-start.128) | collective-permute-done | bytes 13344 | tf_op jit(solution)/shard_map/ppermute | solution.py:259
  1122.5 8.6 collective-permute-done.122
  (1020 shorter events, 722.5 us)
Async XLA Ops:
  37.3 32.6 %collective-permute-start.16 = (bf16[512,1024]{1,0:T(8,128)(2,1)}, bf16[512,1024]{1,0:T(8,128)(2,1)}, u32[]{:S(2)}, u32[]{:S(2)}) collective-permute-start(bf16[512,1024]{1,0:T(8,128)(2,1)} %param.30), channel_id=1, source_target_pairs={{0,2},{1,3},{2,0},{3,1},{4,6},{5,7},{6,4},{7,5},{8,10},{9,11},{10,... | collective-permute-start | bytes 3145736 | tf_op jit(solution)/shard_map/ppermute | solution.py:170
  43.5 34.8 %collective-permute-start.5 = (bf16[256,2048]{1,0:T(8,128)(2,1)}, bf16[256,2048]{1,0:T(8,128)(2,1)}, u32[]{:S(2)}, u32[]{:S(2)}) collective-permute-start(bf16[256,2048]{1,0:T(8,128)(2,1)} %get-tuple-element.672), channel_id=1, source_target_pairs={{0,1},{1,0},{2,3},{3,2},{4,5},{5,4},{6,7},{7,6},{8,9},{9,8},{10,11... | collective-permute-start | bytes 3145736 | tf_op jit(solution)/shard_map/ppermute | solution.py:170
  70.0 28.2 %collective-permute-start.17 = (bf16[256,2048]{1,0:T(8,128)(2,1)}, bf16[256,2048]{1,0:T(8,128)(2,1)}, u32[]{:S(2)}, u32[]{:S(2)}) collective-permute-start(bf16[256,2048]{1,0:T(8,128)(2,1)} %get-tuple-element.672), channel_id=1, source_target_pairs={{0,2},{1,3},{2,0},{3,1},{4,6},{5,7},{6,4},{7,5},{8,10},{9,11},{10,... | collective-permute-start | bytes 3145736 | tf_op jit(solution)/shard_map/ppermute | solution.py:170
  98.2 25.9 %collective-permute-start.23 = (bf16[512,1024]{1,0:T(8,128)(2,1)}, bf16[512,1024]{1,0:T(8,128)(2,1)}, u32[]{:S(2)}, u32[]{:S(2)}) collective-permute-start(bf16[512,1024]{1,0:T(8,128)(2,1)} %param.30), channel_id=1, source_target_pairs={{0,8},{8,16},{16,24},{24,0},{1,9},{9,17},{17,25},{25,1},{2,10},{10... | collective-permute-start | bytes 3145736 | tf_op jit(solution)/shard_map/ppermute | solution.py:173
  124.1 26.7 %collective-permute-start.25 = (bf16[512,1024]{1,0:T(8,128)(2,1)}, bf16[512,1024]{1,0:T(8,128)(2,1)S(1)}, u32[]{:S(2)}, u32[]{:S(2)}) collective-permute-start(bf16[512,1024]{1,0:T(8,128)(2,1)} %collective-permute-done.23), channel_id=1, source_target_pairs={{0,8},{8,16},{16,24},{24,0},{1,9},{9,17},{17,25},{25,1},{2,10},{10... | collective-permute-start | bytes 3145736 | tf_op jit(solution)/shard_map/ppermute | solution.py:173
  124.1 39.6 %collective-permute-start.27 = (bf16[512,1024]{1,0:T(8,128)(2,1)}, bf16[512,1024]{1,0:T(8,128)(2,1)S(1)}, u32[]{:S(2)}, u32[]{:S(2)}) collective-permute-start(bf16[512,1024]{1,0:T(8,128)(2,1)} %collective-permute-done.23), channel_id=1, source_target_pairs={{0,2},{1,3},{2,0},{3,1},{4,6},{5,7},{6,4},{7,5},{8,10},{9,11},{10,... | collective-permute-start | bytes 3145736 | tf_op jit(solution)/shard_map/ppermute | solution.py:170
  150.8 25.9 %collective-permute-start.31 = (bf16[512,1024]{1,0:T(8,128)(2,1)S(1)}, bf16[512,1024]{1,0:T(8,128)(2,1)}, u32[]{:S(2)}, u32[]{:S(2)}) collective-permute-start(bf16[512,1024]{1,0:T(8,128)(2,1)S(1)} %collective-permute-done.25), channel_id=1, source_target_pairs={{0,8},{8,16},{16,24},{24,0},{1,9},{9,17},{17,25},{25,1},{2,10},{10... | collective-permute-start | bytes 3145736 | tf_op jit(solution)/shard_map/ppermute | solution.py:173
  178.0 28.4 %collective-permute-start.29 = (bf16[256,2048]{1,0:T(8,128)(2,1)S(1)}, bf16[256,2048]{1,0:T(8,128)(2,1)S(1)}, u32[]{:S(2)}, u32[]{:S(2)}) collective-permute-start(bf16[256,2048]{1,0:T(8,128)(2,1)S(1)} %get-tuple-element.727), channel_id=1, source_target_pairs={{0,1},{1,0},{2,3},{3,2},{4,5},{5,4},{6,7},{7,6},{8,9},{9,8},{10,11... | collective-permute-start | bytes 3145736 | tf_op jit(solution)/shard_map/ppermute | solution.py:170
  178.3 27.2 %collective-permute-start.30 = (bf16[256,2048]{1,0:T(8,128)(2,1)S(1)}, bf16[256,2048]{1,0:T(8,128)(2,1)S(1)}, u32[]{:S(2)}, u32[]{:S(2)}) collective-permute-start(bf16[256,2048]{1,0:T(8,128)(2,1)S(1)} %add_convert_fusion.23), channel_id=1, source_target_pairs={{0,2},{1,3},{2,0},{3,1},{4,6},{5,7},{6,4},{7,5},{8,10},{9,11},{10,... | collective-permute-start | bytes 3145736 | tf_op jit(solution)/shard_map/ppermute | solution.py:170
  205.5 25.8 %collective-permute-start.34 = (bf16[512,1024]{1,0:T(8,128)(2,1)S(1)}, bf16[512,1024]{1,0:T(8,128)(2,1)S(1)}, u32[]{:S(2)}, u32[]{:S(2)}) collective-permute-start(bf16[512,1024]{1,0:T(8,128)(2,1)S(1)} %collective-permute-done.25), channel_id=1, source_target_pairs={{0,2},{1,3},{2,0},{3,1},{4,6},{5,7},{6,4},{7,5},{8,10},{9,11},{10,... | collective-permute-start | bytes 3145736 | tf_op jit(solution)/shard_map/ppermute | solution.py:170
  231.3 26.0 %collective-permute-start.35 = (bf16[512,1024]{1,0:T(8,128)(2,1)}, bf16[512,1024]{1,0:T(8,128)(2,1)}, u32[]{:S(2)}, u32[]{:S(2)}) collective-permute-start(bf16[512,1024]{1,0:T(8,128)(2,1)} %collective-permute-done.31), channel_id=1, source_target_pairs={{0,2},{1,3},{2,0},{3,1},{4,6},{5,7},{6,4},{7,5},{8,10},{9,11},{10,... | collective-permute-start | bytes 3145736 | tf_op jit(solution)/shard_map/ppermute | solution.py:170
  257.3 27.7 %collective-permute-start.45 = (bf16[512,512]{1,0:T(8,128)(2,1)}, bf16[512,512]{1,0:T(8,128)(2,1)S(1)}, u32[]{:S(2)}, u32[]{:S(2)}) collective-permute-start(bf16[512,512]{1,0:T(8,128)(2,1)} %collective-permute-done.42), channel_id=1, source_target_pairs={{0,8},{8,16},{16,24},{24,0},{1,9},{9,17},{17,25},{25,1},{2,10},{10... | collective-permute-start | bytes 1572872 | tf_op jit(solution)/shard_map/ppermute | solution.py:173
  257.3 28.2 %collective-permute-start.41 = (bf16[512,512]{1,0:T(8,128)(2,1)}, bf16[512,512]{1,0:T(8,128)(2,1)S(1)}, u32[]{:S(2)}, u32[]{:S(2)}) collective-permute-start(bf16[512,512]{1,0:T(8,128)(2,1)} %copy-done.136), channel_id=1, source_target_pairs={{0,2},{1,3},{2,0},{3,1},{4,6},{5,7},{6,4},{7,5},{8,10},{9,11},{10,... | collective-permute-start | bytes 1572872 | tf_op jit(solution)/shard_map/ppermute | solution.py:170
  357.3 25.6 %collective-permute-start.55 = (bf16[1024,256]{1,0:T(8,128)(2,1)S(1)}, bf16[1024,256]{1,0:T(8,128)(2,1)S(1)}, u32[]{:S(2)}, u32[]{:S(2)}) collective-permute-start(bf16[1024,256]{1,0:T(8,128)(2,1)S(1)} %bitcast.338), channel_id=1, source_target_pairs={{0,1},{1,0},{2,3},{3,2},{4,5},{5,4},{6,7},{7,6},{8,9},{9,8},{10,11... | collective-permute-start | bytes 1572872 | tf_op jit(solution)/shard_map/ppermute | solution.py:170
  520.5 25.6 %collective-permute-start.68 = (bf16[256,2048]{1,0:T(8,128)(2,1)S(1)}, bf16[256,2048]{1,0:T(8,128)(2,1)S(1)}, u32[]{:S(2)}, u32[]{:S(2)}) collective-permute-start(bf16[256,2048]{1,0:T(8,128)(2,1)S(1)} %get-tuple-element.910), channel_id=1, source_target_pairs={{0,4},{1,5},{2,6},{3,7},{4,0},{5,1},{6,2},{7,3},{8,12},{9,13},{10,... | collective-permute-start | bytes 3145736 | tf_op jit(solution)/shard_map/ppermute | solution.py:170
  571.7 28.9 %collective-permute-start.74 = (bf16[256,2048]{1,0:T(8,128)(2,1)S(1)}, bf16[256,2048]{1,0:T(8,128)(2,1)S(1)}, u32[]{:S(2)}, u32[]{:S(2)}) collective-permute-start(bf16[256,2048]{1,0:T(8,128)(2,1)S(1)} %get-tuple-element.934), channel_id=1, source_target_pairs={{0,1},{1,0},{2,3},{3,2},{4,5},{5,4},{6,7},{7,6},{8,9},{9,8},{10,11... | collective-permute-start | bytes 3145736 | tf_op jit(solution)/shard_map/ppermute | solution.py:170
  608.7 29.5 %collective-permute-start.73 = (bf16[2,256,512]{2,1,0:T(8,128)(2,1)S(1)}, bf16[2,256,512]{2,1,0:T(8,128)(2,1)S(1)}, u32[]{:S(2)}, u32[]{:S(2)}) collective-permute-start(bf16[2,256,512]{2,1,0:T(8,128)(2,1)S(1)} %get-tuple-element.933), channel_id=1, source_target_pairs={{0,4},{1,5},{2,6},{3,7},{4,0},{5,1},{6,2},{7,3},{8,12},{9,13},{10,... | collective-permute-start | bytes 1572872 | tf_op jit(solution)/shard_map/ppermute | solution.py:170
  610.2 28.0 %collective-permute-start.76 = (bf16[256,2048]{1,0:T(8,128)(2,1)}, bf16[256,2048]{1,0:T(8,128)(2,1)S(1)}, u32[]{:S(2)}, u32[]{:S(2)}) collective-permute-start(bf16[256,2048]{1,0:T(8,128)(2,1)} %get-tuple-element.963), channel_id=1, source_target_pairs={{0,2},{1,3},{2,0},{3,1},{4,6},{5,7},{6,4},{7,5},{8,10},{9,11},{10,... | collective-permute-start | bytes 3145736 | tf_op jit(solution)/shard_map/ppermute | solution.py:170
  672.5 29.0 %collective-permute-start.80 = (bf16[256,2048]{1,0:T(8,128)(2,1)S(1)}, bf16[256,2048]{1,0:T(8,128)(2,1)S(1)}, u32[]{:S(2)}, u32[]{:S(2)}) collective-permute-start(bf16[256,2048]{1,0:T(8,128)(2,1)S(1)} %get-tuple-element.1004), channel_id=1, source_target_pairs={{0,1},{1,0},{2,3},{3,2},{4,5},{5,4},{6,7},{7,6},{8,9},{9,8},{10,11... | collective-permute-start | bytes 3145736 | tf_op jit(solution)/shard_map/ppermute | solution.py:170
  672.9 28.5 %collective-permute-start.81 = (bf16[256,2048]{1,0:T(8,128)(2,1)S(1)}, bf16[256,2048]{1,0:T(8,128)(2,1)S(1)}, u32[]{:S(2)}, u32[]{:S(2)}) collective-permute-start(bf16[256,2048]{1,0:T(8,128)(2,1)S(1)} %add_convert_fusion.18), channel_id=1, source_target_pairs={{0,2},{1,3},{2,0},{3,1},{4,6},{5,7},{6,4},{7,5},{8,10},{9,11},{10,... | collective-permute-start | bytes 3145736 | tf_op jit(solution)/shard_map/ppermute | solution.py:170
  704.2 25.6 %collective-permute-start.84 = (bf16[256,2048]{1,0:T(8,128)(2,1)S(1)}, bf16[256,2048]{1,0:T(8,128)(2,1)S(1)}, u32[]{:S(2)}, u32[]{:S(2)}) collective-permute-start(bf16[256,2048]{1,0:T(8,128)(2,1)S(1)} %get-tuple-element.1054), channel_id=1, source_target_pairs={{0,4},{1,5},{2,6},{3,7},{4,0},{5,1},{6,2},{7,3},{8,12},{9,13},{10,... | collective-permute-start | bytes 3145736 | tf_op jit(solution)/shard_map/ppermute | solution.py:170
  756.6 25.5 %collective-permute-start.88 = (bf16[1024,512]{1,0:T(8,128)(2,1)}, bf16[1024,512]{1,0:T(8,128)(2,1)S(1)}, u32[]{:S(2)}, u32[]{:S(2)}) collective-permute-start(bf16[1024,512]{1,0:T(8,128)(2,1)} %add_convert_fusion.17), channel_id=1, source_target_pairs={{0,2},{1,3},{2,0},{3,1},{4,6},{5,7},{6,4},{7,5},{8,10},{9,11},{10,... | collective-permute-start | bytes 3145736 | tf_op jit(solution)/shard_map/ppermute | solution.py:170
  766.9 41.0 %collective-permute-start.83 = (bf16[256,2048]{1,0:T(8,128)(2,1)S(1)}, bf16[256,2048]{1,0:T(8,128)(2,1)S(1)}, u32[]{:S(2)}, u32[]{:S(2)}) collective-permute-start(bf16[256,2048]{1,0:T(8,128)(2,1)S(1)} %get-tuple-element.1053), channel_id=1, source_target_pairs={{0,1},{1,0},{2,3},{3,2},{4,5},{5,4},{6,7},{7,6},{8,9},{9,8},{10,11... | collective-permute-start | bytes 3145736 | tf_op jit(solution)/shard_map/ppermute | solution.py:170
  817.8 28.1 %collective-permute-start.93 = (bf16[1024,512]{1,0:T(8,128)(2,1)}, bf16[1024,512]{1,0:T(8,128)(2,1)}, u32[]{:S(2)}, u32[]{:S(2)}) collective-permute-start(bf16[1024,512]{1,0:T(8,128)(2,1)} %add_convert_fusion.12), channel_id=1, source_target_pairs={{0,8},{8,16},{16,24},{24,0},{1,9},{9,17},{17,25},{25,1},{2,10},{10... | collective-permute-start | bytes 3145736 | tf_op jit(solution)/shard_map/ppermute | solution.py:173
  859.3 78.6 %collective-permute-start.78 = (bf16[4,256,256]{2,1,0:T(8,128)(2,1)}, bf16[4,256,256]{2,1,0:T(8,128)(2,1)}, u32[]{:S(2)}, u32[]{:S(2)}) collective-permute-start(bf16[4,256,256]{2,1,0:T(8,128)(2,1)} %get-tuple-element.1453), channel_id=1, source_target_pairs={{0,1},{1,0},{2,3},{3,2},{4,5},{5,4},{6,7},{7,6},{8,9},{9,8},{10,11... | collective-permute-start | bytes 1572872 | tf_op jit(solution)/shard_map/ppermute | solution.py:170
  859.9 29.2 %collective-permute-start.100 = (f32[6,1024]{1,0:T(8,128)S(1)}, f32[6,1024]{1,0:T(8,128)S(1)}, u32[]{:S(2)}, u32[]{:S(2)}) collective-permute-start(f32[6,1024]{1,0:T(8,128)S(1)} %constant_dynamic-slice_fusion.6), channel_id=1, source_target_pairs={{0,4},{1,5},{2,6},{3,7},{4,0},{5,1},{6,2},{7,3},{8,12},{9,13},{10,... | collective-permute-start | bytes 73736 | tf_op jit(solution)/shard_map/ppermute | solution.py:170
  860.4 29.1 %collective-permute-start.95 = (bf16[1024,512]{1,0:T(8,128)(2,1)}, bf16[1024,512]{1,0:T(8,128)(2,1)S(1)}, u32[]{:S(2)}, u32[]{:S(2)}) collective-permute-start(bf16[1024,512]{1,0:T(8,128)(2,1)} %add_convert_fusion.7), channel_id=1, source_target_pairs={{0,8},{8,16},{16,24},{24,0},{1,9},{9,17},{17,25},{25,1},{2,10},{10... | collective-permute-start | bytes 3145736 | tf_op jit(solution)/shard_map/ppermute | solution.py:173
  889.1 26.6 %collective-permute-start.101 = (bf16[1024,512]{1,0:T(8,128)(2,1)}, bf16[1024,512]{1,0:T(8,128)(2,1)}, u32[]{:S(2)}, u32[]{:S(2)}) collective-permute-start(bf16[1024,512]{1,0:T(8,128)(2,1)} %pad_maximum_fusion.49), channel_id=1, source_target_pairs={{0,4},{1,5},{2,6},{3,7},{4,0},{5,1},{6,2},{7,3},{8,12},{9,13},{10,... | collective-permute-start | bytes 3145736 | tf_op jit(solution)/shard_map/ppermute | solution.py:170
  939.1 26.4 %collective-permute-start.102 = (bf16[512,1024]{1,0:T(8,128)(2,1)S(1)}, bf16[512,1024]{1,0:T(8,128)(2,1)S(1)}, u32[]{:S(2)}, u32[]{:S(2)}) collective-permute-start(bf16[512,1024]{1,0:T(8,128)(2,1)S(1)} %copy-done.115), channel_id=1, source_target_pairs={{0,8},{8,16},{16,24},{24,0},{1,9},{9,17},{17,25},{25,1},{2,10},{10... | collective-permute-start | bytes 3145736 | tf_op jit(solution)/shard_map/ppermute | solution.py:173
  976.5 26.6 %collective-permute-start.107 = (bf16[512,1024]{1,0:T(8,128)(2,1)S(1)}, bf16[512,1024]{1,0:T(8,128)(2,1)S(1)}, u32[]{:S(2)}, u32[]{:S(2)}) collective-permute-start(bf16[512,1024]{1,0:T(8,128)(2,1)S(1)} %add_convert_fusion.3), channel_id=1, source_target_pairs={{0,8},{8,16},{16,24},{24,0},{1,9},{9,17},{17,25},{25,1},{2,10},{10... | collective-permute-start | bytes 3145736 | tf_op jit(solution)/shard_map/ppermute | solution.py:173
  1060.4 28.2 %collective-permute-start.120 = (bf16[512,1024]{1,0:T(8,128)(2,1)}, bf16[512,1024]{1,0:T(8,128)(2,1)}, u32[]{:S(2)}, u32[]{:S(2)}) collective-permute-start(bf16[512,1024]{1,0:T(8,128)(2,1)} %add_convert_fusion.1), channel_id=1, source_target_pairs={{0,8},{8,16},{16,24},{24,0},{1,9},{9,17},{17,25},{25,1},{2,10},{10... | collective-permute-start | bytes 3145736 | tf_op jit(solution)/shard_map/ppermute | solution.py:173
  1088.6 25.6 %collective-permute-start.121 = (bf16[512,768]{1,0:T(8,128)(2,1)S(1)}, bf16[512,768]{1,0:T(8,128)(2,1)S(1)}, u32[]{:S(2)}, u32[]{:S(2)}) collective-permute-start(bf16[512,768]{1,0:T(8,128)(2,1)S(1)} %copy-done.126), channel_id=1, source_target_pairs={{0,8},{8,16},{16,24},{24,0},{1,9},{9,17},{17,25},{25,1},{2,10},{10... | collective-permute-start | bytes 2359304 | tf_op jit(solution)/shard_map/ppermute | solution.py:173
  (283 other events, 3152.0 us)

commit v5 on v4

--- a/solution.py
+++ b/solution.py
@@ -948,16 +948,21 @@
             both.keep()
         grads = (dr1, *own_sums, sent)
     clock.wait(own_sums)
-    for step in range(rows):
-        out.advance()
+    out.advance()
+    clock.wait(up.got[2])
+    up.send(rows - len(up.got))
+    out.advance()
+    both.send()
+    both.advance()
+    out.advance()
     grad = run(lambda *items: plus(*items).astype(bf16)[None], *grads)
     grad = place.features_send(grad, place.a, lane_a)
-    both.send(rows - 2)
-    both.advance()
+    up.advance()
+    while out.step < rows:
+        out.advance()
+    both.send(rows - 3)
     grad = run(lambda *items: place.features_merge(*items, place.a, 0), *grad)
-    up.send(rows - len(up.got))
     grad = place.features_send(grad, place.b, lane_b)
-    up.advance()
     both.advance()
     grad = run(lambda *items: place.features_merge(*items, place.b, 1), *grad)
     for mask in place.rest[::-1]:

time: 1140 us -> 1130 us (level)
  waiting for transfers between devices: 446 us -> 429 us
    ppermute x97, waiting for transfers between devices: 266 us -> 244 us  [swap(): return lax.ppermute(value, 'col', [(i, i ^ mask) for i in range(self.cols)])]
    ppermute x30, waiting for transfers between devices: 159 us -> 177 us  [shift(): lax.ppermute(value, 'row', [(i, (i + 1) % self.rows) for i in range(self....]
    ppermute x2, waiting for transfers between devices: 20.7 us -> 8.37 us  [row_sum(): value = value + lax.ppermute(value, 'row', pairs)]
    unnamed x395 -> x419, local copies, waits for them, and re-layouts: 31.7 us -> 32.9 us
  transfers between devices with their start and end apart: 129 -> 129, of which waited for: 74 -> 72; matrix products, arithmetic and copies ran while one was open for 37% -> 38% of each run, Pallas kernels for 3% -> 4%
where the time goes in v5:
time: 1130 us; the launch traced here: 1120 us
  waiting for transfers between devices  429 us (38%)
  matrix products  324 us (29%)
  local copies, waits for them, and re-layouts  126 us (11%)
  other arithmetic  93.1 us (8%)
  starting transfers between devices  90.9 us (8%)
  Pallas kernels  53.8 us (5%)
    ppermute x97, waiting for transfers between devices, swap(): return lax.ppermute(value, 'col', [(i, i ^ mask) for i in range(self.cols)])  244 us
    ppermute x30, waiting for transfers between devices, shift(): lax.ppermute(value, 'row', [(i, (i + 1) % self.rows) for i in range(self....  177 us
    dot_general x64, matrix products, dot_g(): lax.dot_general(left, right, (((0,), (0,)), ((), ())), preferred_element_...  114 us
    dot_general x16, matrix products, dot_t(): lax.dot_general(left, right, (((1,), (1,)), ((), ())), preferred_element_...  110 us
    dot_general x16, matrix products, dot(): lax.dot_general(left, right, (((1,), (0,)), ((), ())), preferred_element_...  100 us
    ppermute x97, starting transfers between devices, swap(): return lax.ppermute(value, 'col', [(i, i ^ mask) for i in range(self.cols)])  73.3 us
    dynamic_update_slice x40, local copies, waits for them, and re-layouts, put(): lax.dynamic_update_slice(total, item, start)  49.1 us
    unnamed x419, local copies, waits for them, and re-layouts  32.9 us
  transfers between devices with their start and end apart: 129, of which 72 were waited for; matrix products, arithmetic and copies ran while one was open for 38% of the time, Pallas kernels for 4%

profile of v5, /device:TPU:0, one launch (start us, length us, event | category | flops | bytes accessed | tf_op | source)
XLA Modules:
  0.0 1122.5 jit_solution(16230414068432419946)
XLA Ops:
  56.9 13.0 %collective-permute-done.13 = bf16[512,768]{1,0:T(8,128)(2,1)} collective-permute-done((bf16[512,768]{1,0:T(8,128)(2,1)S(1)}, bf16[512,768]{1,0:T(8,128)(2,1)}, u32[]{:S(2)}, u32[]{:S(2)}) %collective-permute-start.13) | collective-permute-done | bytes 786464 | tf_op jit(solution)/shard_map/ppermute | solution.py:173
  110.6 12.9 %collective-permute-done.15 = bf16[512,768]{1,0:T(8,128)(2,1)} collective-permute-done((bf16[512,768]{1,0:T(8,128)(2,1)}, bf16[512,768]{1,0:T(8,128)(2,1)}, u32[]{:S(2)}, u32[]{:S(2)}) %collective-permute-start.15) | collective-permute-done | bytes 786464 | tf_op jit(solution)/shard_map/ppermute | solution.py:170
  151.0 12.6 %attend.2 = (bf16[1024,512]{1,0:T(8,128)(2,1)S(1)}, f32[4,1,1024]{2,1,0:T(1,128)S(1)}) custom-call(bf16[1024,1536]{1,0:T(8,128)(2,1)S(1)} %constant_dynamic-update-slice_fusion.8.qkv_ref, s32[1,1024]{1,0:T(1,128)S(1)} %bitcast.315, s32[1024,1]{1,0:T(8,128)S(1)} %copy.40.docs_col_ref), custom_call_target="tpu_custom_call" | custom-call | flops 4294967296 | bytes 4194304 | tf_op jit(solution)/shard_map/attend/pallas_call | solution.py:65
  180.3 10.9 collective-permute-done.32
  209.4 8.8 collective-permute-done.39
  219.7 11.1 collective-permute-done.40
  243.0 14.2 %collective-permute-done.43 = bf16[512,512]{1,0:T(8,128)(2,1)S(1)} collective-permute-done((bf16[512,512]{1,0:T(8,128)(2,1)}, bf16[512,512]{1,0:T(8,128)(2,1)S(1)}, u32[]{:S(2)}, u32[]{:S(2)}) %collective-permute-start.43) | collective-permute-done | bytes 524320 | tf_op jit(solution)/shard_map/ppermute | solution.py:173
  264.2 10.4 fusion.7
  274.6 10.4 fusion.15
  338.7 15.4 %collective-permute-done.51 = bf16[256,2048]{1,0:T(8,128)(2,1)S(1)} collective-permute-done((bf16[256,2048]{1,0:T(8,128)(2,1)S(1)}, bf16[256,2048]{1,0:T(8,128)(2,1)S(1)}, u32[]{:S(2)}, u32[]{:S(2)}) %collective-permute-start.51) | collective-permute-done | bytes 1048608 | tf_op jit(solution)/shard_map/ppermute | solution.py:170
  363.5 19.3 %collective-permute-done.53 = bf16[256,2048]{1,0:T(8,128)(2,1)S(1)} collective-permute-done((bf16[256,2048]{1,0:T(8,128)(2,1)S(1)}, bf16[256,2048]{1,0:T(8,128)(2,1)S(1)}, u32[]{:S(2)}, u32[]{:S(2)}) %collective-permute-start.53) | collective-permute-done | bytes 1048608 | tf_op jit(solution)/shard_map/ppermute | solution.py:170
  389.3 12.8 %attend.3 = (bf16[1024,512]{1,0:T(8,128)(2,1)S(1)}, f32[4,1,1024]{2,1,0:T(1,128)S(1)}) custom-call(bf16[1024,1536]{1,0:T(8,128)(2,1)S(1)} %constant_dynamic-update-slice_fusion.18.qkv_ref, s32[1,1024]{1,0:T(1,128)S(1)} %bitcast.316, s32[1024,1]{1,0:T(8,128)S(1)} %copy.40.docs_col_ref), custom_call_target="tpu_custom_call" | custom-call | flops 4294967296 | bytes 4194304 | tf_op jit(solution)/shard_map/attend/pallas_call | solution.py:65
  415.4 19.9 %collective-permute-done.59 = bf16[256,2048]{1,0:T(8,128)(2,1)S(1)} collective-permute-done((bf16[256,2048]{1,0:T(8,128)(2,1)S(1)}, bf16[256,2048]{1,0:T(8,128)(2,1)S(1)}, u32[]{:S(2)}, u32[]{:S(2)}) %collective-permute-start.59) | collective-permute-done | bytes 1048608 | tf_op jit(solution)/shard_map/ppermute | solution.py:170
  441.0 10.9 fusion.23
  467.1 10.4 fusion.31
  499.1 15.8 %collective-permute-done.66 = bf16[256,2048]{1,0:T(8,128)(2,1)S(1)} collective-permute-done((bf16[256,2048]{1,0:T(8,128)(2,1)S(1)}, bf16[256,2048]{1,0:T(8,128)(2,1)S(1)}, u32[]{:S(2)}, u32[]{:S(2)}) %collective-permute-start.66) | collective-permute-done | bytes 1048608 | tf_op jit(solution)/shard_map/ppermute | solution.py:170
  523.3 10.9 multiply_convert_fusion.3
  534.2 10.1 convolution_convert_fusion.7
  550.1 10.2 multiply_convert_fusion.2
  560.3 8.8 convolution_convert_fusion.6
  645.0 14.4 %attend_back.2 = bf16[1024,1536]{1,0:T(8,128)(2,1)S(1)} custom-call(bf16[1024,1536]{1,0:T(8,128)(2,1)} %copy-done.7, bf16[1024,512]{1,0:T(8,128)(2,1)S(1)} %constant_dynamic-update-slice_fusion.32.grad_ref, f32[4,1,1024]{2,1,0:T(1,128)S(1)} %get-tuple-element.843.log_ref, s32[1,1024]{1,0:T(1,128)S(1)} %bitcast.317, s32[1024,1]{1,0:T(8,128)S(1)} %copy.40.docs_col_ref), custom_call_target="tpu_custom_call" | custom-call | flops 10737418240 | bytes 8388608 | tf_op jit(solution)/shard_map/attend_back/pallas_call | solution.py:124
  707.1 10.2 multiply_convert_fusion.1
  745.8 10.9 multiply_convert_fusion
  768.4 13.8 %collective-permute-done.88 = bf16[1024,512]{1,0:T(8,128)(2,1)S(1)} collective-permute-done((bf16[1024,512]{1,0:T(8,128)(2,1)}, bf16[1024,512]{1,0:T(8,128)(2,1)S(1)}, u32[]{:S(2)}, u32[]{:S(2)}) %collective-permute-start.88) | collective-permute-done | bytes 1048608 | tf_op jit(solution)/shard_map/ppermute | solution.py:170
  797.5 9.1 collective-permute-done.90
  819.1 11.3 %collective-permute-done.91 = bf16[1024,512]{1,0:T(8,128)(2,1)} collective-permute-done((bf16[1024,512]{1,0:T(8,128)(2,1)}, bf16[1024,512]{1,0:T(8,128)(2,1)}, u32[]{:S(2)}, u32[]{:S(2)}) %collective-permute-start.91) | collective-permute-done | bytes 1048608 | tf_op jit(solution)/shard_map/ppermute | solution.py:170
  861.2 15.4 %collective-permute-done.96 = bf16[1024,512]{1,0:T(8,128)(2,1)} collective-permute-done((bf16[1024,512]{1,0:T(8,128)(2,1)}, bf16[1024,512]{1,0:T(8,128)(2,1)}, u32[]{:S(2)}, u32[]{:S(2)}) %collective-permute-start.96) | collective-permute-done | bytes 1048608 | tf_op jit(solution)/shard_map/ppermute | solution.py:170
  901.6 14.1 %attend_back.3 = bf16[1024,1536]{1,0:T(8,128)(2,1)S(1)} custom-call(bf16[1024,1536]{1,0:T(8,128)(2,1)} %copy-done.6, bf16[1024,512]{1,0:T(8,128)(2,1)S(1)} %constant_dynamic-update-slice_fusion.42.grad_ref, f32[4,1,1024]{2,1,0:T(1,128)S(1)} %get-tuple-element.708.log_ref, s32[1,1024]{1,0:T(1,128)S(1)} %bitcast.318, s32[1024,1]{1,0:T(8,128)S(1)} %copy.40.docs_col_ref), custom_call_target="tpu_custom_call" | custom-call | flops 10737418240 | bytes 8388608 | tf_op jit(solution)/shard_map/attend_back/pallas_call | solution.py:124
  948.0 10.8 collective-permute-done.104
  980.7 22.1 %collective-permute-done.107 = bf16[512,1024]{1,0:T(8,128)(2,1)S(1)} collective-permute-done((bf16[512,1024]{1,0:T(8,128)(2,1)}, bf16[512,1024]{1,0:T(8,128)(2,1)S(1)}, u32[]{:S(2)}, u32[]{:S(2)}) %collective-permute-start.107) | collective-permute-done | bytes 1048608 | tf_op jit(solution)/shard_map/ppermute | solution.py:173
  1083.3 16.4 %collective-permute-done.121 = bf16[512,768]{1,0:T(8,128)(2,1)S(1)} collective-permute-done((bf16[512,768]{1,0:T(8,128)(2,1)S(1)}, bf16[512,768]{1,0:T(8,128)(2,1)S(1)}, u32[]{:S(2)}, u32[]{:S(2)}) %collective-permute-start.121) | collective-permute-done | bytes 786464 | tf_op jit(solution)/shard_map/ppermute | solution.py:173
  1106.7 12.7 %collective-permute-done.122 = bf16[512,768]{1,0:T(8,128)(2,1)S(1)} collective-permute-done((bf16[512,768]{1,0:T(8,128)(2,1)S(1)}, bf16[512,768]{1,0:T(8,128)(2,1)S(1)}, u32[]{:S(2)}, u32[]{:S(2)}) %collective-permute-start.122) | collective-permute-done | bytes 786464 | tf_op jit(solution)/shard_map/ppermute | solution.py:173
  (1044 shorter events, 707.7 us)
Async XLA Ops:
  37.3 32.6 %collective-permute-start.16 = (bf16[512,1024]{1,0:T(8,128)(2,1)}, bf16[512,1024]{1,0:T(8,128)(2,1)}, u32[]{:S(2)}, u32[]{:S(2)}) collective-permute-start(bf16[512,1024]{1,0:T(8,128)(2,1)} %param.30), channel_id=1, source_target_pairs={{0,2},{1,3},{2,0},{3,1},{4,6},{5,7},{6,4},{7,5},{8,10},{9,11},{10,... | collective-permute-start | bytes 3145736 | tf_op jit(solution)/shard_map/ppermute | solution.py:170
  43.5 34.8 %collective-permute-start.5 = (bf16[256,2048]{1,0:T(8,128)(2,1)}, bf16[256,2048]{1,0:T(8,128)(2,1)}, u32[]{:S(2)}, u32[]{:S(2)}) collective-permute-start(bf16[256,2048]{1,0:T(8,128)(2,1)} %get-tuple-element.672), channel_id=1, source_target_pairs={{0,1},{1,0},{2,3},{3,2},{4,5},{5,4},{6,7},{7,6},{8,9},{9,8},{10,11... | collective-permute-start | bytes 3145736 | tf_op jit(solution)/shard_map/ppermute | solution.py:170
  70.0 28.2 %collective-permute-start.17 = (bf16[256,2048]{1,0:T(8,128)(2,1)}, bf16[256,2048]{1,0:T(8,128)(2,1)}, u32[]{:S(2)}, u32[]{:S(2)}) collective-permute-start(bf16[256,2048]{1,0:T(8,128)(2,1)} %get-tuple-element.672), channel_id=1, source_target_pairs={{0,2},{1,3},{2,0},{3,1},{4,6},{5,7},{6,4},{7,5},{8,10},{9,11},{10,... | collective-permute-start | bytes 3145736 | tf_op jit(solution)/shard_map/ppermute | solution.py:170
  98.2 25.9 %collective-permute-start.23 = (bf16[512,1024]{1,0:T(8,128)(2,1)}, bf16[512,1024]{1,0:T(8,128)(2,1)}, u32[]{:S(2)}, u32[]{:S(2)}) collective-permute-start(bf16[512,1024]{1,0:T(8,128)(2,1)} %param.30), channel_id=1, source_target_pairs={{0,8},{8,16},{16,24},{24,0},{1,9},{9,17},{17,25},{25,1},{2,10},{10... | collective-permute-start | bytes 3145736 | tf_op jit(solution)/shard_map/ppermute | solution.py:173
  124.0 26.7 %collective-permute-start.25 = (bf16[512,1024]{1,0:T(8,128)(2,1)}, bf16[512,1024]{1,0:T(8,128)(2,1)S(1)}, u32[]{:S(2)}, u32[]{:S(2)}) collective-permute-start(bf16[512,1024]{1,0:T(8,128)(2,1)} %collective-permute-done.23), channel_id=1, source_target_pairs={{0,8},{8,16},{16,24},{24,0},{1,9},{9,17},{17,25},{25,1},{2,10},{10... | collective-permute-start | bytes 3145736 | tf_op jit(solution)/shard_map/ppermute | solution.py:173
  124.1 39.6 %collective-permute-start.27 = (bf16[512,1024]{1,0:T(8,128)(2,1)}, bf16[512,1024]{1,0:T(8,128)(2,1)S(1)}, u32[]{:S(2)}, u32[]{:S(2)}) collective-permute-start(bf16[512,1024]{1,0:T(8,128)(2,1)} %collective-permute-done.23), channel_id=1, source_target_pairs={{0,2},{1,3},{2,0},{3,1},{4,6},{5,7},{6,4},{7,5},{8,10},{9,11},{10,... | collective-permute-start | bytes 3145736 | tf_op jit(solution)/shard_map/ppermute | solution.py:170
  150.8 25.9 %collective-permute-start.31 = (bf16[512,1024]{1,0:T(8,128)(2,1)S(1)}, bf16[512,1024]{1,0:T(8,128)(2,1)}, u32[]{:S(2)}, u32[]{:S(2)}) collective-permute-start(bf16[512,1024]{1,0:T(8,128)(2,1)S(1)} %collective-permute-done.25), channel_id=1, source_target_pairs={{0,8},{8,16},{16,24},{24,0},{1,9},{9,17},{17,25},{25,1},{2,10},{10... | collective-permute-start | bytes 3145736 | tf_op jit(solution)/shard_map/ppermute | solution.py:173
  178.0 28.4 %collective-permute-start.29 = (bf16[256,2048]{1,0:T(8,128)(2,1)S(1)}, bf16[256,2048]{1,0:T(8,128)(2,1)S(1)}, u32[]{:S(2)}, u32[]{:S(2)}) collective-permute-start(bf16[256,2048]{1,0:T(8,128)(2,1)S(1)} %get-tuple-element.727), channel_id=1, source_target_pairs={{0,1},{1,0},{2,3},{3,2},{4,5},{5,4},{6,7},{7,6},{8,9},{9,8},{10,11... | collective-permute-start | bytes 3145736 | tf_op jit(solution)/shard_map/ppermute | solution.py:170
  178.2 27.2 %collective-permute-start.30 = (bf16[256,2048]{1,0:T(8,128)(2,1)S(1)}, bf16[256,2048]{1,0:T(8,128)(2,1)S(1)}, u32[]{:S(2)}, u32[]{:S(2)}) collective-permute-start(bf16[256,2048]{1,0:T(8,128)(2,1)S(1)} %add_convert_fusion.23), channel_id=1, source_target_pairs={{0,2},{1,3},{2,0},{3,1},{4,6},{5,7},{6,4},{7,5},{8,10},{9,11},{10,... | collective-permute-start | bytes 3145736 | tf_op jit(solution)/shard_map/ppermute | solution.py:170
  205.4 25.7 %collective-permute-start.34 = (bf16[512,1024]{1,0:T(8,128)(2,1)S(1)}, bf16[512,1024]{1,0:T(8,128)(2,1)S(1)}, u32[]{:S(2)}, u32[]{:S(2)}) collective-permute-start(bf16[512,1024]{1,0:T(8,128)(2,1)S(1)} %collective-permute-done.25), channel_id=1, source_target_pairs={{0,2},{1,3},{2,0},{3,1},{4,6},{5,7},{6,4},{7,5},{8,10},{9,11},{10,... | collective-permute-start | bytes 3145736 | tf_op jit(solution)/shard_map/ppermute | solution.py:170
  231.2 26.1 %collective-permute-start.35 = (bf16[512,1024]{1,0:T(8,128)(2,1)}, bf16[512,1024]{1,0:T(8,128)(2,1)}, u32[]{:S(2)}, u32[]{:S(2)}) collective-permute-start(bf16[512,1024]{1,0:T(8,128)(2,1)} %collective-permute-done.31), channel_id=1, source_target_pairs={{0,2},{1,3},{2,0},{3,1},{4,6},{5,7},{6,4},{7,5},{8,10},{9,11},{10,... | collective-permute-start | bytes 3145736 | tf_op jit(solution)/shard_map/ppermute | solution.py:170
  257.2 27.8 %collective-permute-start.45 = (bf16[512,512]{1,0:T(8,128)(2,1)}, bf16[512,512]{1,0:T(8,128)(2,1)S(1)}, u32[]{:S(2)}, u32[]{:S(2)}) collective-permute-start(bf16[512,512]{1,0:T(8,128)(2,1)} %collective-permute-done.42), channel_id=1, source_target_pairs={{0,8},{8,16},{16,24},{24,0},{1,9},{9,17},{17,25},{25,1},{2,10},{10... | collective-permute-start | bytes 1572872 | tf_op jit(solution)/shard_map/ppermute | solution.py:173
  257.3 28.3 %collective-permute-start.41 = (bf16[512,512]{1,0:T(8,128)(2,1)}, bf16[512,512]{1,0:T(8,128)(2,1)S(1)}, u32[]{:S(2)}, u32[]{:S(2)}) collective-permute-start(bf16[512,512]{1,0:T(8,128)(2,1)} %copy-done.145), channel_id=1, source_target_pairs={{0,2},{1,3},{2,0},{3,1},{4,6},{5,7},{6,4},{7,5},{8,10},{9,11},{10,... | collective-permute-start | bytes 1572872 | tf_op jit(solution)/shard_map/ppermute | solution.py:170
  357.2 25.6 %collective-permute-start.55 = (bf16[1024,256]{1,0:T(8,128)(2,1)S(1)}, bf16[1024,256]{1,0:T(8,128)(2,1)S(1)}, u32[]{:S(2)}, u32[]{:S(2)}) collective-permute-start(bf16[1024,256]{1,0:T(8,128)(2,1)S(1)} %bitcast.338), channel_id=1, source_target_pairs={{0,1},{1,0},{2,3},{3,2},{4,5},{5,4},{6,7},{7,6},{8,9},{9,8},{10,11... | collective-permute-start | bytes 1572872 | tf_op jit(solution)/shard_map/ppermute | solution.py:170
  520.4 25.6 %collective-permute-start.68 = (bf16[256,2048]{1,0:T(8,128)(2,1)S(1)}, bf16[256,2048]{1,0:T(8,128)(2,1)S(1)}, u32[]{:S(2)}, u32[]{:S(2)}) collective-permute-start(bf16[256,2048]{1,0:T(8,128)(2,1)S(1)} %get-tuple-element.910), channel_id=1, source_target_pairs={{0,4},{1,5},{2,6},{3,7},{4,0},{5,1},{6,2},{7,3},{8,12},{9,13},{10,... | collective-permute-start | bytes 3145736 | tf_op jit(solution)/shard_map/ppermute | solution.py:170
  571.1 28.9 %collective-permute-start.74 = (bf16[256,2048]{1,0:T(8,128)(2,1)S(1)}, bf16[256,2048]{1,0:T(8,128)(2,1)S(1)}, u32[]{:S(2)}, u32[]{:S(2)}) collective-permute-start(bf16[256,2048]{1,0:T(8,128)(2,1)S(1)} %get-tuple-element.934), channel_id=1, source_target_pairs={{0,1},{1,0},{2,3},{3,2},{4,5},{5,4},{6,7},{7,6},{8,9},{9,8},{10,11... | collective-permute-start | bytes 3145736 | tf_op jit(solution)/shard_map/ppermute | solution.py:170
  607.9 29.6 %collective-permute-start.73 = (bf16[2,256,512]{2,1,0:T(8,128)(2,1)S(1)}, bf16[2,256,512]{2,1,0:T(8,128)(2,1)S(1)}, u32[]{:S(2)}, u32[]{:S(2)}) collective-permute-start(bf16[2,256,512]{2,1,0:T(8,128)(2,1)S(1)} %get-tuple-element.933), channel_id=1, source_target_pairs={{0,4},{1,5},{2,6},{3,7},{4,0},{5,1},{6,2},{7,3},{8,12},{9,13},{10,... | collective-permute-start | bytes 1572872 | tf_op jit(solution)/shard_map/ppermute | solution.py:170
  609.4 28.9 %collective-permute-start.76 = (bf16[256,2048]{1,0:T(8,128)(2,1)}, bf16[256,2048]{1,0:T(8,128)(2,1)S(1)}, u32[]{:S(2)}, u32[]{:S(2)}) collective-permute-start(bf16[256,2048]{1,0:T(8,128)(2,1)} %get-tuple-element.963), channel_id=1, source_target_pairs={{0,2},{1,3},{2,0},{3,1},{4,6},{5,7},{6,4},{7,5},{8,10},{9,11},{10,... | collective-permute-start | bytes 3145736 | tf_op jit(solution)/shard_map/ppermute | solution.py:170
  672.6 29.0 %collective-permute-start.80 = (bf16[256,2048]{1,0:T(8,128)(2,1)S(1)}, bf16[256,2048]{1,0:T(8,128)(2,1)S(1)}, u32[]{:S(2)}, u32[]{:S(2)}) collective-permute-start(bf16[256,2048]{1,0:T(8,128)(2,1)S(1)} %get-tuple-element.1004), channel_id=1, source_target_pairs={{0,1},{1,0},{2,3},{3,2},{4,5},{5,4},{6,7},{7,6},{8,9},{9,8},{10,11... | collective-permute-start | bytes 3145736 | tf_op jit(solution)/shard_map/ppermute | solution.py:170
  673.0 28.5 %collective-permute-start.81 = (bf16[256,2048]{1,0:T(8,128)(2,1)S(1)}, bf16[256,2048]{1,0:T(8,128)(2,1)S(1)}, u32[]{:S(2)}, u32[]{:S(2)}) collective-permute-start(bf16[256,2048]{1,0:T(8,128)(2,1)S(1)} %add_convert_fusion.18), channel_id=1, source_target_pairs={{0,2},{1,3},{2,0},{3,1},{4,6},{5,7},{6,4},{7,5},{8,10},{9,11},{10,... | collective-permute-start | bytes 3145736 | tf_op jit(solution)/shard_map/ppermute | solution.py:170
  704.3 25.6 %collective-permute-start.84 = (bf16[256,2048]{1,0:T(8,128)(2,1)S(1)}, bf16[256,2048]{1,0:T(8,128)(2,1)S(1)}, u32[]{:S(2)}, u32[]{:S(2)}) collective-permute-start(bf16[256,2048]{1,0:T(8,128)(2,1)S(1)} %get-tuple-element.1054), channel_id=1, source_target_pairs={{0,4},{1,5},{2,6},{3,7},{4,0},{5,1},{6,2},{7,3},{8,12},{9,13},{10,... | collective-permute-start | bytes 3145736 | tf_op jit(solution)/shard_map/ppermute | solution.py:170
  767.0 41.0 %collective-permute-start.83 = (bf16[256,2048]{1,0:T(8,128)(2,1)S(1)}, bf16[256,2048]{1,0:T(8,128)(2,1)S(1)}, u32[]{:S(2)}, u32[]{:S(2)}) collective-permute-start(bf16[256,2048]{1,0:T(8,128)(2,1)S(1)} %get-tuple-element.1053), channel_id=1, source_target_pairs={{0,1},{1,0},{2,3},{3,2},{4,5},{5,4},{6,7},{7,6},{8,9},{9,8},{10,11... | collective-permute-start | bytes 3145736 | tf_op jit(solution)/shard_map/ppermute | solution.py:170
  818.0 28.1 %collective-permute-start.93 = (bf16[1024,512]{1,0:T(8,128)(2,1)}, bf16[1024,512]{1,0:T(8,128)(2,1)}, u32[]{:S(2)}, u32[]{:S(2)}) collective-permute-start(bf16[1024,512]{1,0:T(8,128)(2,1)} %add_convert_fusion.12), channel_id=1, source_target_pairs={{0,8},{8,16},{16,24},{24,0},{1,9},{9,17},{17,25},{25,1},{2,10},{10... | collective-permute-start | bytes 3145736 | tf_op jit(solution)/shard_map/ppermute | solution.py:173
  859.4 77.2 %collective-permute-start.78 = (bf16[4,256,256]{2,1,0:T(8,128)(2,1)}, bf16[4,256,256]{2,1,0:T(8,128)(2,1)}, u32[]{:S(2)}, u32[]{:S(2)}) collective-permute-start(bf16[4,256,256]{2,1,0:T(8,128)(2,1)} %get-tuple-element.1453), channel_id=1, source_target_pairs={{0,1},{1,0},{2,3},{3,2},{4,5},{5,4},{6,7},{7,6},{8,9},{9,8},{10,11... | collective-permute-start | bytes 1572872 | tf_op jit(solution)/shard_map/ppermute | solution.py:170
  860.0 29.2 %collective-permute-start.100 = (f32[6,1024]{1,0:T(8,128)S(1)}, f32[6,1024]{1,0:T(8,128)S(1)}, u32[]{:S(2)}, u32[]{:S(2)}) collective-permute-start(f32[6,1024]{1,0:T(8,128)S(1)} %constant_dynamic-slice_fusion.6), channel_id=1, source_target_pairs={{0,4},{1,5},{2,6},{3,7},{4,0},{5,1},{6,2},{7,3},{8,12},{9,13},{10,... | collective-permute-start | bytes 73736 | tf_op jit(solution)/shard_map/ppermute | solution.py:170
  860.6 29.1 %collective-permute-start.95 = (bf16[1024,512]{1,0:T(8,128)(2,1)}, bf16[1024,512]{1,0:T(8,128)(2,1)S(1)}, u32[]{:S(2)}, u32[]{:S(2)}) collective-permute-start(bf16[1024,512]{1,0:T(8,128)(2,1)} %add_convert_fusion.7), channel_id=1, source_target_pairs={{0,8},{8,16},{16,24},{24,0},{1,9},{9,17},{17,25},{25,1},{2,10},{10... | collective-permute-start | bytes 3145736 | tf_op jit(solution)/shard_map/ppermute | solution.py:173
  889.2 26.6 %collective-permute-start.101 = (bf16[1024,512]{1,0:T(8,128)(2,1)}, bf16[1024,512]{1,0:T(8,128)(2,1)}, u32[]{:S(2)}, u32[]{:S(2)}) collective-permute-start(bf16[1024,512]{1,0:T(8,128)(2,1)} %pad_maximum_fusion.49), channel_id=1, source_target_pairs={{0,4},{1,5},{2,6},{3,7},{4,0},{5,1},{6,2},{7,3},{8,12},{9,13},{10,... | collective-permute-start | bytes 3145736 | tf_op jit(solution)/shard_map/ppermute | solution.py:170
  937.8 26.3 %collective-permute-start.102 = (bf16[512,1024]{1,0:T(8,128)(2,1)S(1)}, bf16[512,1024]{1,0:T(8,128)(2,1)S(1)}, u32[]{:S(2)}, u32[]{:S(2)}) collective-permute-start(bf16[512,1024]{1,0:T(8,128)(2,1)S(1)} %copy-done.118), channel_id=1, source_target_pairs={{0,8},{8,16},{16,24},{24,0},{1,9},{9,17},{17,25},{25,1},{2,10},{10... | collective-permute-start | bytes 3145736 | tf_op jit(solution)/shard_map/ppermute | solution.py:173
  976.1 26.7 %collective-permute-start.107 = (bf16[512,1024]{1,0:T(8,128)(2,1)}, bf16[512,1024]{1,0:T(8,128)(2,1)S(1)}, u32[]{:S(2)}, u32[]{:S(2)}) collective-permute-start(bf16[512,1024]{1,0:T(8,128)(2,1)} %add_convert_fusion.3), channel_id=1, source_target_pairs={{0,8},{8,16},{16,24},{24,0},{1,9},{9,17},{17,25},{25,1},{2,10},{10... | collective-permute-start | bytes 3145736 | tf_op jit(solution)/shard_map/ppermute | solution.py:173
  977.4 27.6 %collective-permute-start.109 = (bf16[512,1024]{1,0:T(8,128)(2,1)S(1)}, bf16[512,1024]{1,0:T(8,128)(2,1)S(1)}, u32[]{:S(2)}, u32[]{:S(2)}) collective-permute-start(bf16[512,1024]{1,0:T(8,128)(2,1)S(1)} %copy-done.174), channel_id=1, source_target_pairs={{0,2},{1,3},{2,0},{3,1},{4,6},{5,7},{6,4},{7,5},{8,10},{9,11},{10,... | collective-permute-start | bytes 3145736 | tf_op jit(solution)/shard_map/ppermute | solution.py:170
  1005.0 43.8 %collective-permute-start.116 = (bf16[512,1024]{1,0:T(8,128)(2,1)S(1)}, bf16[512,1024]{1,0:T(8,128)(2,1)S(1)}, u32[]{:S(2)}, u32[]{:S(2)}) collective-permute-start(bf16[512,1024]{1,0:T(8,128)(2,1)S(1)} %copy-done.173), channel_id=1, source_target_pairs={{0,2},{1,3},{2,0},{3,1},{4,6},{5,7},{6,4},{7,5},{8,10},{9,11},{10,... | collective-permute-start | bytes 3145736 | tf_op jit(solution)/shard_map/ppermute | solution.py:170
  1054.0 26.6 %collective-permute-start.120 = (bf16[512,1024]{1,0:T(8,128)(2,1)}, bf16[512,1024]{1,0:T(8,128)(2,1)}, u32[]{:S(2)}, u32[]{:S(2)}) collective-permute-start(bf16[512,1024]{1,0:T(8,128)(2,1)} %add_convert_fusion.1), channel_id=1, source_target_pairs={{0,8},{8,16},{16,24},{24,0},{1,9},{9,17},{17,25},{25,1},{2,10},{10... | collective-permute-start | bytes 3145736 | tf_op jit(solution)/shard_map/ppermute | solution.py:173
  (295 other events, 3256.4 us)
